TPU v7x, 32 devices: a whole 2x2x4 slice. The times are simulated.
32 devices in a mesh: dp: 4 (over y, x), head: 8 (over z, core).
Axes of the slice: x: 2, y: 2, z: 4, core: 2. Of those that a mesh axis runs over, the one named last changes fastest.
Arguments:
- hidden: bfloat16 [4, 512, 1024], P('dp', 'head'), may hold values from -6 to 6
- core_grad: bfloat16 [4, 512, 1024], P('dp', 'head'), may hold values from -4 to 4
- query_weight: bfloat16 [1024, 512], P(None, 'head'), may hold values from -0.1875 to 0.1875
- key_weight: bfloat16 [1024, 512], P(None, 'head'), may hold values from -0.1875 to 0.1875
- value_weight: bfloat16 [1024, 1024], P(None, 'head'), may hold values from -0.1875 to 0.1875
- beta_weight: bfloat16 [1024, 8], P(None, 'head'), may hold values from -0.1875 to 0.1875
- decay_weight: bfloat16 [1024, 8], P(None, 'head'), may hold values from -0.1875 to 0.1875
- decay_log: float32 [8], P('head'), may hold values from 0 to 2.7
- decay_bias: float32 [8], P('head'), may hold values from -6 to -1
Outputs:
- token_grad: bfloat16 [4, 512, 1024], P('dp', 'head')
- query_grad: float32 [1024, 512], P(None, 'head')
- key_grad: float32 [1024, 512], P(None, 'head')
- value_grad: float32 [1024, 1024], P(None, 'head')
All inputs are finite; a program needn't handle non-finite values.
Results may differ from a plain program's by a relative error of at most 0.013.
Values may be sent and summed in bfloat16 or wider, within the bound.
No kernel may reach another device: no remote copies, remote signals or barrier semaphores. Data moves between devices by JAX's collectives and lax.ppermute only.
A program may use at most 128 MiB of HBM per device.

v0:
```python
import jax
import jax.numpy as jnp
from jax import lax
from jax.sharding import PartitionSpec as P

BLOCK = 64


eps_norm = 1e-06


def partner(block, axis, distance):
    count = lax.axis_size(axis)
    route = []
    for low in range(count):
        high = low | 1 << distance
        if high != low and high < count:
            route += [(low, high), (high, low)]
    return lax.ppermute(block, axis, route)


def exact_dot(left, right):
    return jnp.dot(left, right, precision=lax.Precision.HIGHEST)


def blockwise_core(queries, keys, values, betas, logdecay, span_rows):
    total_rows = queries.shape[0]
    feature = queries.shape[1]
    num_blocks = total_rows // span_rows
    lower_mask = jnp.tril(jnp.ones((span_rows, span_rows), dtype=bool))
    strict_mask = jnp.tril(jnp.ones((span_rows, span_rows), dtype=bool), -1)
    identity = jnp.eye(span_rows, dtype=queries.dtype)

    def advance(memory, block_in):
        q_blk, k_blk, v_blk, b_blk, g_blk = block_in
        cumulative = jnp.cumsum(g_blk)
        spread = cumulative[:, None] - cumulative[None, :]
        decay_ratio = jnp.where(lower_mask, jnp.exp(jnp.where(lower_mask, spread, 0.0)), 0.0)
        decay_now = jnp.exp(cumulative)
        mixing = jnp.where(
            strict_mask, b_blk[:, None] * decay_ratio * exact_dot(k_blk, k_blk.T), 0.0
        )
        target = b_blk[:, None] * (v_blk - decay_now[:, None] * exact_dot(k_blk, memory.T))
        fresh_vals = jax.scipy.linalg.solve_triangular(
            identity + mixing, target, lower=True, unit_diagonal=True
        )
        attend = decay_ratio * exact_dot(q_blk, k_blk.T)
        result = decay_now[:, None] * exact_dot(q_blk, memory.T) + exact_dot(attend, fresh_vals)
        tail_weight = jnp.exp(cumulative[-1] - cumulative)
        memory = jnp.exp(cumulative[-1]) * memory + exact_dot(
            (fresh_vals * tail_weight[:, None]).T, k_blk
        )
        return (memory, result)

    block_inputs = (
        queries.reshape(num_blocks, span_rows, feature),
        keys.reshape(num_blocks, span_rows, feature),
        values.reshape(num_blocks, span_rows, feature),
        betas.reshape(num_blocks, span_rows),
        logdecay.reshape(num_blocks, span_rows),
    )
    start_memory = jnp.zeros((feature, feature), queries.dtype)
    final_memory, outputs = lax.scan(advance, start_memory, block_inputs)
    return outputs.reshape(total_rows, feature)


def core_forward(
    query_pre, key_pre, value_pre, beta_pre, decay_pre, log_rate, rate_bias, span_rows
):
    feature = query_pre.shape[1]
    queries = (
        query_pre
        * lax.rsqrt(jnp.sum(query_pre * query_pre, axis=1, keepdims=True) + eps_norm)
        * feature ** (-0.5)
    )
    keys = key_pre * lax.rsqrt(jnp.sum(key_pre * key_pre, axis=1, keepdims=True) + eps_norm)
    betas = jax.nn.sigmoid(beta_pre)
    logdecay = -jnp.exp(log_rate) * jax.nn.softplus(decay_pre + rate_bias)
    return blockwise_core(queries, keys, value_pre, betas, logdecay, span_rows)


def body(
    hidden,
    core_grad,
    query_weight,
    key_weight,
    value_weight,
    beta_weight,
    decay_weight,
    decay_log,
    decay_bias,
):
    half_width = query_weight.shape[1]
    head_width = value_weight.shape[1]
    is_first = lax.axis_index("head") % 2 == 0
    own_start = jnp.where(is_first, 0, half_width).astype(jnp.int32)
    other_start = half_width - own_start
    query_other, key_other = partner((query_weight, key_weight), "head", 0)
    query_full = jnp.where(
        is_first,
        jnp.concatenate([query_weight, query_other], 1),
        jnp.concatenate([query_other, query_weight], 1),
    )
    key_full = jnp.where(
        is_first,
        jnp.concatenate([key_weight, key_other], 1),
        jnp.concatenate([key_other, key_weight], 1),
    )
    all_weights = jnp.concatenate(
        [query_full, key_full, value_weight, beta_weight, decay_weight], 1
    )
    cotangent = lax.all_to_all(core_grad, "head", split_axis=2, concat_axis=1, tiled=True)[
        0
    ].astype(jnp.float32)
    all_rows = lax.all_gather(hidden, "head", axis=1, tiled=True)[0]
    projected = jnp.dot(all_rows, all_weights, preferred_element_type=jnp.float32)
    query_pre = projected[:, :head_width]
    key_pre = projected[:, head_width : 2 * head_width]
    value_pre = projected[:, 2 * head_width : 3 * head_width]
    beta_pre = projected[:, 3 * head_width]
    decay_pre = projected[:, 3 * head_width + 1]

    def forward(q_in, k_in, v_in, b_in, a_in):
        return core_forward(q_in, k_in, v_in, b_in, a_in, decay_log[0], decay_bias[0], BLOCK)

    output, pull = jax.vjp(forward, query_pre, key_pre, value_pre, beta_pre, decay_pre)
    grads = pull(cotangent)
    grad_q = grads[0].astype(jnp.bfloat16)
    grad_k = grads[1].astype(jnp.bfloat16)
    grad_v = grads[2].astype(jnp.bfloat16)
    grad_b = grads[3].astype(jnp.bfloat16)
    grad_a = grads[4].astype(jnp.bfloat16)
    grads_all = jnp.concatenate([grad_q, grad_k, grad_v, grad_b[:, None], grad_a[:, None]], 1)
    token_part = lax.psum_scatter(
        jnp.einsum("lc,dc->ld", grads_all, all_weights, preferred_element_type=jnp.float32).astype(
            jnp.bfloat16
        ),
        "head",
        scatter_dimension=0,
        tiled=True,
    )
    token_grad = token_part[None]
    factors = jnp.concatenate([grad_q, grad_k, grad_v], 1)
    weight_terms = jnp.einsum("ld,lc->dc", all_rows, factors, preferred_element_type=jnp.float32)
    query_part = weight_terms[:, :head_width]
    key_part = weight_terms[:, head_width : 2 * head_width]
    value_sum = weight_terms[:, 2 * head_width :]
    recv_qw, recv_kw = (
        partner(
            lax.dynamic_slice_in_dim(query_part, other_start, half_width, 1).astype(jnp.bfloat16),
            "head",
            0,
        ).astype(jnp.float32),
        partner(
            lax.dynamic_slice_in_dim(key_part, other_start, half_width, 1).astype(jnp.bfloat16),
            "head",
            0,
        ).astype(jnp.float32),
    )
    query_sum = lax.dynamic_slice_in_dim(query_part, own_start, half_width, 1) + recv_qw
    key_sum = lax.dynamic_slice_in_dim(key_part, own_start, half_width, 1) + recv_kw
    data_count = lax.axis_size("dp")
    query_total, key_total, value_total = (
        lax.psum(query_sum.astype(jnp.bfloat16), "dp").astype(jnp.float32),
        lax.psum(key_sum.astype(jnp.bfloat16), "dp").astype(jnp.float32),
        lax.psum(value_sum.astype(jnp.bfloat16), "dp").astype(jnp.float32),
    )
    return (token_grad, query_total / data_count, key_total / data_count, value_total / data_count)


def solution(mesh):
    placed = (
        P("dp", "head", None),
        P("dp", "head", None),
        P(None, "head"),
        P(None, "head"),
        P(None, "head"),
        P(None, "head"),
        P(None, "head"),
        P("head"),
        P("head"),
    )
    return jax.shard_map(
        body,
        mesh=mesh,
        in_specs=placed,
        out_specs=(P("dp", "head", None), P(None, "head"), P(None, "head"), P(None, "head")),
        check_vma=False,
    )
```

profile of v0, /device:TPU:0, one launch (start us, length us, event | category | flops | bytes accessed | tf_op | source)
XLA Modules:
  0.0 495.6 jit_solution(4948123523511978578)
XLA Ops:
  12.4 2.3 reduce.17
  15.6 6.3 %all-to-all-start = ((bf16[8,2,4096]{2,1,0:T(2,128)(2,1)}), bf16[8,2,4096]{2,1,0:T(2,128)(2,1)S(1)}, u32[]{:S(2)}, u32[]{:S(2)}) async-start(bf16[8,2,4096]{2,1,0:T(2,128)(2,1)} %reshape.610), calls=%async_computation | async-start | bytes 262144 | tf_op jit(solution)/shard_map/all_to_all | solution.py:112
  25.4 2.2 concatenate.25
  27.6 4.6 all-to-all-done
  33.7 2.9 all-gather.2.cloned.1.call-done
  36.6 2.0 convolution_bitcast_fusion.2
  43.1 115.6 %while.88 = (s32[]{:T(128)}, f32[128,128]{1,0:T(8,128)S(1)}, f32[8,64,64]{2,1,0:T(8,128)}, f32[8,64]{1,0:T(8,128)S(1)}, f32[8,64,64]{2,1,0:T(8,128)}, /*index=5*...) while((s32[]{:T(128)}, f32[128,128]{1,0:T(8,128)S(1)}, ...), condition=%wide.region_4.5_spmd.clone.clone, body=%wide.region_2.4_spmd.clone.clone.sunk | while | flops 56930432 | bytes 1708391 | solution.py:63
  47.1 4.9 custom-call.45
  61.6 4.9 custom-call.45
  76.0 4.9 custom-call.45
  90.5 4.9 custom-call.45
  104.9 4.9 custom-call.45
  119.3 4.9 custom-call.45
  133.8 4.9 custom-call.45
  148.3 4.9 custom-call.45
  159.5 240.1 %while.89 = (s32[]{:T(128)}, f32[128,128]{1,0:T(8,128)S(1)}, f32[8,64,128]{2,1,0:T(8,128)S(1)}, f32[8,64,128]{2,1,0:T(8,128)S(1)}, bf16[8,64,128]{2,1,0:T(8,128)...) while((s32[]{:T(128)}, f32[128,128]{1,0:T(8,128)S(1)}, ...), condition=%wide.region_16.17_spmd.clone.clone, body=%wide.region_5.16_spmd.clone.clone.sunk | while | flops 129442176 | bytes 2691273 | solution.py:63
  164.0 4.9 custom-call.46
  174.4 1.5 fusion.262
  194.1 4.9 custom-call.46
  204.4 1.5 fusion.262
  224.2 4.9 custom-call.46
  234.5 1.5 fusion.262
  254.1 4.9 custom-call.46
  284.2 4.9 custom-call.46
  294.5 1.5 fusion.262
  314.1 4.9 custom-call.46
  344.1 4.9 custom-call.46
  374.1 4.9 custom-call.46
  401.5 1.7 copy.115
  408.5 1.8 convolution_convert_fusion
  410.3 43.4 %all-reduce.5.cloned.1.call-done = (bf16[1024,64]{0,1:T(8,128)(2,1)}, bf16[1024,64]{0,1:T(8,128)(2,1)}, bf16[1024,128]{0,1:T(8,128)(2,1)}) async-done(((bf16[1024,64]{0,1:T(8,128)(2,1)}, bf16[1024,64]{0,1:T(8,128)(2,1)}, bf16[1024,128]{0,1:T(8,128)(2,1)}), (bf16[1024,64]{0,1:T(8,128)(2,1)}, bf16[1024,64]{0,1:T(8,128)(2,1)}, bf16[1024,128]{0,1:T(8,128)(2,1)})) %all-reduce.5.cloned.1.call-update) | async-done | bytes 524304 | tf_op jit(solution)/shard_map/psum | solution.py:164
  457.2 31.9 %reduce-scatter.2.cloned.1.call-done = bf16[64,1024]{1,0:T(8,128)(2,1)} async-done(((bf16[512,1024]{1,0:T(8,128)(2,1)}), bf16[64,1024]{1,0:T(8,128)(2,1)}) %reduce-scatter.2.cloned.1.call-update) | async-done | bytes 131088 | tf_op jit(solution)/shard_map/reduce_scatter | solution.py:134
  (595 shorter events, 279.9 us)
Async XLA Ops:
  7.2 29.4 %all-gather.2.cloned.1.call-start = ((), (), s32[]{:S(2)}) async-start(), calls=%async_computation.2 | async-start | bytes 1179648 | tf_op jit(solution)/shard_map/all_gather | solution.py:115
  7.9 15.1 %copy-start.23 = (bf16[1024,1]{0,1:T(2,128)(2,1)S(1)}, bf16[1024,1]{0,1:T(2,128)(2,1)}, u32[]{:S(2)}) copy-start(bf16[1024,1]{0,1:T(2,128)(2,1)} %param.18) | copy-start | bytes 6148
  9.0 14.2 %copy-start.24 = (bf16[1024,1]{0,1:T(2,128)(2,1)S(1)}, bf16[1024,1]{0,1:T(2,128)(2,1)}, u32[]{:S(2)}) copy-start(bf16[1024,1]{0,1:T(2,128)(2,1)} %param.19) | copy-start | bytes 6148
  9.0 15.8 %collective-permute-start = (bf16[1024,64]{1,0:T(8,128)(2,1)S(1)}, bf16[1024,64]{1,0:T(8,128)(2,1)S(1)}, u32[]{:S(2)}, u32[]{:S(2)}) collective-permute-start(bf16[1024,64]{1,0:T(8,128)(2,1)S(1)} %copy.93), channel_id=1, source_target_pairs={{0,1},{1,0},{2,3},{3,2},{4,5},{5,4},{6,7},{7,6},{8,9},{9,8},{10,11... | collective-permute-start | bytes 393224 | tf_op jit(solution)/shard_map/ppermute | solution.py:19
  10.6 14.5 %collective-permute-start.1 = (bf16[1024,64]{1,0:T(8,128)(2,1)S(1)}, bf16[1024,64]{1,0:T(8,128)(2,1)S(1)}, u32[]{:S(2)}, u32[]{:S(2)}) collective-permute-start(bf16[1024,64]{1,0:T(8,128)(2,1)S(1)} %copy.96), channel_id=1, source_target_pairs={{0,1},{1,0},{2,3},{3,2},{4,5},{5,4},{6,7},{7,6},{8,9},{9,8},{10,11... | collective-permute-start | bytes 393224 | tf_op jit(solution)/shard_map/ppermute | solution.py:19
  14.7 10.7 %copy-start.7 = (bf16[1024,128]{1,0:T(8,128)(2,1)S(1)}, bf16[1024,128]{1,0:T(8,128)(2,1)}, u32[]{:S(2)}) copy-start(bf16[1024,128]{1,0:T(8,128)(2,1)} %param.17) | copy-start | bytes 786436
  15.6 16.6 %all-to-all-start = ((bf16[8,2,4096]{2,1,0:T(2,128)(2,1)}), bf16[8,2,4096]{2,1,0:T(2,128)(2,1)S(1)}, u32[]{:S(2)}, u32[]{:S(2)}) async-start(bf16[8,2,4096]{2,1,0:T(2,128)(2,1)} %reshape.610), calls=%async_computation | async-start | bytes 262144 | tf_op jit(solution)/shard_map/all_to_all | solution.py:112
  22.0 431.7 %all-reduce.5.cloned.1.call-start = ((), (), s32[]{:S(2)}) async-start(), calls=%async_computation.4 | async-start | bytes 1048576 | tf_op jit(solution)/shard_map/psum | solution.py:164
  38.7 0.7 copy-start.12
  158.7 0.7 copy-start.6
  158.7 0.7 copy-start.10
  158.8 0.7 copy-start.11
  158.8 0.7 copy-start.21
  158.8 0.7 copy-start.25
  158.8 0.7 copy-start.26
  399.6 0.6 copy-start.17
  399.6 0.7 copy-start.5
  399.6 3.7 copy-start.14
  399.7 3.7 copy-start.16
  400.3 3.8 copy-start
  403.2 1.0 copy-start.3
  404.2 0.7 copy-start.1
  404.9 3.3 copy-start.20
  404.9 3.4 copy-start.18
  404.9 3.5 copy-start.22
  404.9 3.5 copy-start.4
  404.9 3.5 copy-start.2
  405.0 1.4 collective-permute-start.3
  406.0 1.4 collective-permute-start.2
  408.1 80.9 %reduce-scatter.2.cloned.1.call-start = ((), (), s32[]{:S(2)}) async-start(), calls=%async_computation.3 | async-start | bytes 1179648 | tf_op jit(solution)/shard_map/reduce_scatter | solution.py:134
  453.7 2.0 copy-start.9
  453.7 2.8 copy-start.8
  (3 other events, 1.7 us)
Sparse Core Ops, SparseCore 0:
  9.6 26.9 all-gather.1
  408.3 45.3 all-reduce.4
  456.5 32.4 reduce-scatter.1
where the time goes:
time: 503 us; the launch traced here: 496 us
  other arithmetic  168 us (33%)
  matrix products  134 us (27%)
  waiting for transfers between devices  83.9 us (17%)
  local copies, waits for them, and re-layouts  68.4 us (14%)
  loops' own time  16.6 us (3%)
  between operations  15.8 us (3%)
  starting transfers between devices  7.9 us (2%)
    dot_general x136, matrix products, exact_dot(): return jnp.dot(left, right, precision=lax.Precision.HIGHEST)  113 us
    another operation x48, other arithmetic, advance(): jax.scipy.linalg.solve_triangular(identity + mixing, target, lower=True,...  85.9 us
    psum x1, waiting for transfers between devices, body(): lax.psum(query_sum.astype(jnp.bfloat16), 'dp').astype(jnp.float32)  43.4 us
    reduce_scatter x1, waiting for transfers between devices, body(): lax.psum_scatter(jnp.einsum('lc,dc->ld', grads_all, all_weights, preferre...  31.9 us
    dynamic_slice x32, local copies, waits for them, and re-layouts, blockwise_core(): final_memory, outputs = lax.scan(advance, start_memory, block_inputs)  18.1 us
    another operation x2, loops' own time, blockwise_core(): final_memory, outputs = lax.scan(advance, start_memory, block_inputs)  16.6 us
    dynamic_update_slice x24, other arithmetic, blockwise_core(): final_memory, outputs = lax.scan(advance, start_memory, block_inputs)  15.5 us
    another operation x24, matrix products, advance(): jax.scipy.linalg.solve_triangular(identity + mixing, target, lower=True,...  15.3 us
  transfers between devices with their start and end apart: 8, of which 5 were waited for; matrix products, arithmetic and copies ran while one was open for 4% of the time, Pallas kernels for 0%

commit v1 on v0

v1 whole, which is shorter than its diff:
```python
import jax
import jax.numpy as jnp
from jax import lax
from jax.experimental import pallas as pl
from jax.experimental.pallas import tpu as pltpu
from jax.sharding import PartitionSpec as P

CHUNK = 128
GROUP = 4
NORM_EPS = 1e-06
F32 = jnp.float32
BF16 = jnp.bfloat16


def nn(a, b):
    return lax.dot_general(a, b, (((1,), (0,)), ((), ())), preferred_element_type=F32)


def nt(a, b):
    return lax.dot_general(a, b, (((1,), (1,)), ((), ())), preferred_element_type=F32)


def tn(a, b):
    return lax.dot_general(a, b, (((0,), (0,)), ((), ())), preferred_element_type=F32)


def halves(a):
    high = a.astype(BF16)
    return high, (a - high.astype(F32)).astype(BF16)


def fine_nn(a, b):
    left = jnp.concatenate(a, 1)
    right = jnp.concatenate(b, 1)
    both = nn(left, jnp.concatenate([right, right], 0))
    width = b[0].shape[1]
    return both[:, :width] + both[:, width:]


def fine_gram(a):
    left = jnp.concatenate(a, 1)
    both = nt(left, jnp.concatenate([jnp.concatenate([p, p], 1) for p in a], 0))
    width = a[0].shape[0]
    return both[:, :width] + both[:, width:]


def row_sum(a):
    return jnp.sum(a, axis=1, keepdims=True)


def core_kernel(
    rows_ref, wq_ref, wq2_ref, wk_ref, wk2_ref, wv_ref, wb_ref, wa_ref, log_ref, bias_ref, cot_ref,
    out_ref,
    q_s, k_s, b_s, e_s, tail_s, gam_s, p_s, t_s, w_s, u0_s, kt_s, x_s, qn_s, kn_s,
    f_s, g_s, h_s, ec_s, m_s, d_s,
):
    total, head = cot_ref.shape
    num = total // CHUNK
    group = min(GROUP, num)
    scale = head ** -0.5
    row_id = lax.broadcasted_iota(jnp.int32, (CHUNK, CHUNK), 0)
    col_id = lax.broadcasted_iota(jnp.int32, (CHUNK, CHUNK), 1)
    low = row_id >= col_id
    strict = row_id > col_id
    low_ones = jnp.where(low, 1.0, 0.0).astype(BF16)
    high_ones = jnp.where(row_id <= col_id, 1.0, 0.0).astype(BF16)
    rate = -jnp.exp(log_ref[...])
    bias = bias_ref[...]

    def loop(body):
        if num == group:
            body(0)
        else:
            lax.fori_loop(0, num // group, lambda i, c: (body(i * group), c)[1], 0)

    def at(first, i):
        if isinstance(first, int):
            return pl.ds((first + i) * CHUNK, CHUNK)
        return pl.ds(pl.multiple_of((first + i) * CHUNK, CHUNK), CHUNK)

    features = wv_ref.shape[0]
    narrow = jnp.concatenate(
        [wq_ref[...], wq2_ref[...], wk_ref[...], wk2_ref[...],
         jnp.broadcast_to(wb_ref[...], (head, features)), jnp.broadcast_to(wa_ref[...], (head, features))], 0)

    def prepare(first):
        each = range(group)
        spans = [at(first, i) for i in each]
        mats, kparts, ek_bv = [], [], []
        for i in each:
            rows = rows_ref[spans[i], :]
            pre = nt(rows, narrow)
            v = nn(rows, wv_ref[...])
            qp, kp = pre[:, :head], pre[:, head : 2 * head]
            qn = lax.rsqrt(row_sum(qp * qp) + NORM_EPS)
            kn = lax.rsqrt(row_sum(kp * kp) + NORM_EPS)
            q = qp * (qn * scale)
            k = kp * kn
            beta = 1.0 / (1.0 + jnp.exp(-pre[:, 2 * head : 3 * head]))
            x = pre[:, 3 * head :] + bias
            g = rate * (jnp.maximum(x, 0.0) + jnp.log1p(jnp.exp(-jnp.abs(x))))
            g1 = g.astype(BF16)
            rest = g - g1.astype(F32)
            g2, g3 = halves(rest)
            sums = nn(low_ones, jnp.concatenate([g1, g2, g3], 1))
            c = sums[:, :head] + (sums[:, head : 2 * head] + sums[:, 2 * head :])
            last = c[CHUNK - 1 : CHUNK, :]
            e = jnp.exp(c)
            tail = jnp.exp(last - c)
            gam = jnp.exp(jnp.where(low, c - c.T, -1e30))
            kpair = halves(k)
            kk = fine_gram(kpair)
            qk = nt(q.astype(BF16), kpair[0])
            a = jnp.where(strict, beta * gam * kk, 0.0)
            p = (gam * qk).astype(BF16)
            kt = (tail * k).astype(BF16)
            q_s[spans[i], :] = q
            k_s[spans[i], :] = k
            b_s[spans[i], :] = beta
            e_s[spans[i], :] = e
            tail_s[spans[i], :] = tail
            gam_s[spans[i], :] = gam
            x_s[spans[i], :] = x
            p_s[spans[i], :] = p
            kt_s[spans[i], :] = kt
            qn_s[spans[i], :] = jnp.broadcast_to(qn * scale, (CHUNK, head))
            kn_s[spans[i], :] = jnp.broadcast_to(kn, (CHUNK, head))
            ec_s[first + i] = jnp.exp(jnp.broadcast_to(last, (8, head)))
            mats.append(a)
            ek_bv.append(jnp.concatenate([beta * e * k, beta * v], 1))
        eye = jnp.where(row_id == col_id, 1.0, 0.0)
        inv = [eye - jnp.where((row_id >> 1) == (col_id >> 1), a, 0.0) for a in mats]
        pairs = [halves(a) for a in mats]
        level = 1
        while (2 << level) <= CHUNK:
            joint = ((row_id >> (level + 1)) == (col_id >> (level + 1))) & ((row_id >> level) > (col_id >> level))
            tp = [halves(t) for t in inv]
            left = [
                fine_nn(tp[i], tuple(jnp.where(joint, half, jnp.zeros_like(half)) for half in pairs[i]))
                for i in each
            ]
            lp = [halves(z) for z in left]
            inv = [inv[i] - fine_nn(lp[i], tp[i]) for i in each]
            level += 1
        for i in each:
            tp = halves(inv[i])
            t_s[spans[i], :] = tp[0]
            ep = halves(ek_bv[i])
            wu = nn(jnp.concatenate(tp, 1), jnp.concatenate([ep[0], ep[0]], 0)) + nn(tp[0], ep[1])
            w = wu[:, :head].astype(BF16)
            w_s[spans[i], :] = w
            u0_s[spans[i], :] = wu[:, head:]
            fg = tn(kt_s[spans[i], :], jnp.concatenate([w, wu[:, head:].astype(BF16)], 1))
            f_s[spans[i], :] = fg[:, :head].astype(BF16)
            g_s[spans[i], :] = fg[:, head:]
            pw = nn(p_s[spans[i], :], w)
            h_s[spans[i], :] = tn((e_s[spans[i], :] * q_s[spans[i], :] - pw).astype(BF16), cot_ref[spans[i], :])

    loop(prepare)

    m_s[pl.ds(0, head), :] = jnp.zeros((head, head), F32)
    d_s[pl.ds((num - 1) * head, head), :] = jnp.zeros((head, head), F32)
    m = jnp.zeros((head, head), F32)
    d = jnp.zeros((head, head), F32)
    for i in range(num):
        span = pl.ds(i * CHUNK, CHUNK)
        if i == 0:
            m = g_s[span, :]
        else:
            m = ec_s[i][:1] * m - nn(f_s[span, :], m.astype(BF16)) + g_s[span, :]
        m_s[pl.ds((i + 1) * head, head), :] = m
        r = num - 1 - i
        if r > 0:
            back = pl.ds(r * CHUNK, CHUNK)
            if r == num - 1:
                d = h_s[back, :]
            else:
                d = ec_s[r][:1] * d - tn(f_s[back, :], d.astype(BF16)) + h_s[back, :]
            d_s[pl.ds((r - 1) * head, head), :] = d

    def finish(first):
        for i in range(group):
            span = at(first, i)
            nxt = at(first, i + 1)
            q, k, beta = q_s[span, :], k_s[span, :], b_s[span, :]
            gam, e, tail = gam_s[span, :], e_s[span, :], tail_s[span, :]
            do = cot_ref[span, :]
            m, d = m_s[span, :].astype(BF16), d_s[span, :]
            d16 = d.astype(BF16)
            q16, k16 = q.astype(BF16), k.astype(BF16)
            u = u0_s[span, :] - nn(w_s[span, :], m)
            u16 = u.astype(BF16)
            du = tn(p_s[span, :], do) + nn(kt_s[span, :], d16)
            dr = tn(t_s[span, :], du.astype(BF16))
            dv = beta * dr
            stacked = jnp.concatenate([do, dv.astype(BF16)], 0)
            wide = nt(stacked, jnp.concatenate([u16, m], 0))
            y = (wide[:CHUNK, :CHUNK] * gam).astype(BF16)
            x = jnp.where(strict, wide[CHUNK:, :CHUNK] * gam, 0.0).astype(BF16)
            yx = jnp.concatenate([y, x], 0)
            by_k = nn(yx, k16)
            dq = e * wide[:CHUNK, CHUNK:] + by_k[:CHUNK]
            dkr = -(e * wide[CHUNK:, CHUNK:] + by_k[CHUNK:])
            dkw = tail * nt(u16, d16) + tn(yx, jnp.concatenate([q16, -k16], 0))
            qdq = q * dq
            z = halves(qdq + k * (dkr - dkw))
            sums = nn(high_ones, jnp.concatenate(z, 1))
            dg = row_sum(sums[:, :head] + sums[:, head:]) + jnp.sum(m_s[nxt, :] * d)
            xs = x_s[span, :]
            ga = (dg * rate) * (1.0 / (1.0 + jnp.exp(-xs)))
            gb = row_sum(dr * u) * (1.0 - beta)
            dk = dkr + dkw
            out_ref[span, 0:head] = (qn_s[span, :] * (dq - q * (row_sum(qdq) * head))).astype(BF16)
            out_ref[span, head : 2 * head] = (kn_s[span, :] * (dk - k * row_sum(k * dk))).astype(BF16)
            out_ref[span, 2 * head : 3 * head] = dv.astype(BF16)
            lane = lax.broadcasted_iota(jnp.int32, (CHUNK, head), 1)
            out_ref[span, 3 * head :] = jnp.where(lane == 0, gb, jnp.where(lane == 1, ga, 0.0)).astype(BF16)

    loop(finish)


def core_grads(rows, wq, wq2, wk, wk2, wv, wb, wa, log_rate, rate_bias, cot):
    total, head = cot.shape
    num = total // CHUNK
    col = lambda dt: pltpu.VMEM((total, head), dt)
    states = pltpu.VMEM(((num + 1) * head, head), F32)
    return pl.pallas_call(
        core_kernel,
        out_shape=jax.ShapeDtypeStruct((total, 4 * head), BF16),
        in_specs=[pl.BlockSpec(memory_space=pltpu.VMEM)] * 11,
        out_specs=pl.BlockSpec(memory_space=pltpu.VMEM),
        scratch_shapes=[
            col(F32), col(F32), col(F32), col(F32), col(F32), col(F32), col(BF16), col(BF16), col(BF16), col(F32),
            col(BF16), col(F32), col(F32), col(F32),
            col(BF16), col(F32), col(F32), pltpu.VMEM((num, 8, head), F32), states, states,
        ],
        compiler_params=pltpu.CompilerParams(vmem_limit_bytes=48 * 1024 * 1024),
        name="core_grads",
    )(rows, wq, wq2, wk, wk2, wv, wb, wa, log_rate, rate_bias, cot)


def partner(block, axis):
    count = lax.axis_size(axis)
    return lax.ppermute(block, axis, [(i, i ^ 1) for i in range(count)])


def body(
    hidden, core_grad, query_weight, key_weight, value_weight, beta_weight, decay_weight, decay_log, decay_bias,
):
    half = query_weight.shape[1]
    head = value_weight.shape[1]
    devices = lax.axis_size("head")
    span = hidden.shape[1]
    wq, wk = query_weight.T, key_weight.T
    wq2, wk2 = partner((wq, wk), "head")
    cot = lax.all_to_all(
        core_grad[0].reshape(span, devices, head).transpose(1, 0, 2), "head", split_axis=0, concat_axis=0
    ).reshape(devices * span, head)
    rows = lax.all_gather(hidden[0], "head", axis=0, tiled=True)
    wb, wa = beta_weight.T, decay_weight.T
    grads = core_grads(
        rows, wq, wq2, wk, wk2, value_weight, wb, wa, decay_log.reshape(1, 1), decay_bias.reshape(1, 1), cot
    )
    gq, gk, gv, gba = jnp.split(grads, 4, axis=1)
    dot = lambda a, b, dims: lax.dot_general(a, b, (dims, ((), ())), preferred_element_type=jnp.float32)
    whole_weights = jnp.concatenate([wq, wq2, wk, wk2, value_weight.T, wb, wa], 0)
    term = dot(grads[:, : whole_weights.shape[0]], whole_weights, ((1,), (0,))).astype(jnp.bfloat16)
    token = lax.psum_scatter(term, "head", scatter_dimension=0, tiled=True)
    by_qk = dot(grads[:, : 2 * head], rows, ((0,), (0,)))
    value_sum = dot(rows, gv, ((0,), (0,))).astype(jnp.bfloat16)
    away = jnp.concatenate([by_qk[half:head], by_qk[head + half :]], 0).astype(jnp.bfloat16)
    near = jnp.concatenate([by_qk[:half], by_qk[head : head + half]], 0)
    qk_sum = (near + partner(away, "head").astype(jnp.float32)).astype(jnp.bfloat16)
    qk_total, value_total = lax.psum((qk_sum, value_sum), "dp")
    count = lax.axis_size("dp")
    qk_mean = qk_total.astype(jnp.float32) / count
    return token[None], qk_mean[:half].T, qk_mean[half:].T, value_total.astype(jnp.float32) / count


def solution(mesh):
    rows = P("dp", "head", None)
    cols = P(None, "head")
    return jax.shard_map(
        body,
        mesh=mesh,
        in_specs=(rows, rows, cols, cols, cols, cols, cols, P("head"), P("head")),
        out_specs=(rows, cols, cols, cols),
        check_vma=False,
    )
```

time: 503 us -> 137 us (0.27); the launches traced: 496 us -> 137 us
  other arithmetic: 168 us -> 1.86 us
  matrix products: 134 us -> 3.25 us
  local copies, waits for them, and re-layouts: 68.4 us -> 12.1 us
  loops' own time: 16.6 us -> 0 us
  Pallas kernels: 0 us -> 8.06 us
  waiting for transfers between devices: 83.9 us -> 89 us
    dot_general x147 -> x3, matrix products: 119 us -> 3.25 us  [body(): lax.dot_general(a, b, (dims, ((), ())), preferred_element_type=jnp.float32)]
    another operation x79 -> x0, other arithmetic: 101 us -> none  [the longest x48 85.9 us: advance(): jax.scipy.linalg.solve_triangular(identity + mixing, target, lower=True,...]
    reduce_sum x34 -> x0, other arithmetic: 31.8 us -> none  [the longest x8 11.7 us: advance(): jnp.exp(cumulative[-1]) * memory]
    dynamic_slice x32 -> x0, local copies, waits for them, and re-layouts: 18.1 us -> none  [blockwise_core(): final_memory, outputs = lax.scan(advance, start_memory, block_inputs)]
    another operation x2 -> x0, loops' own time: 16.6 us -> none  [blockwise_core(): final_memory, outputs = lax.scan(advance, start_memory, block_inputs)]
    mul x35 -> x0, local copies, waits for them, and re-layouts: 15.9 us -> none  [the longest x8 5.19 us: advance(): fresh_vals * tail_weight[:, None]]
    dynamic_update_slice x24 -> x0, other arithmetic: 15.5 us -> none  [blockwise_core(): final_memory, outputs = lax.scan(advance, start_memory, block_inputs)]
    another operation x24 -> x0, matrix products: 15.3 us -> none  [advance(): jax.scipy.linalg.solve_triangular(identity + mixing, target, lower=True,...]
  transfers between devices with their start and end apart: 8 -> 7, of which waited for: 5 -> 6; matrix products, arithmetic and copies ran while one was open for 4% -> 8% of each run, Pallas kernels for 0% -> 0%
where the time goes in v1:
time: 137 us
  waiting for transfers between devices  89 us (65%)
  between operations  15.2 us (11%)
  local copies, waits for them, and re-layouts  12.1 us (9%)
  Pallas kernels  8.06 us (6%)
  starting transfers between devices  7.33 us (5%)
  matrix products  3.25 us (2%)
  other arithmetic  1.86 us (1%)
    psum x1, waiting for transfers between devices, body(): qk_total, value_total = lax.psum((qk_sum, value_sum), 'dp')  39.2 us
    reduce_scatter x1, waiting for transfers between devices, body(): token = lax.psum_scatter(term, 'head', scatter_dimension=0, tiled=True)  32.3 us
    all_gather x1, waiting for transfers between devices, body(): rows = lax.all_gather(hidden[0], 'head', axis=0, tiled=True)  11.7 us
    pallas_call x1, Pallas kernels, core_grads(): pl.pallas_call(core_kernel, out_shape=jax.ShapeDtypeStruct((total, 4 * he...  8.06 us
    unnamed x24, local copies, waits for them, and re-layouts  6.37 us
    all_to_all x1, starting transfers between devices, body(): lax.all_to_all(core_grad[0].reshape(span, devices, head).transpose(1, 0,...  6.34 us
    all_to_all x1, waiting for transfers between devices, body(): lax.all_to_all(core_grad[0].reshape(span, devices, head).transpose(1, 0,...  4.82 us
    dot_general x3, matrix products, body(): lax.dot_general(a, b, (dims, ((), ())), preferred_element_type=jnp.float32)  3.25 us
  transfers between devices with their start and end apart: 7, of which 6 were waited for; matrix products, arithmetic and copies ran while one was open for 8% of the time, Pallas kernels for 0%

profile of v1, /device:TPU:0, one launch (start us, length us, event | category | flops | bytes accessed | tf_op | source)
XLA Modules:
  0.0 136.8 jit_solution(15555797542077730869)
XLA Ops:
  7.2 0.7 all-gather.3.cloned.1.call-update
  7.9 0.9 copy.21
  8.8 0.7 copy.23
  9.5 6.3 %all-to-all-start = ((bf16[8,64,128]{2,1,0:T(8,128)(2,1)}), bf16[8,64,128]{2,1,0:T(8,128)(2,1)S(1)}, u32[]{:S(2)}, u32[]{:S(2)}) async-start(bf16[8,64,128]{2,1,0:T(8,128)(2,1)} %bitcast.28), calls=%async_computation | async-start | bytes 262144 | tf_op jit(solution)/shard_map/all_to_all | solution.py:256
  15.9 0.5 collective-permute-start
  17.8 0.1 collective-permute-done.1.wk2_ref
  17.9 4.8 %all-to-all-done = bf16[8,64,128]{2,1,0:T(8,128)(2,1)S(1)} async-done(((bf16[8,64,128]{2,1,0:T(8,128)(2,1)}), bf16[8,64,128]{2,1,0:T(8,128)(2,1)S(1)}, u32[]{:S(2)}, u32[]{:S(2)}) %all-to-all-start) | async-done | bytes 131104 | tf_op jit(solution)/shard_map/all_to_all | solution.py:256
  22.7 11.7 %all-gather.3.cloned.1.call-done = bf16[1,512,1024]{2,1,0:T(8,128)(2,1)} async-done(((bf16[1,64,1024]{2,1,0:T(8,128)(2,1)}), bf16[1,512,1024]{2,1,0:T(8,128)(2,1)}) %all-gather.3.cloned.1.call-update) | async-done | bytes 1048592 | tf_op jit(solution)/shard_map/all_gather | solution.py:259
  34.4 1.2 copy-done
  35.7 0.9 copy-done.2
  36.6 0.9 copy-done.4
  37.5 0.7 copy-done.6
  38.2 0.7 copy-done.8
  38.9 8.1 %core_grads.1 = bf16[512,512]{1,0:T(8,128)(2,1)S(1)} custom-call(bf16[512,1024]{1,0:T(8,128)(2,1)S(1)} %bitcast.31, bf16[64,1024]{1,0:T(8,128)(2,1)S(1)} %bitcast.34, bf16[64,1024]{1,0:T(8,128)(2,1)S(1)} %collective-permute-done.wq2_ref, bf16[64,1024]{1,0:T(8,128)(2,1)S(1)} %bitcast.37, bf16[64,1024]{1,0:T(8,128)(2,1)S(1)} %collective-permute-done.1.wk2_ref, ...), custom_call_target="tpu_custom_call" | custom-call | tf_op jit(solution)/shard_map/core_grads/pallas_call | solution.py:227
  46.9 0.5 fusion.10
  47.4 0.3 collective-permute-start.2
  47.8 1.0 fusion
  48.8 0.2 collective-permute-done.2
  49.0 0.8 fusion.2
  49.9 0.2 copy.14
  50.1 0.2 copy.16
  50.3 0.2 copy.18
  50.5 0.2 copy.19
  50.7 0.2 copy.15
  50.9 0.2 copy.17
  51.0 3.0 %concatenate.10 = bf16[386,1024]{0,1:T(8,128)(2,1)S(1)} concatenate(bf16[64,1024]{0,1:T(8,128)(2,1)S(1)} %copy.14, bf16[64,1024]{0,1:T(8,128)(2,1)S(1)} %copy.15, bf16[64,1024]{0,1:T(8,128)(2,1)S(1)} %copy.16, bf16[64,1024]{0,1:T(8,128)(2,1)S(1)} %copy.17, bf16[128,1024]{0,1:T(8,128)(2,1)S(1)} %bitcast.32, bf16[1,1024]{0,1:T(8,128)(2,1)S(1)} %copy.18, bf16[1,1024]{0,1:T(8,128)(2,1)S(1)} %copy.19), dimensions={0} | concatenate | bytes 1581056 | tf_op jit(solution)/shard_map/concatenate | solution.py:266
  54.1 1.8 %convolution_convert_fusion = bf16[512,1024]{1,0:T(8,128)(2,1)} fusion(bf16[386,1024]{0,1:T(8,128)(2,1)S(1)} %concatenate.10, bf16[512,512]{1,0:T(8,128)(2,1)S(1)} %core_grads.1), kind=kOutput, calls=%fused_computation | convolution fusion | flops 405274624 | bytes 2363392 | tf_op jit(solution)/shard_map/dot_general | solution.py:265
  55.9 39.2 %all-reduce.3.cloned.1.call-done = (bf16[128,1024]{1,0:T(8,128)(2,1)}, bf16[1024,128]{0,1:T(8,128)(2,1)}) async-done(((bf16[128,1024]{1,0:T(8,128)(2,1)}, bf16[1024,128]{0,1:T(8,128)(2,1)}), (bf16[128,1024]{1,0:T(8,128)(2,1)}, bf16[1024,128]{0,1:T(8,128)(2,1)})) %all-reduce.3.cloned.1.call-update) | async-done | bytes 524304 | tf_op jit(solution)/shard_map/psum | solution.py:274
  95.0 1.0 convert_multiply_fusion
  96.1 1.0 copy.20
  97.1 0.8 slice_bitcast_fusion
  98.0 32.3 %reduce-scatter.2.cloned.1.call-done = bf16[64,1024]{1,0:T(8,128)(2,1)} async-done(((bf16[512,1024]{1,0:T(8,128)(2,1)}), bf16[64,1024]{1,0:T(8,128)(2,1)}) %reduce-scatter.2.cloned.1.call-update) | async-done | bytes 131088 | tf_op jit(solution)/shard_map/reduce_scatter | solution.py:268
  (28 shorter events, 0.4 us)
Async XLA Ops:
  7.2 27.3 %copy-start.1 = (bf16[1024,128]{1,0:T(8,128)(2,1)S(1)}, bf16[1024,128]{1,0:T(8,128)(2,1)}, u32[]{:S(2)}) copy-start(bf16[1024,128]{1,0:T(8,128)(2,1)} %wv_ref.1) | copy-start | bytes 786436
  7.2 27.3 %all-gather.3.cloned.1.call-start = ((), (), s32[]{:S(2)}) async-start(), calls=%async_computation.3 | async-start | bytes 1179648 | tf_op jit(solution)/shard_map/all_gather | solution.py:259
  9.5 13.2 %all-to-all-start = ((bf16[8,64,128]{2,1,0:T(8,128)(2,1)}), bf16[8,64,128]{2,1,0:T(8,128)(2,1)S(1)}, u32[]{:S(2)}, u32[]{:S(2)}) async-start(bf16[8,64,128]{2,1,0:T(8,128)(2,1)} %bitcast.28), calls=%async_computation | async-start | bytes 262144 | tf_op jit(solution)/shard_map/all_to_all | solution.py:256
  15.9 79.2 %all-reduce.3.cloned.1.call-start = ((), (), s32[]{:S(2)}) async-start(), calls=%async_computation.4 | async-start | bytes 1048576 | tf_op jit(solution)/shard_map/psum | solution.py:274
  15.9 1.9 %collective-permute-start = (bf16[64,1024]{1,0:T(8,128)(2,1)}, bf16[64,1024]{1,0:T(8,128)(2,1)S(1)}, u32[]{:S(2)}, u32[]{:S(2)}) collective-permute-start(bf16[64,1024]{1,0:T(8,128)(2,1)} %bitcast.33), channel_id=1, source_target_pairs={{0,1},{1,0},{2,3},{3,2},{4,5},{5,4},{6,7},{7,6},{8,9},{9,8},{10,11... | collective-permute-start | bytes 393224 | tf_op jit(solution)/shard_map/ppermute | solution.py:244
  16.4 1.6 %collective-permute-start.1 = (bf16[64,1024]{1,0:T(8,128)(2,1)}, bf16[64,1024]{1,0:T(8,128)(2,1)S(1)}, u32[]{:S(2)}, u32[]{:S(2)}) collective-permute-start(bf16[64,1024]{1,0:T(8,128)(2,1)} %bitcast.36), channel_id=1, source_target_pairs={{0,1},{1,0},{2,3},{3,2},{4,5},{5,4},{6,7},{7,6},{8,9},{9,8},{10,11... | collective-permute-start | bytes 393224 | tf_op jit(solution)/shard_map/ppermute | solution.py:244
  34.4 1.2 copy-start
  35.7 0.9 copy-start.2
  36.6 0.9 copy-start.4
  37.5 0.7 copy-start.6
  38.2 0.7 copy-start.8
  47.4 1.6 %collective-permute-start.2 = (bf16[128,1024]{1,0:T(8,128)(2,1)S(1)}, bf16[128,1024]{1,0:T(8,128)(2,1)S(1)}, u32[]{:S(2)}, u32[]{:S(2)}) collective-permute-start(bf16[128,1024]{1,0:T(8,128)(2,1)S(1)} %pad_maximum_fusion), channel_id=1, source_target_pairs={{0,1},{1,0},{2,3},{3,2},{4,5},{5,4},{6,7},{7,6},{8,9},{9,8},{10,11... | collective-permute-start | bytes 786440 | tf_op jit(solution)/shard_map/ppermute | solution.py:244
  48.8 1.1 copy-start.3
  48.8 1.2 copy-start.5
  49.0 1.2 copy-start.7
  49.8 0.7 copy-start.9
  49.8 80.5 %reduce-scatter.2.cloned.1.call-start = ((), (), s32[]{:S(2)}) async-start(), calls=%async_computation.2 | async-start | bytes 1179648 | tf_op jit(solution)/shard_map/reduce_scatter | solution.py:268
  95.0 2.0 %copy-start.10 = (bf16[128,1024]{1,0:T(8,128)(2,1)S(1)}, bf16[128,1024]{1,0:T(8,128)(2,1)}, u32[]{:S(2)}) copy-start(bf16[128,1024]{1,0:T(8,128)(2,1)} %get-tuple-element.8) | copy-start | bytes 786436
Sparse Core Ops, SparseCore 0:
  9.6 24.7 all-gather.2
  49.9 45.0 all-reduce.2
  97.9 32.3 reduce-scatter.1

commit v2 on v1

--- a/solution.py
+++ b/solution.py
@@ -1,3 +1,5 @@
+import functools
+
 import jax
 import jax.numpy as jnp
 from jax import lax
@@ -49,12 +51,29 @@
 
 
 def core_kernel(
-    rows_ref, wq_ref, wq2_ref, wk_ref, wk2_ref, wv_ref, wb_ref, wa_ref, log_ref, bias_ref, cot_ref,
-    out_ref,
-    q_s, k_s, b_s, e_s, tail_s, gam_s, p_s, t_s, w_s, u0_s, kt_s, x_s, qn_s, kn_s,
-    f_s, g_s, h_s, ec_s, m_s, d_s,
+    chips,
+    *refs,
 ):
-    total, head = cot_ref.shape
+    inputs, refs = refs[: 2 * chips], refs[2 * chips :]
+    (
+        wq_ref, wq2_ref, wk_ref, wk2_ref, wv_ref, wb_ref, wa_ref, log_ref, bias_ref,
+        rows_ref, near_ref, away_ref, vsum_ref, mine_ref, theirs_ref,
+        cot_ref, value_ref, kk_s, qk_s, q_s, k_s, b_s, e_s, tail_s, gam_s, p_s, t_s, w_s, u0_s, kt_s, x_s, qn_s, kn_s,
+        f_s, g_s, h_s, ec_s, m_s, d_s,
+    ) = refs
+    place = lax.axis_index("head")
+    core, chip = lax.rem(place, 2), place // 2
+    part = inputs[0].shape[0]
+    features, head = rows_ref.shape[1], cot_ref.shape[1]
+    column = pl.ds(pl.multiple_of(features + core * head, head), head)
+    for far in range(chips):
+        for other in range(2):
+            who = 2 * (chip ^ far) + (core ^ other)
+            span = pl.ds(pl.multiple_of(who * part, part), part)
+            message = inputs[2 * far + other]
+            rows_ref[span, :] = message[:, :features]
+            cot_ref[span, :] = message[:, column]
+    total = cot_ref.shape[0]
     num = total // CHUNK
     group = min(GROUP, num)
     scale = head ** -0.5
@@ -64,6 +83,7 @@
     strict = row_id > col_id
     low_ones = jnp.where(low, 1.0, 0.0).astype(BF16)
     high_ones = jnp.where(row_id <= col_id, 1.0, 0.0).astype(BF16)
+    below_ones = jnp.where(strict, 1.0, 0.0).astype(BF16)
     rate = -jnp.exp(log_ref[...])
     bias = bias_ref[...]
 
@@ -78,7 +98,6 @@
             return pl.ds((first + i) * CHUNK, CHUNK)
         return pl.ds(pl.multiple_of((first + i) * CHUNK, CHUNK), CHUNK)
 
-    features = wv_ref.shape[0]
     narrow = jnp.concatenate(
         [wq_ref[...], wq2_ref[...], wk_ref[...], wk2_ref[...],
          jnp.broadcast_to(wb_ref[...], (head, features)), jnp.broadcast_to(wa_ref[...], (head, features))], 0)
@@ -114,6 +133,8 @@
             a = jnp.where(strict, beta * gam * kk, 0.0)
             p = (gam * qk).astype(BF16)
             kt = (tail * k).astype(BF16)
+            kk_s[spans[i], :] = kk
+            qk_s[spans[i], :] = qk
             q_s[spans[i], :] = q
             k_s[spans[i], :] = k
             b_s[spans[i], :] = beta
@@ -195,53 +216,155 @@
             dv = beta * dr
             stacked = jnp.concatenate([do, dv.astype(BF16)], 0)
             wide = nt(stacked, jnp.concatenate([u16, m], 0))
-            y = (wide[:CHUNK, :CHUNK] * gam).astype(BF16)
-            x = jnp.where(strict, wide[CHUNK:, :CHUNK] * gam, 0.0).astype(BF16)
-            yx = jnp.concatenate([y, x], 0)
+            y32 = wide[:CHUNK, :CHUNK] * gam
+            x32 = jnp.where(strict, wide[CHUNK:, :CHUNK] * gam, 0.0)
+            yx = jnp.concatenate([y32.astype(BF16), x32.astype(BF16)], 0)
             by_k = nn(yx, k16)
-            dq = e * wide[:CHUNK, CHUNK:] + by_k[:CHUNK]
-            dkr = -(e * wide[CHUNK:, CHUNK:] + by_k[CHUNK:])
-            dkw = tail * nt(u16, d16) + tn(yx, jnp.concatenate([q16, -k16], 0))
+            from_q = e * wide[:CHUNK, CHUNK:]
+            from_k = e * wide[CHUNK:, CHUNK:]
+            to_k = tail * nt(u16, d16)
+            dq = from_q + by_k[:CHUNK]
+            dk = to_k - from_k - by_k[CHUNK:] + tn(yx, jnp.concatenate([q16, -k16], 0))
+            zc = halves(jnp.where(strict, y32 * qk_s[span, :], 0.0) - x32 * kk_s[span, :])
+            zr = halves(q * from_q - k * from_k)
+            zt = halves(k * to_k)
+            up = nn(high_ones, jnp.concatenate([*zc, *zr], 1))
+            down = nn(below_ones, jnp.concatenate(zt, 1))
+            crossing = jnp.where(strict, up[:, :head] + up[:, head : 2 * head], 0.0)
+            single = up[:, 2 * head : 3 * head] + up[:, 3 * head :] + down[:, :head] + down[:, head:]
+            dg = row_sum(crossing + single) + jnp.sum(ec_s[first + i][:1] * m_s[span, :] * d)
             qdq = q * dq
-            z = halves(qdq + k * (dkr - dkw))
-            sums = nn(high_ones, jnp.concatenate(z, 1))
-            dg = row_sum(sums[:, :head] + sums[:, head:]) + jnp.sum(m_s[nxt, :] * d)
             xs = x_s[span, :]
             ga = (dg * rate) * (1.0 / (1.0 + jnp.exp(-xs)))
             gb = row_sum(dr * u) * (1.0 - beta)
-            dk = dkr + dkw
-            out_ref[span, 0:head] = (qn_s[span, :] * (dq - q * (row_sum(qdq) * head))).astype(BF16)
-            out_ref[span, head : 2 * head] = (kn_s[span, :] * (dk - k * row_sum(k * dk))).astype(BF16)
-            out_ref[span, 2 * head : 3 * head] = dv.astype(BF16)
+            gq = (qn_s[span, :] * (dq - q * (row_sum(qdq) * head))).astype(BF16)
+            gk = (kn_s[span, :] * (dk - k * row_sum(k * dk))).astype(BF16)
+            gv = dv.astype(BF16)
             lane = lax.broadcasted_iota(jnp.int32, (CHUNK, head), 1)
-            out_ref[span, 3 * head :] = jnp.where(lane == 0, gb, jnp.where(lane == 1, ga, 0.0)).astype(BF16)
+            gba = jnp.where(lane == 2 * core, gb, jnp.where(lane == 2 * core + 1, ga, 0.0)).astype(BF16)
+            half = head // 2
+            near_ref[span, :] = jnp.concatenate([gq[:, :half], gk[:, :half]], 1)
+            away_ref[span, :] = jnp.concatenate([gq[:, half:], gk[:, half:]], 1)
+            value_ref[span, :] = gv
+            g_s2 = jnp.concatenate([gq, gk, gv, gba], 1)
+            swapped = jnp.concatenate([gq[:, half:], gq[:, :half], gk[:, half:], gk[:, :half], gv, gba], 1)
+            pieces = CHUNK // (2 * part)
+            for j in range(pieces):
+                lo = slice(2 * j * part, (2 * j + 1) * part)
+                hi = slice((2 * j + 1) * part, (2 * j + 2) * part)
+                slot = (first + i) * pieces + j
+                to = pl.ds(pl.multiple_of(slot * part, part), part)
+                first_core = core == 0
+                mine_ref[to, :] = jnp.where(first_core, g_s2[lo], g_s2[hi])
+                theirs_ref[to, :] = jnp.where(first_core, swapped[hi], swapped[lo])
 
     loop(finish)
-
-
-def core_grads(rows, wq, wq2, wk, wk2, wv, wb, wa, log_rate, rate_bias, cot):
-    total, head = cot.shape
+    vsum_ref[...] = tn(value_ref[...], rows_ref[...]).astype(BF16)
+
+
+def core_grads(messages, wq, wq2, wk, wk2, wv, wb, wa, log_rate, rate_bias):
+    part, features = messages[0].shape[0], wv.shape[0]
+    head = wv.shape[1]
+    total = part * len(messages)
     num = total // CHUNK
     col = lambda dt: pltpu.VMEM((total, head), dt)
     states = pltpu.VMEM(((num + 1) * head, head), F32)
+    out = lambda rows, cols: jax.ShapeDtypeStruct((rows, cols), BF16)
+    args = (*messages, wq, wq2, wk, wk2, wv, wb, wa, log_rate, rate_bias)
     return pl.pallas_call(
-        core_kernel,
-        out_shape=jax.ShapeDtypeStruct((total, 4 * head), BF16),
-        in_specs=[pl.BlockSpec(memory_space=pltpu.VMEM)] * 11,
-        out_specs=pl.BlockSpec(memory_space=pltpu.VMEM),
+        functools.partial(core_kernel, len(messages) // 2),
+        out_shape=(
+            out(total, features), out(total, head), out(total, head), out(head, features),
+            out(total // 2, 4 * head), out(total // 2, 4 * head),
+        ),
+        in_specs=[pl.BlockSpec(memory_space=pltpu.VMEM)] * len(args),
+        out_specs=[pl.BlockSpec(memory_space=pltpu.VMEM)] * 6,
         scratch_shapes=[
+            col(BF16), col(BF16), col(F32), col(F32),
             col(F32), col(F32), col(F32), col(F32), col(F32), col(F32), col(BF16), col(BF16), col(BF16), col(F32),
             col(BF16), col(F32), col(F32), col(F32),
             col(BF16), col(F32), col(F32), pltpu.VMEM((num, 8, head), F32), states, states,
         ],
         compiler_params=pltpu.CompilerParams(vmem_limit_bytes=48 * 1024 * 1024),
         name="core_grads",
-    )(rows, wq, wq2, wk, wk2, wv, wb, wa, log_rate, rate_bias, cot)
-
-
-def partner(block, axis):
-    count = lax.axis_size(axis)
-    return lax.ppermute(block, axis, [(i, i ^ 1) for i in range(count)])
+    )(*args)
+
+
+def pack_kernel(chips, hidden_ref, cot_ref, *outs):
+    chip = lax.axis_index("head") // 2
+    width, features = cot_ref.shape[1] // chips, hidden_ref.shape[1]
+    for far, out in enumerate(outs):
+        out[:, :features] = hidden_ref[...]
+        out[:, features:] = cot_ref[:, pl.ds(pl.multiple_of((chip ^ far) * width, width), width)]
+
+
+def product_kernel(
+    part, rows_ref, near_ref, away_ref, mine_ref, recv_ref,
+    wq_ref, wq2_ref, wk_ref, wk2_ref, wv_ref, wv2_ref, wb_ref, wa_ref, wb2_ref, wa2_ref, out_ref, *outs
+):
+    rows = rows_ref[...]
+    out_ref[...] = (tn(near_ref[...], rows) + tn(away_ref[...], rows)).astype(BF16)
+    place = lax.axis_index("head")
+    core, chip = lax.rem(place, 2), place // 2
+    head = wv_ref.shape[1]
+    narrow = jnp.concatenate([wq_ref[...], wq2_ref[...], wk_ref[...], wk2_ref[...]], 0)
+    features = narrow.shape[1]
+    line = lax.broadcasted_iota(jnp.int32, (16, features), 0)
+    small = jnp.zeros((16, features), F32)
+    for offset, ref in ((2 * core, wb_ref), (2 * core + 1, wa_ref), (2 - 2 * core, wb2_ref), (3 - 2 * core, wa2_ref)):
+        small = jnp.where(line == offset, ref[...].astype(F32), small)
+    small = small.astype(BF16)
+    for far, out in enumerate(outs):
+        to = pl.ds(pl.multiple_of((chip ^ far) * part, part), part)
+        mine, recv = mine_ref[to, :], recv_ref[to, :]
+        both = nn(jnp.concatenate([mine[:, : 2 * head], recv[:, : 2 * head]], 1), jnp.concatenate([narrow, narrow], 0))
+        both = both + nt(mine[:, 2 * head : 3 * head], wv_ref[...]) + nt(recv[:, 2 * head : 3 * head], wv2_ref[...])
+        both = both + nn((mine[:, 3 * head :] + recv[:, 3 * head :])[:, :16], small)
+        out[...] = both.astype(BF16)
+
+
+def sum_kernel(*refs):
+    total = refs[0][...].astype(F32)
+    for ref in refs[1:-1]:
+        total = total + ref[...].astype(F32)
+    refs[-1][...] = total.astype(BF16)
+
+
+def mean_kernel(count, own_qk, recv_qk, own_v, recv_v, q_ref, k_ref, v_ref):
+    half = q_ref.shape[0]
+    qk = (own_qk[...].astype(F32) + recv_qk[...].astype(F32)) * (1.0 / count)
+    q_ref[...] = qk[:half]
+    k_ref[...] = qk[half:]
+    v_ref[...] = ((own_v[...].astype(F32) + recv_v[...].astype(F32)) * (1.0 / count)).T
+
+
+def local_call(body, outs, args, name):
+    many = isinstance(outs, tuple)
+    spec = pl.BlockSpec(memory_space=pltpu.VMEM)
+    return pl.pallas_call(
+        body,
+        out_shape=outs,
+        in_specs=[spec] * len(args),
+        out_specs=[spec] * len(outs) if many else spec,
+        compiler_params=pltpu.CompilerParams(vmem_limit_bytes=48 * 1024 * 1024),
+        name=name,
+    )(*args)
+
+
+def across(block, distance):
+    count = lax.axis_size("head")
+    return lax.ppermute(block, "head", [(i, i ^ distance) for i in range(count)])
+
+
+def across_data(block, step):
+    groups, places = lax.axis_size("dp"), lax.axis_size("head")
+    bits = groups.bit_length() - 1
+    route = []
+    for g in range(groups):
+        for p in range(places):
+            bit = step if p % 2 == 0 else bits - 1 - step
+            route.append((g * places + p, (g ^ (1 << bit)) * places + p))
+    return lax.ppermute(block, ("dp", "head"), route)
 
 
 def body(
@@ -249,32 +372,47 @@
 ):
     half = query_weight.shape[1]
     head = value_weight.shape[1]
-    devices = lax.axis_size("head")
-    span = hidden.shape[1]
+    chips = lax.axis_size("head") // 2
+    part, features = hidden.shape[1:]
+    order = sorted(range(1, chips), key=lambda d: -d)
+    block = lambda rows, dt: jax.ShapeDtypeStruct((rows, features), dt)
+    sent = local_call(
+        functools.partial(pack_kernel, chips),
+        (jax.ShapeDtypeStruct((part, features + 2 * head), BF16),) * chips, (hidden[0], core_grad[0]), "pack",
+    )
     wq, wk = query_weight.T, key_weight.T
-    wq2, wk2 = partner((wq, wk), "head")
-    cot = lax.all_to_all(
-        core_grad[0].reshape(span, devices, head).transpose(1, 0, 2), "head", split_axis=0, concat_axis=0
-    ).reshape(devices * span, head)
-    rows = lax.all_gather(hidden[0], "head", axis=0, tiled=True)
     wb, wa = beta_weight.T, decay_weight.T
-    grads = core_grads(
-        rows, wq, wq2, wk, wk2, value_weight, wb, wa, decay_log.reshape(1, 1), decay_bias.reshape(1, 1), cot
+    got = {d: across(sent[d], 2 * d) for d in order}
+    got[0] = sent[0]
+    messages = []
+    for d in range(chips):
+        messages += [got[d], across(got[d], 1)]
+    wq2, wk2, wv2, wb2, wa2 = (across(w, 1) for w in (wq, wk, value_weight, wb, wa))
+
+    all_rows, near, away, value, mine, theirs = core_grads(
+        messages, wq, wq2, wk, wk2, value_weight, wb, wa, decay_log.reshape(1, 1), decay_bias.reshape(1, 1)
     )
-    gq, gk, gv, gba = jnp.split(grads, 4, axis=1)
-    dot = lambda a, b, dims: lax.dot_general(a, b, (dims, ((), ())), preferred_element_type=jnp.float32)
-    whole_weights = jnp.concatenate([wq, wq2, wk, wk2, value_weight.T, wb, wa], 0)
-    term = dot(grads[:, : whole_weights.shape[0]], whole_weights, ((1,), (0,))).astype(jnp.bfloat16)
-    token = lax.psum_scatter(term, "head", scatter_dimension=0, tiled=True)
-    by_qk = dot(grads[:, : 2 * head], rows, ((0,), (0,)))
-    value_sum = dot(rows, gv, ((0,), (0,))).astype(jnp.bfloat16)
-    away = jnp.concatenate([by_qk[half:head], by_qk[head + half :]], 0).astype(jnp.bfloat16)
-    near = jnp.concatenate([by_qk[:half], by_qk[head : head + half]], 0)
-    qk_sum = (near + partner(away, "head").astype(jnp.float32)).astype(jnp.bfloat16)
-    qk_total, value_total = lax.psum((qk_sum, value_sum), "dp")
-    count = lax.axis_size("dp")
-    qk_mean = qk_total.astype(jnp.float32) / count
-    return token[None], qk_mean[:half].T, qk_mean[half:].T, value_total.astype(jnp.float32) / count
+    recv = across(away, 1)
+    other = across(theirs, 1)
+    qk, *terms = local_call(
+        functools.partial(product_kernel, part), (block(head, BF16),) + (block(part, BF16),) * chips,
+        (all_rows, near, recv, mine, other, wq, wq2, wk, wk2, value_weight, wv2, wb, wa, wb2, wa2), "products",
+    )
+    received = [across(terms[d], 2 * d) for d in order]
+    groups = lax.axis_size("dp")
+    rounds = groups.bit_length() - 1
+    sums = {"value": value, "qk": qk}
+    for step in range(rounds - 1):
+        for name in sums:
+            sums[name] = (sums[name].astype(F32) + across_data(sums[name], step).astype(F32)).astype(BF16)
+    last = {name: across_data(sums[name], rounds - 1) for name in sums}
+    token = local_call(sum_kernel, block(part, BF16), (terms[0], *received), "token_sum")
+    q_mean, k_mean, v_mean = local_call(
+        functools.partial(mean_kernel, groups),
+        (block(half, F32), block(half, F32), jax.ShapeDtypeStruct((features, head), F32)),
+        (sums["qk"], last["qk"], sums["value"], last["value"]), "weight_mean",
+    )
+    return token[None], q_mean.T, k_mean.T, v_mean
 
 
 def solution(mesh):

time: 137 us -> 65.4 us (0.48)
  waiting for transfers between devices: 89 us -> 28.4 us
  between operations: 15.2 us -> 2.05 us
  starting transfers between devices: 7.33 us -> 18.5 us
  local copies, waits for them, and re-layouts: 12.1 us -> 3.78 us
  Pallas kernels: 8.06 us -> 12.2 us
  matrix products: 3.25 us -> 0 us
  other arithmetic: 1.86 us -> 0.13 us
    psum x1 -> x0, waiting for transfers between devices: 39.2 us -> none  [body(): qk_total, value_total = lax.psum((qk_sum, value_sum), 'dp')]
    reduce_scatter x1 -> x0, waiting for transfers between devices: 32.3 us -> none  [body(): token = lax.psum_scatter(term, 'head', scatter_dimension=0, tiled=True)]
    ppermute x3 -> x21, waiting for transfers between devices: 0.35 us -> 28.4 us  [the longest x17 22.1 us: across(): lax.ppermute(block, 'head', [(i, i ^ distance) for i in range(count)])]
    ppermute x3 -> x21, starting transfers between devices: 0.87 us -> 18.5 us  [the longest x17 12.9 us: across(): lax.ppermute(block, 'head', [(i, i ^ distance) for i in range(count)])]
    all_gather x1 -> x0, waiting for transfers between devices: 11.7 us -> none  [body(): rows = lax.all_gather(hidden[0], 'head', axis=0, tiled=True)]
    all_to_all x1 -> x0, starting transfers between devices: 6.34 us -> none  [body(): lax.all_to_all(core_grad[0].reshape(span, devices, head).transpose(1, 0,...]
    all_to_all x1 -> x0, waiting for transfers between devices: 4.82 us -> none  [body(): lax.all_to_all(core_grad[0].reshape(span, devices, head).transpose(1, 0,...]
    pallas_call x1 -> x5, Pallas kernels: 8.06 us -> 12.2 us  [the longest x1 8.23 us: core_grads(): pl.pallas_call(functools.partial(core_kernel, len(messages) // 2), out_sh...]
  transfers between devices with their start and end apart: 7 -> 21, of which waited for: 6 -> 8; matrix products, arithmetic and copies ran while one was open for 8% -> 0% of each run, Pallas kernels for 0% -> 17%
where the time goes in v2:
time: 65.4 us; the launch traced here: 65.1 us
  waiting for transfers between devices  28.4 us (43%)
  starting transfers between devices  18.5 us (28%)
  Pallas kernels  12.2 us (19%)
  local copies, waits for them, and re-layouts  3.78 us (6%)
  between operations  2.05 us (3%)
    ppermute x17, waiting for transfers between devices, across(): lax.ppermute(block, 'head', [(i, i ^ distance) for i in range(count)])  22.1 us
    ppermute x17, starting transfers between devices, across(): lax.ppermute(block, 'head', [(i, i ^ distance) for i in range(count)])  12.9 us
    pallas_call x1, Pallas kernels, core_grads(): pl.pallas_call(functools.partial(core_kernel, len(messages) // 2), out_sh...  8.23 us
    ppermute x4, waiting for transfers between devices, across_data(): return lax.ppermute(block, ('dp', 'head'), route)  6.3 us
    ppermute x4, starting transfers between devices, across_data(): return lax.ppermute(block, ('dp', 'head'), route)  5.68 us
    pallas_call x4, Pallas kernels, local_call(): pl.pallas_call(body, out_shape=outs, in_specs=[spec] * len(args), out_spe...  3.98 us
    unnamed x14, local copies, waits for them, and re-layouts  3.78 us
  transfers between devices with their start and end apart: 21, of which 8 were waited for; matrix products, arithmetic and copies ran while one was open for 0% of the time, Pallas kernels for 17%

profile of v2, /device:TPU:0, one launch (start us, length us, event | category | flops | bytes accessed | tf_op | source)
XLA Modules:
  0.0 65.1 jit_solution(15509023516125439491)
XLA Ops:
  0.7 0.9 %copy-done.3 = bf16[1,64,1024]{2,1,0:T(8,128)(2,1)S(1)} copy-done((bf16[1,64,1024]{2,1,0:T(8,128)(2,1)S(1)}, bf16[1,64,1024]{2,1,0:T(8,128)(2,1)}, u32[]{:S(2)}) %copy-start.3) | copy-done | bytes 131096
  1.6 0.9 %copy-done.4 = bf16[1,64,1024]{2,1,0:T(8,128)(2,1)S(1)} copy-done((bf16[1,64,1024]{2,1,0:T(8,128)(2,1)S(1)}, bf16[1,64,1024]{2,1,0:T(8,128)(2,1)}, u32[]{:S(2)}) %copy-start.4) | copy-done | bytes 131096
  2.5 3.1 %collective-permute-start.1 = (bf16[64,1280]{1,0:T(8,128)(2,1)S(1)}, bf16[64,1280]{1,0:T(8,128)(2,1)S(1)}, u32[]{:S(2)}, u32[]{:S(2)}) collective-permute-start(bf16[64,1280]{1,0:T(8,128)(2,1)S(1)} %get-tuple-element.23), channel_id=1, source_target_pairs={{0,2},{1,3},{2,0},{3,1},{4,6},{5,7},{6,4},{7,5},{8,10},{9,11},{10,... | collective-permute-start | bytes 491528 | tf_op jit(solution)/shard_map/ppermute | solution.py:356
  5.6 2.6 %collective-permute-start.3 = (bf16[64,1280]{1,0:T(8,128)(2,1)S(1)}, bf16[64,1280]{1,0:T(8,128)(2,1)S(1)}, u32[]{:S(2)}, u32[]{:S(2)}) collective-permute-start(bf16[64,1280]{1,0:T(8,128)(2,1)S(1)} %get-tuple-element.24), channel_id=1, source_target_pairs={{0,4},{1,5},{2,6},{3,7},{4,0},{5,1},{6,2},{7,3},{8,12},{9,13},{10,... | collective-permute-start | bytes 491528 | tf_op jit(solution)/shard_map/ppermute | solution.py:356
  8.2 0.5 collective-permute-start
  8.7 3.6 %collective-permute-done.1.refs_2_ = bf16[64,1280]{1,0:T(8,128)(2,1)S(1)} collective-permute-done((bf16[64,1280]{1,0:T(8,128)(2,1)S(1)}, bf16[64,1280]{1,0:T(8,128)(2,1)S(1)}, u32[]{:S(2)}, u32[]{:S(2)}) %collective-permute-start.1) | collective-permute-done | bytes 163872 | tf_op jit(solution)/shard_map/ppermute | solution.py:356
  12.3 8.4 %collective-permute-done.3.refs_4_ = bf16[64,1280]{1,0:T(8,128)(2,1)S(1)} collective-permute-done((bf16[64,1280]{1,0:T(8,128)(2,1)S(1)}, bf16[64,1280]{1,0:T(8,128)(2,1)S(1)}, u32[]{:S(2)}, u32[]{:S(2)}) %collective-permute-start.3) | collective-permute-done | bytes 163872 | tf_op jit(solution)/shard_map/ppermute | solution.py:356
  20.7 0.5 collective-permute-start.6
  22.6 0.2 collective-permute-done.8.refs_11_.wk2_ref
  22.8 0.4 collective-permute-start.11
  23.2 0.1 copy-done.5
  23.3 0.9 %copy-done.1 = bf16[1024,64]{0,1:T(8,128)(2,1)S(1)} copy-done((bf16[1024,64]{0,1:T(8,128)(2,1)S(1)}, bf16[1024,64]{0,1:T(8,128)(2,1)}, u32[]{:S(2)}) %copy-start.1) | copy-done | bytes 131096
  24.2 0.9 %copy-done.2 = bf16[1024,64]{0,1:T(8,128)(2,1)S(1)} copy-done((bf16[1024,64]{0,1:T(8,128)(2,1)S(1)}, bf16[1024,64]{0,1:T(8,128)(2,1)}, u32[]{:S(2)}) %copy-start.2) | copy-done | bytes 131096
  25.1 8.2 %core_grads.1 = (bf16[512,1024]{1,0:T(8,128)(2,1)S(1)}, bf16[512,128]{1,0:T(8,128)(2,1)S(1)}, bf16[512,128]{1,0:T(8,128)(2,1)S(1)}, bf16[128,1024]{1,0:T(8,128)(...) custom-call(bf16[64,1280]{1,0:T(8,128)(2,1)S(1)} %get-tuple-element.22.refs_0_, ...), custom_call_target="tpu_custom_call" | custom-call | tf_op jit(solution)/shard_map/core_grads/pallas_call | solution.py:274
  33.3 0.5 collective-permute-start.10
  33.8 1.5 %collective-permute-start.19 = (bf16[128,1024]{1,0:T(8,128)(2,1)S(1)}, bf16[128,1024]{1,0:T(8,128)(2,1)S(1)}, u32[]{:S(2)}, u32[]{:S(2)}) collective-permute-start(bf16[128,1024]{1,0:T(8,128)(2,1)S(1)} %get-tuple-element.36), channel_id=1, source_target_pairs={{0,8},{1,17},{2,10},{3,19},{4,12},{5,21},{6,14},{7,23},{8,0},{9,25... | collective-permute-start | bytes 786440 | tf_op jit(solution)/shard_map/ppermute | solution.py:367
  35.3 0.5 collective-permute-start.12
  35.8 0.8 %collective-permute-done.12.wb2_ref = bf16[1,1024]{1,0:T(2,128)(2,1)S(1)} collective-permute-done((bf16[1,1024]{1,0:T(2,128)(2,1)S(1)}, bf16[1,1024]{1,0:T(2,128)(2,1)S(1)}, u32[]{:S(2)}, u32[]{:S(2)}) %collective-permute-start.12) | collective-permute-done | bytes 2080 | tf_op jit(solution)/shard_map/ppermute | solution.py:356
  36.7 0.3 collective-permute-start.13
  37.0 0.8 %collective-permute-done.13.wa2_ref = bf16[1,1024]{1,0:T(2,128)(2,1)S(1)} collective-permute-done((bf16[1,1024]{1,0:T(2,128)(2,1)S(1)}, bf16[1,1024]{1,0:T(2,128)(2,1)S(1)}, u32[]{:S(2)}, u32[]{:S(2)}) %collective-permute-start.13) | collective-permute-done | bytes 2080 | tf_op jit(solution)/shard_map/ppermute | solution.py:356
  37.9 2.0 %products.1 = (bf16[128,1024]{1,0:T(8,128)(2,1)S(1)}, bf16[64,1024]{1,0:T(8,128)(2,1)S(1)}, bf16[64,1024]{1,0:T(8,128)(2,1)S(1)}, bf16[64,1024]{1,0:T(8,128)(2,1)S(1)}, bf16[64,1024]{1,0:T(8,128)(2,1)S(1)}) custom-call(bf16[512,1024]{1,0:T(8,128)(2,1)S(1)} %get-tuple-element.26.rows_ref, bf16[512,128]{1,0:T(8,128)(2,1)S(1)} %get-tuple-element.27.near_ref, ...), custom_call_target="tpu_custom_call" | custom-call | tf_op jit(solution)/shard_map/products/pallas_call | solution.py:344
  39.9 1.2 %collective-permute-start.17 = (bf16[128,1024]{1,0:T(8,128)(2,1)S(1)}, bf16[128,1024]{1,0:T(8,128)(2,1)S(1)}, u32[]{:S(2)}, u32[]{:S(2)}) collective-permute-start(bf16[128,1024]{1,0:T(8,128)(2,1)S(1)} %get-tuple-element.35), channel_id=1, source_target_pairs={{0,8},{1,17},{2,10},{3,19},{4,12},{5,21},{6,14},{7,23},{8,0},{9,25... | collective-permute-start | bytes 786440 | tf_op jit(solution)/shard_map/ppermute | solution.py:367
  41.2 1.0 %collective-permute-start.20 = (bf16[128,1024]{1,0:T(8,128)(2,1)S(1)}, bf16[128,1024]{1,0:T(8,128)(2,1)S(1)}, u32[]{:S(2)}, u32[]{:S(2)}) collective-permute-start(bf16[128,1024]{1,0:T(8,128)(2,1)S(1)} %add_convert_fusion.own_v), channel_id=1, source_target_pairs={{0,16},{1,9},{2,18},{3,11},{4,20},{5,13},{6,22},{7,15},{8,24},{9,1... | collective-permute-start | bytes 786440 | tf_op jit(solution)/shard_map/ppermute | solution.py:367
  42.2 6.3 %collective-permute-done.17 = bf16[128,1024]{1,0:T(8,128)(2,1)S(1)} collective-permute-done((bf16[128,1024]{1,0:T(8,128)(2,1)S(1)}, bf16[128,1024]{1,0:T(8,128)(2,1)S(1)}, u32[]{:S(2)}, u32[]{:S(2)}) %collective-permute-start.17) | collective-permute-done | bytes 262176 | tf_op jit(solution)/shard_map/ppermute | solution.py:367
  48.5 2.0 %collective-permute-start.18 = (bf16[128,1024]{1,0:T(8,128)(2,1)S(1)}, bf16[128,1024]{1,0:T(8,128)(2,1)S(1)}, u32[]{:S(2)}, u32[]{:S(2)}) collective-permute-start(bf16[128,1024]{1,0:T(8,128)(2,1)S(1)} %add_convert_fusion.1.own_qk), channel_id=1, source_target_pairs={{0,16},{1,9},{2,18},{3,11},{4,20},{5,13},{6,22},{7,15},{8,24},{9,1... | collective-permute-start | bytes 786440 | tf_op jit(solution)/shard_map/ppermute | solution.py:367
  50.5 2.3 %collective-permute-start.14 = (bf16[64,1024]{1,0:T(8,128)(2,1)S(1)}, bf16[64,1024]{1,0:T(8,128)(2,1)S(1)}, u32[]{:S(2)}, u32[]{:S(2)}) collective-permute-start(bf16[64,1024]{1,0:T(8,128)(2,1)S(1)} %get-tuple-element.32), channel_id=1, source_target_pairs={{0,6},{1,7},{2,4},{3,5},{4,2},{5,3},{6,0},{7,1},{8,14},{9,15},{10,... | collective-permute-start | bytes 393224 | tf_op jit(solution)/shard_map/ppermute | solution.py:356
  52.8 1.4 %collective-permute-start.15 = (bf16[64,1024]{1,0:T(8,128)(2,1)S(1)}, bf16[64,1024]{1,0:T(8,128)(2,1)S(1)}, u32[]{:S(2)}, u32[]{:S(2)}) collective-permute-start(bf16[64,1024]{1,0:T(8,128)(2,1)S(1)} %get-tuple-element.33), channel_id=1, source_target_pairs={{0,4},{1,5},{2,6},{3,7},{4,0},{5,1},{6,2},{7,3},{8,12},{9,13},{10,... | collective-permute-start | bytes 393224 | tf_op jit(solution)/shard_map/ppermute | solution.py:356
  54.2 0.7 %collective-permute-start.16 = (bf16[64,1024]{1,0:T(8,128)(2,1)S(1)}, bf16[64,1024]{1,0:T(8,128)(2,1)S(1)}, u32[]{:S(2)}, u32[]{:S(2)}) collective-permute-start(bf16[64,1024]{1,0:T(8,128)(2,1)S(1)} %get-tuple-element.34), channel_id=1, source_target_pairs={{0,2},{1,3},{2,0},{3,1},{4,6},{5,7},{6,4},{7,5},{8,10},{9,11},{10,... | collective-permute-start | bytes 393224 | tf_op jit(solution)/shard_map/ppermute | solution.py:356
  54.9 3.8 %collective-permute-done.14.refs_1_ = bf16[64,1024]{1,0:T(8,128)(2,1)S(1)} collective-permute-done((bf16[64,1024]{1,0:T(8,128)(2,1)S(1)}, bf16[64,1024]{1,0:T(8,128)(2,1)S(1)}, u32[]{:S(2)}, u32[]{:S(2)}) %collective-permute-start.14) | collective-permute-done | bytes 131104 | tf_op jit(solution)/shard_map/ppermute | solution.py:356
  58.7 4.5 %collective-permute-done.15.refs_2_ = bf16[64,1024]{1,0:T(8,128)(2,1)S(1)} collective-permute-done((bf16[64,1024]{1,0:T(8,128)(2,1)S(1)}, bf16[64,1024]{1,0:T(8,128)(2,1)S(1)}, u32[]{:S(2)}, u32[]{:S(2)}) %collective-permute-start.15) | collective-permute-done | bytes 131104 | tf_op jit(solution)/shard_map/ppermute | solution.py:356
  63.2 0.7 %token_sum.1 = bf16[64,1024]{1,0:T(8,128)(2,1)} custom-call(bf16[64,1024]{1,0:T(8,128)(2,1)S(1)} %get-tuple-element.31.refs_0_, bf16[64,1024]{1,0:T(8,128)(2,1)S(1)} %collective-permute-done.14.refs_1_, bf16[64,1024]{1,0:T(8,128)(2,1)S(1)} %collective-permute-done.15.refs_2_, bf16[64,1024]{1,0:T(8,128)(2,1)S(1)} %collective-permute-done.16.refs_3_), custom_call_target="tpu_custom_call" | custom-call | tf_op jit(solution)/shard_map/token_sum/pallas_call | solution.py:344
  64.0 1.2 %weight_mean.1 = (f32[64,1024]{1,0:T(8,128)}, f32[64,1024]{1,0:T(8,128)}, f32[1024,128]{1,0:T(8,128)}) custom-call(bf16[128,1024]{1,0:T(8,128)(2,1)S(1)} %add_convert_fusion.1.own_qk, bf16[128,1024]{1,0:T(8,128)(2,1)S(1)} %collective-permute-done.18.recv_qk, bf16[128,1024]{1,0:T(8,128)(2,1)S(1)} %add_convert_fusion.own_v, ...), custom_call_target="tpu_custom_call" | custom-call | tf_op jit(solution)/shard_map/weight_mean/pallas_call | solution.py:344
  (31 shorter events, 0.3 us)
Async XLA Ops:
  0.6 22.1 %copy-start = (bf16[1024,128]{1,0:T(8,128)(2,1)S(1)}, bf16[1024,128]{1,0:T(8,128)(2,1)}, u32[]{:S(2)}) copy-start(bf16[1024,128]{1,0:T(8,128)(2,1)} %wv_ref.1) | copy-start | bytes 786436
  0.6 0.9 %copy-start.3 = (bf16[1,64,1024]{2,1,0:T(8,128)(2,1)S(1)}, bf16[1,64,1024]{2,1,0:T(8,128)(2,1)}, u32[]{:S(2)}) copy-start(bf16[1,64,1024]{2,1,0:T(8,128)(2,1)} %param.9) | copy-start | bytes 393220
  1.6 0.9 %copy-start.4 = (bf16[1,64,1024]{2,1,0:T(8,128)(2,1)S(1)}, bf16[1,64,1024]{2,1,0:T(8,128)(2,1)}, u32[]{:S(2)}) copy-start(bf16[1,64,1024]{2,1,0:T(8,128)(2,1)} %param.10) | copy-start | bytes 393220
  2.5 9.8 %collective-permute-start.1 = (bf16[64,1280]{1,0:T(8,128)(2,1)S(1)}, bf16[64,1280]{1,0:T(8,128)(2,1)S(1)}, u32[]{:S(2)}, u32[]{:S(2)}) collective-permute-start(bf16[64,1280]{1,0:T(8,128)(2,1)S(1)} %get-tuple-element.23), channel_id=1, source_target_pairs={{0,2},{1,3},{2,0},{3,1},{4,6},{5,7},{6,4},{7,5},{8,10},{9,11},{10,... | collective-permute-start | bytes 491528 | tf_op jit(solution)/shard_map/ppermute | solution.py:356
  5.6 15.0 %collective-permute-start.3 = (bf16[64,1280]{1,0:T(8,128)(2,1)S(1)}, bf16[64,1280]{1,0:T(8,128)(2,1)S(1)}, u32[]{:S(2)}, u32[]{:S(2)}) collective-permute-start(bf16[64,1280]{1,0:T(8,128)(2,1)S(1)} %get-tuple-element.24), channel_id=1, source_target_pairs={{0,4},{1,5},{2,6},{3,7},{4,0},{5,1},{6,2},{7,3},{8,12},{9,13},{10,... | collective-permute-start | bytes 491528 | tf_op jit(solution)/shard_map/ppermute | solution.py:356
  8.2 12.5 %collective-permute-start.5 = (bf16[64,1280]{1,0:T(8,128)(2,1)S(1)}, bf16[64,1280]{1,0:T(8,128)(2,1)S(1)}, u32[]{:S(2)}, u32[]{:S(2)}) collective-permute-start(bf16[64,1280]{1,0:T(8,128)(2,1)S(1)} %get-tuple-element.25), channel_id=1, source_target_pairs={{0,6},{1,7},{2,4},{3,5},{4,2},{5,3},{6,0},{7,1},{8,14},{9,15},{10,... | collective-permute-start | bytes 491528 | tf_op jit(solution)/shard_map/ppermute | solution.py:356
  8.2 13.0 %collective-permute-start.7 = (bf16[64,1024]{1,0:T(8,128)(2,1)}, bf16[64,1024]{1,0:T(8,128)(2,1)S(1)}, u32[]{:S(2)}, u32[]{:S(2)}) collective-permute-start(bf16[64,1024]{1,0:T(8,128)(2,1)} %bitcast.13), channel_id=1, source_target_pairs={{0,1},{1,0},{2,3},{3,2},{4,5},{5,4},{6,7},{7,6},{8,9},{9,8},{10,11... | collective-permute-start | bytes 393224 | tf_op jit(solution)/shard_map/ppermute | solution.py:356
  8.2 14.9 %collective-permute-start = (bf16[64,1280]{1,0:T(8,128)(2,1)S(1)}, bf16[64,1280]{1,0:T(8,128)(2,1)S(1)}, u32[]{:S(2)}, u32[]{:S(2)}) collective-permute-start(bf16[64,1280]{1,0:T(8,128)(2,1)S(1)} %get-tuple-element.22.refs_0_), channel_id=1, source_target_pairs={{0,1},{1,0},{2,3},{3,2},{4,5},{5,4},{6,7},{7,6},{8,9},{9,8},{10,11... | collective-permute-start | bytes 491528 | tf_op jit(solution)/shard_map/ppermute | solution.py:356
  12.3 10.8 %collective-permute-start.2 = (bf16[64,1280]{1,0:T(8,128)(2,1)S(1)}, bf16[64,1280]{1,0:T(8,128)(2,1)S(1)}, u32[]{:S(2)}, u32[]{:S(2)}) collective-permute-start(bf16[64,1280]{1,0:T(8,128)(2,1)S(1)} %collective-permute-done.1.refs_2_), channel_id=1, source_target_pairs={{0,1},{1,0},{2,3},{3,2},{4,5},{5,4},{6,7},{7,6},{8,9},{9,8},{10,11... | collective-permute-start | bytes 491528 | tf_op jit(solution)/shard_map/ppermute | solution.py:356
  20.7 2.5 %collective-permute-start.4 = (bf16[64,1280]{1,0:T(8,128)(2,1)S(1)}, bf16[64,1280]{1,0:T(8,128)(2,1)S(1)}, u32[]{:S(2)}, u32[]{:S(2)}) collective-permute-start(bf16[64,1280]{1,0:T(8,128)(2,1)S(1)} %collective-permute-done.3.refs_4_), channel_id=1, source_target_pairs={{0,1},{1,0},{2,3},{3,2},{4,5},{5,4},{6,7},{7,6},{8,9},{9,8},{10,11... | collective-permute-start | bytes 491528 | tf_op jit(solution)/shard_map/ppermute | solution.py:356
  20.7 2.5 %collective-permute-start.6 = (bf16[64,1280]{1,0:T(8,128)(2,1)S(1)}, bf16[64,1280]{1,0:T(8,128)(2,1)S(1)}, u32[]{:S(2)}, u32[]{:S(2)}) collective-permute-start(bf16[64,1280]{1,0:T(8,128)(2,1)S(1)} %collective-permute-done.5.refs_6_), channel_id=1, source_target_pairs={{0,1},{1,0},{2,3},{3,2},{4,5},{5,4},{6,7},{7,6},{8,9},{9,8},{10,11... | collective-permute-start | bytes 491528 | tf_op jit(solution)/shard_map/ppermute | solution.py:356
  21.2 1.6 %collective-permute-start.8 = (bf16[64,1024]{1,0:T(8,128)(2,1)}, bf16[64,1024]{1,0:T(8,128)(2,1)S(1)}, u32[]{:S(2)}, u32[]{:S(2)}) collective-permute-start(bf16[64,1024]{1,0:T(8,128)(2,1)} %bitcast.16), channel_id=1, source_target_pairs={{0,1},{1,0},{2,3},{3,2},{4,5},{5,4},{6,7},{7,6},{8,9},{9,8},{10,11... | collective-permute-start | bytes 393224 | tf_op jit(solution)/shard_map/ppermute | solution.py:356
  21.9 1.2 %copy-start.6 = (bf16[1024,1]{0,1:T(2,128)(2,1)S(1)}, bf16[1024,1]{0,1:T(2,128)(2,1)}, u32[]{:S(2)}) copy-start(bf16[1024,1]{0,1:T(2,128)(2,1)} %param.15) | copy-start | bytes 6148
  22.6 0.7 %copy-start.5 = (bf16[1024,1]{0,1:T(2,128)(2,1)S(1)}, bf16[1024,1]{0,1:T(2,128)(2,1)}, u32[]{:S(2)}) copy-start(bf16[1024,1]{0,1:T(2,128)(2,1)} %param.14) | copy-start | bytes 6148
  22.8 15.1 %collective-permute-start.11 = (bf16[1024,128]{1,0:T(8,128)(2,1)S(1)}, bf16[1024,128]{1,0:T(8,128)(2,1)S(1)}, u32[]{:S(2)}, u32[]{:S(2)}) collective-permute-start(bf16[1024,128]{1,0:T(8,128)(2,1)S(1)} %copy-done), channel_id=1, source_target_pairs={{0,1},{1,0},{2,3},{3,2},{4,5},{5,4},{6,7},{7,6},{8,9},{9,8},{10,11... | collective-permute-start | bytes 786440 | tf_op jit(solution)/shard_map/ppermute | solution.py:356
  23.3 0.9 %copy-start.1 = (bf16[1024,64]{0,1:T(8,128)(2,1)S(1)}, bf16[1024,64]{0,1:T(8,128)(2,1)}, u32[]{:S(2)}) copy-start(bf16[1024,64]{0,1:T(8,128)(2,1)} %param.11) | copy-start | bytes 393220
  24.2 0.9 %copy-start.2 = (bf16[1024,64]{0,1:T(8,128)(2,1)S(1)}, bf16[1024,64]{0,1:T(8,128)(2,1)}, u32[]{:S(2)}) copy-start(bf16[1024,64]{0,1:T(8,128)(2,1)} %param.12) | copy-start | bytes 393220
  33.3 4.5 %collective-permute-start.10 = (bf16[256,512]{1,0:T(8,128)(2,1)S(1)}, bf16[256,512]{1,0:T(8,128)(2,1)S(1)}, u32[]{:S(2)}, u32[]{:S(2)}) collective-permute-start(bf16[256,512]{1,0:T(8,128)(2,1)S(1)} %get-tuple-element.30), channel_id=1, source_target_pairs={{0,1},{1,0},{2,3},{3,2},{4,5},{5,4},{6,7},{7,6},{8,9},{9,8},{10,11... | collective-permute-start | bytes 786440 | tf_op jit(solution)/shard_map/ppermute | solution.py:356
  33.8 7.3 %collective-permute-start.19 = (bf16[128,1024]{1,0:T(8,128)(2,1)S(1)}, bf16[128,1024]{1,0:T(8,128)(2,1)S(1)}, u32[]{:S(2)}, u32[]{:S(2)}) collective-permute-start(bf16[128,1024]{1,0:T(8,128)(2,1)S(1)} %get-tuple-element.36), channel_id=1, source_target_pairs={{0,8},{1,17},{2,10},{3,19},{4,12},{5,21},{6,14},{7,23},{8,0},{9,25... | collective-permute-start | bytes 786440 | tf_op jit(solution)/shard_map/ppermute | solution.py:367
  35.3 2.5 %collective-permute-start.9 = (bf16[512,128]{1,0:T(8,128)(2,1)S(1)}, bf16[512,128]{1,0:T(8,128)(2,1)S(1)}, u32[]{:S(2)}, u32[]{:S(2)}) collective-permute-start(bf16[512,128]{1,0:T(8,128)(2,1)S(1)} %get-tuple-element.28), channel_id=1, source_target_pairs={{0,1},{1,0},{2,3},{3,2},{4,5},{5,4},{6,7},{7,6},{8,9},{9,8},{10,11... | collective-permute-start | bytes 393224 | tf_op jit(solution)/shard_map/ppermute | solution.py:356
  35.3 1.4 %collective-permute-start.12 = (bf16[1,1024]{1,0:T(2,128)(2,1)S(1)}, bf16[1,1024]{1,0:T(2,128)(2,1)S(1)}, u32[]{:S(2)}, u32[]{:S(2)}) collective-permute-start(bf16[1,1024]{1,0:T(2,128)(2,1)S(1)} %bitcast.22), channel_id=1, source_target_pairs={{0,1},{1,0},{2,3},{3,2},{4,5},{5,4},{6,7},{7,6},{8,9},{9,8},{10,11... | collective-permute-start | bytes 6152 | tf_op jit(solution)/shard_map/ppermute | solution.py:356
  36.7 1.2 %collective-permute-start.13 = (bf16[1,1024]{1,0:T(2,128)(2,1)S(1)}, bf16[1,1024]{1,0:T(2,128)(2,1)S(1)}, u32[]{:S(2)}, u32[]{:S(2)}) collective-permute-start(bf16[1,1024]{1,0:T(2,128)(2,1)S(1)} %bitcast.25), channel_id=1, source_target_pairs={{0,1},{1,0},{2,3},{3,2},{4,5},{5,4},{6,7},{7,6},{8,9},{9,8},{10,11... | collective-permute-start | bytes 6152 | tf_op jit(solution)/shard_map/ppermute | solution.py:356
  39.9 8.5 %collective-permute-start.17 = (bf16[128,1024]{1,0:T(8,128)(2,1)S(1)}, bf16[128,1024]{1,0:T(8,128)(2,1)S(1)}, u32[]{:S(2)}, u32[]{:S(2)}) collective-permute-start(bf16[128,1024]{1,0:T(8,128)(2,1)S(1)} %get-tuple-element.35), channel_id=1, source_target_pairs={{0,8},{1,17},{2,10},{3,19},{4,12},{5,21},{6,14},{7,23},{8,0},{9,25... | collective-permute-start | bytes 786440 | tf_op jit(solution)/shard_map/ppermute | solution.py:367
  41.2 22.8 %collective-permute-start.20 = (bf16[128,1024]{1,0:T(8,128)(2,1)S(1)}, bf16[128,1024]{1,0:T(8,128)(2,1)S(1)}, u32[]{:S(2)}, u32[]{:S(2)}) collective-permute-start(bf16[128,1024]{1,0:T(8,128)(2,1)S(1)} %add_convert_fusion.own_v), channel_id=1, source_target_pairs={{0,16},{1,9},{2,18},{3,11},{4,20},{5,13},{6,22},{7,15},{8,24},{9,1... | collective-permute-start | bytes 786440 | tf_op jit(solution)/shard_map/ppermute | solution.py:367
  48.5 15.4 %collective-permute-start.18 = (bf16[128,1024]{1,0:T(8,128)(2,1)S(1)}, bf16[128,1024]{1,0:T(8,128)(2,1)S(1)}, u32[]{:S(2)}, u32[]{:S(2)}) collective-permute-start(bf16[128,1024]{1,0:T(8,128)(2,1)S(1)} %add_convert_fusion.1.own_qk), channel_id=1, source_target_pairs={{0,16},{1,9},{2,18},{3,11},{4,20},{5,13},{6,22},{7,15},{8,24},{9,1... | collective-permute-start | bytes 786440 | tf_op jit(solution)/shard_map/ppermute | solution.py:367
  50.5 8.2 %collective-permute-start.14 = (bf16[64,1024]{1,0:T(8,128)(2,1)S(1)}, bf16[64,1024]{1,0:T(8,128)(2,1)S(1)}, u32[]{:S(2)}, u32[]{:S(2)}) collective-permute-start(bf16[64,1024]{1,0:T(8,128)(2,1)S(1)} %get-tuple-element.32), channel_id=1, source_target_pairs={{0,6},{1,7},{2,4},{3,5},{4,2},{5,3},{6,0},{7,1},{8,14},{9,15},{10,... | collective-permute-start | bytes 393224 | tf_op jit(solution)/shard_map/ppermute | solution.py:356
  52.8 10.4 %collective-permute-start.15 = (bf16[64,1024]{1,0:T(8,128)(2,1)S(1)}, bf16[64,1024]{1,0:T(8,128)(2,1)S(1)}, u32[]{:S(2)}, u32[]{:S(2)}) collective-permute-start(bf16[64,1024]{1,0:T(8,128)(2,1)S(1)} %get-tuple-element.33), channel_id=1, source_target_pairs={{0,4},{1,5},{2,6},{3,7},{4,0},{5,1},{6,2},{7,3},{8,12},{9,13},{10,... | collective-permute-start | bytes 393224 | tf_op jit(solution)/shard_map/ppermute | solution.py:356
  54.2 9.0 %collective-permute-start.16 = (bf16[64,1024]{1,0:T(8,128)(2,1)S(1)}, bf16[64,1024]{1,0:T(8,128)(2,1)S(1)}, u32[]{:S(2)}, u32[]{:S(2)}) collective-permute-start(bf16[64,1024]{1,0:T(8,128)(2,1)S(1)} %get-tuple-element.34), channel_id=1, source_target_pairs={{0,2},{1,3},{2,0},{3,1},{4,6},{5,7},{6,4},{7,5},{8,10},{9,11},{10,... | collective-permute-start | bytes 393224 | tf_op jit(solution)/shard_map/ppermute | solution.py:356

commit v3 on v2

v3 whole, which is shorter than its diff:
```python
import functools

import jax
import jax.numpy as jnp
from jax import lax
from jax.experimental import pallas as pl
from jax.experimental.pallas import tpu as pltpu
from jax.sharding import PartitionSpec as P

CHUNK = 128
GROUP = 4
NORM_EPS = 1e-06
F32 = jnp.float32
BF16 = jnp.bfloat16


def nn(a, b):
    return lax.dot_general(a, b, (((1,), (0,)), ((), ())), preferred_element_type=F32)


def nt(a, b):
    return lax.dot_general(a, b, (((1,), (1,)), ((), ())), preferred_element_type=F32)


def tn(a, b):
    return lax.dot_general(a, b, (((0,), (0,)), ((), ())), preferred_element_type=F32)


def halves(a):
    high = a.astype(BF16)
    return high, (a - high.astype(F32)).astype(BF16)


def fine_nn(a, b):
    left = jnp.concatenate(a, 1)
    right = jnp.concatenate(b, 1)
    both = nn(left, jnp.concatenate([right, right], 0))
    width = b[0].shape[1]
    return both[:, :width] + both[:, width:]


def fine_gram(a):
    left = jnp.concatenate(a, 1)
    both = nt(left, jnp.concatenate([jnp.concatenate([p, p], 1) for p in a], 0))
    width = a[0].shape[0]
    return both[:, :width] + both[:, width:]


def row_sum(a):
    return jnp.sum(a, axis=1, keepdims=True)


def core_kernel(
    order,
    *refs,
):
    inputs, refs = refs[: 2 * len(order)], refs[2 * len(order) :]
    (
        narrow_ref, narrow2_ref, wv_ref, log_ref, bias_ref,
        rows_ref, near_ref, away_ref, vsum_ref, mine_ref, theirs_ref,
        cot_ref, value_ref, kk_s, qk_s, q_s, k_s, b_s, e_s, tail_s, gam_s, p_s, t_s, w_s, u0_s, kt_s, x_s, qn_s, kn_s,
        f_s, g_s, h_s, ec_s, m_s, d_s,
    ) = refs
    place = lax.axis_index("head")
    core, chip = lax.rem(place, 2), place // 2
    part = inputs[0].shape[0]
    features, head = rows_ref.shape[1], cot_ref.shape[1]
    column = pl.ds(pl.multiple_of(features + core * head, head), head)
    for slot, far in enumerate(order):
        for other in range(2):
            who = 2 * (chip ^ far) + (core ^ other)
            span = pl.ds(pl.multiple_of(who * part, part), part)
            message = inputs[2 * slot + other]
            rows_ref[span, :] = message[:, :features]
            cot_ref[span, :] = message[:, column]
    total = cot_ref.shape[0]
    num = total // CHUNK
    group = min(GROUP, num)
    scale = head ** -0.5
    row_id = lax.broadcasted_iota(jnp.int32, (CHUNK, CHUNK), 0)
    col_id = lax.broadcasted_iota(jnp.int32, (CHUNK, CHUNK), 1)
    low = row_id >= col_id
    strict = row_id > col_id
    low_ones = jnp.where(low, 1.0, 0.0).astype(BF16)
    high_ones = jnp.where(row_id <= col_id, 1.0, 0.0).astype(BF16)
    below_ones = jnp.where(strict, 1.0, 0.0).astype(BF16)
    rate = -jnp.exp(log_ref[...])
    bias = bias_ref[...]

    def loop(body):
        if num == group:
            body(0)
        else:
            lax.fori_loop(0, num // group, lambda i, c: (body(i * group), c)[1], 0)

    def at(first, i):
        if isinstance(first, int):
            return pl.ds((first + i) * CHUNK, CHUNK)
        return pl.ds(pl.multiple_of((first + i) * CHUNK, CHUNK), CHUNK)

    half = head // 2
    own, partner = narrow_ref, narrow2_ref
    spread = lambda row: jnp.broadcast_to(own[pl.ds(head, 16), :][row : row + 1], (head, features))
    narrow = jnp.concatenate(
        [own[:half, :], partner[:half, :], own[half:head, :], partner[half:head, :], spread(0), spread(1)], 0)

    def rows_of(first):
        if isinstance(first, int):
            return pl.ds(first * CHUNK, group * CHUNK)
        return pl.ds(pl.multiple_of(first * CHUNK, CHUNK), group * CHUNK)

    each = range(group)
    cut = lambda a: [a[i * CHUNK : (i + 1) * CHUNK] for i in each]
    join = lambda parts: jnp.concatenate(parts, 0)

    def prepare(first):
        here = rows_of(first)
        spans = [at(first, i) for i in each]
        rows = rows_ref[here, :]
        pre = nt(rows, narrow)
        v = nn(rows, wv_ref[...])
        qp, kp = pre[:, :head], pre[:, head : 2 * head]
        qn = lax.rsqrt(row_sum(qp * qp) + NORM_EPS) * scale
        kn = lax.rsqrt(row_sum(kp * kp) + NORM_EPS)
        q = qp * qn
        k = kp * kn
        beta = 1.0 / (1.0 + jnp.exp(-pre[:, 2 * head : 3 * head]))
        x = pre[:, 3 * head :] + bias
        g = rate * (jnp.maximum(x, 0.0) + jnp.log1p(jnp.exp(-jnp.abs(x))))
        g1 = g.astype(BF16)
        g2, g3 = halves(g - g1.astype(F32))
        split = cut(jnp.concatenate([g1, g2, g3], 1))
        sums = [nn(low_ones, split[i]) for i in each]
        cs = [s[:, :head] + (s[:, head : 2 * head] + s[:, 2 * head :]) for s in sums]
        lasts = [c[CHUNK - 1 : CHUNK, :] for c in cs]
        e = jnp.exp(join(cs))
        tail = jnp.exp(join([last - c for last, c in zip(lasts, cs)]))
        gam = jnp.exp(join([jnp.where(low, c - c.T, -1e30) for c in cs]))
        kpair = halves(k)
        khigh, klow = cut(kpair[0]), cut(kpair[1])
        q16 = cut(q.astype(BF16))
        kk = join([fine_gram((khigh[i], klow[i])) for i in each])
        qk = join([nt(q16[i], khigh[i]) for i in each])
        strict_all, low_all = join([strict] * group), join([low] * group)
        mats = cut(jnp.where(strict_all, beta * gam * kk, 0.0))
        p_all = (gam * qk).astype(BF16)
        kt_all = (tail * k).astype(BF16)
        ek_bv = cut(jnp.concatenate([beta * e * k, beta * v], 1))
        p, kt, eq = cut(p_all), cut(kt_all), cut(e * q)
        for ref, value in (
            (kk_s, kk), (qk_s, qk), (q_s, q), (k_s, k), (b_s, beta), (e_s, e), (tail_s, tail), (gam_s, gam), (x_s, x),
            (p_s, p_all), (kt_s, kt_all),
            (qn_s, jnp.broadcast_to(qn, q.shape)), (kn_s, jnp.broadcast_to(kn, q.shape)),
        ):
            ref[here, :] = value
        for i in each:
            ec_s[first + i] = jnp.exp(jnp.broadcast_to(lasts[i], (8, head)))
        eye = jnp.where(row_id == col_id, 1.0, 0.0)
        inv = [eye - jnp.where((row_id >> 1) == (col_id >> 1), a, 0.0) for a in mats]
        pairs = [halves(a) for a in mats]
        level = 1
        while (2 << level) <= CHUNK:
            joint = ((row_id >> (level + 1)) == (col_id >> (level + 1))) & ((row_id >> level) > (col_id >> level))
            tp = [halves(t) for t in inv]
            left = [
                fine_nn(tp[i], tuple(jnp.where(joint, half, jnp.zeros_like(half)) for half in pairs[i]))
                for i in each
            ]
            lp = [halves(z) for z in left]
            inv = [inv[i] - fine_nn(lp[i], tp[i]) for i in each]
            level += 1
        tp = [halves(t) for t in inv]
        ep = [halves(y) for y in ek_bv]
        wu = [
            nn(jnp.concatenate(tp[i], 1), jnp.concatenate([ep[i][0], ep[i][0]], 0)) + nn(tp[i][0], ep[i][1])
            for i in each
        ]
        w = [y[:, :head].astype(BF16) for y in wu]
        fg = [tn(kt[i], jnp.concatenate([w[i], wu[i][:, head:].astype(BF16)], 1)) for i in each]
        pw = [nn(p[i], w[i]) for i in each]
        hs = [tn((eq[i] - pw[i]).astype(BF16), cot_ref[spans[i], :]) for i in each]
        t_s[here, :] = join([t[0] for t in tp])
        w_s[here, :] = join(w)
        u0_s[here, :] = join([y[:, head:] for y in wu])
        f_s[here, :] = join([y[:, :head].astype(BF16) for y in fg])
        g_s[here, :] = join([y[:, head:] for y in fg])
        h_s[here, :] = join(hs)

    loop(prepare)

    m_s[pl.ds(0, head), :] = jnp.zeros((head, head), F32)
    d_s[pl.ds((num - 1) * head, head), :] = jnp.zeros((head, head), F32)
    m = jnp.zeros((head, head), F32)
    d = jnp.zeros((head, head), F32)
    for i in range(num):
        span = pl.ds(i * CHUNK, CHUNK)
        if i == 0:
            m = g_s[span, :]
        else:
            m = ec_s[i][:1] * m - nn(f_s[span, :], m.astype(BF16)) + g_s[span, :]
        m_s[pl.ds((i + 1) * head, head), :] = m
        r = num - 1 - i
        if r > 0:
            back = pl.ds(r * CHUNK, CHUNK)
            if r == num - 1:
                d = h_s[back, :]
            else:
                d = ec_s[r][:1] * d - tn(f_s[back, :], d.astype(BF16)) + h_s[back, :]
            d_s[pl.ds((r - 1) * head, head), :] = d

    def finish(first):
        here = rows_of(first)
        q, k, beta = q_s[here, :], k_s[here, :], b_s[here, :]
        gam, e, tail = gam_s[here, :], e_s[here, :], tail_s[here, :]
        do = cot_ref[here, :]
        m32, d32 = m_s[here, :], d_s[here, :]
        m, d = cut(m32.astype(BF16)), cut(d32.astype(BF16))
        q16, k16 = q.astype(BF16), k.astype(BF16)
        k_parts, qk_parts = cut(k16), [join([a, b]) for a, b in zip(cut(q16), cut(-k16))]
        p, kt, t, w, dos = cut(p_s[here, :]), cut(kt_s[here, :]), cut(t_s[here, :]), cut(w_s[here, :]), cut(do)
        strict_all = join([strict] * group)
        du = [tn(p[i], dos[i]) + nn(kt[i], d[i]) for i in each]
        u = u0_s[here, :] - join([nn(w[i], m[i]) for i in each])
        u16 = cut(u.astype(BF16))
        dr = join([tn(t[i], du[i].astype(BF16)) for i in each])
        dv = beta * dr
        dv16 = dv.astype(BF16)
        dvs = cut(dv16)
        wide = [nt(join([dos[i], dvs[i]]), join([u16[i], m[i]])) for i in each]
        ud = join([nt(u16[i], d[i]) for i in each])
        y32 = join([a[:CHUNK, :CHUNK] for a in wide]) * gam
        x32 = jnp.where(strict_all, join([a[CHUNK:, :CHUNK] for a in wide]) * gam, 0.0)
        yx = [join([a, b]) for a, b in zip(cut(y32.astype(BF16)), cut(x32.astype(BF16)))]
        by_k = [nn(yx[i], k_parts[i]) for i in each]
        by_qk = join([tn(yx[i], qk_parts[i]) for i in each])
        from_q = e * join([a[:CHUNK, CHUNK:] for a in wide])
        from_k = e * join([a[CHUNK:, CHUNK:] for a in wide])
        to_k = tail * ud
        dq = from_q + join([a[:CHUNK] for a in by_k])
        dk = to_k - from_k - join([a[CHUNK:] for a in by_k]) + by_qk
        zc = halves(jnp.where(strict_all, y32 * qk_s[here, :], 0.0) - x32 * kk_s[here, :])
        zr = halves(q * from_q - k * from_k)
        zt = cut(jnp.concatenate(halves(k * to_k), 1))
        zs = cut(jnp.concatenate([*zc, *zr], 1))
        up = join([nn(high_ones, zs[i]) for i in each])
        down = join([nn(below_ones, zt[i]) for i in each])
        crossing = jnp.where(strict_all, up[:, :head] + up[:, head : 2 * head], 0.0)
        single = up[:, 2 * head : 3 * head] + up[:, 3 * head :] + down[:, :head] + down[:, head:]
        carried = join([
            jnp.broadcast_to(row_sum(jnp.sum(ec_s[first + i][:1] * a, axis=0, keepdims=True)), (CHUNK, 1))
            for i, a in enumerate(cut(m32 * d32))
        ])
        dg = row_sum(crossing + single) + carried
        ga = (dg * rate) * (1.0 / (1.0 + jnp.exp(-x_s[here, :])))
        gb = row_sum(dr * u) * (1.0 - beta)
        gq = (qn_s[here, :] * (dq - q * (row_sum(q * dq) * head))).astype(BF16)
        gk = (kn_s[here, :] * (dk - k * row_sum(k * dk))).astype(BF16)
        lane = lax.broadcasted_iota(jnp.int32, q.shape, 1)
        gba = jnp.where(lane == 0, gb, jnp.where(lane == 1, ga, 0.0)).astype(BF16)
        near_ref[here, :] = jnp.concatenate([gq[:, :half], gk[:, :half]], 1)
        away_ref[here, :] = jnp.concatenate([gq[:, half:], gk[:, half:]], 1)
        value_ref[here, :] = dv16
        forth = jnp.concatenate([gq, gk, dv16, gba], 1)
        swapped = jnp.concatenate([gq[:, half:], gq[:, :half], gk[:, half:], gk[:, :half], dv16, gba], 1)
        first_core = core == 0
        pieces = group * CHUNK // (2 * part)
        for j in range(pieces):
            lo = slice(2 * j * part, (2 * j + 1) * part)
            hi = slice((2 * j + 1) * part, (2 * j + 2) * part)
            slot = first * CHUNK // (2 * part) + j
            to = pl.ds(slot * part if isinstance(slot, int) else pl.multiple_of(slot * part, part), part)
            mine_ref[to, :] = jnp.where(first_core, forth[lo], forth[hi])
            theirs_ref[to, :] = jnp.where(first_core, swapped[hi], swapped[lo])

    loop(finish)
    vsum_ref[...] = tn(value_ref[...], rows_ref[...]).astype(BF16)


def core_grads(order, messages, narrow, narrow2, wv, log_rate, rate_bias):
    part, features = messages[0].shape[0], wv.shape[0]
    head = wv.shape[1]
    total = part * len(messages)
    num = total // CHUNK
    col = lambda dt: pltpu.VMEM((total, head), dt)
    states = pltpu.VMEM(((num + 1) * head, head), F32)
    out = lambda rows, cols: jax.ShapeDtypeStruct((rows, cols), BF16)
    args = (*messages, narrow, narrow2, wv, log_rate, rate_bias)
    return pl.pallas_call(
        functools.partial(core_kernel, order),
        out_shape=(
            out(total, features), out(total, head), out(total, head), out(head, features),
            out(total // 2, 4 * head), out(total // 2, 4 * head),
        ),
        in_specs=[pl.BlockSpec(memory_space=pltpu.VMEM)] * len(args),
        out_specs=[pl.BlockSpec(memory_space=pltpu.VMEM)] * 6,
        scratch_shapes=[
            col(BF16), col(BF16), col(F32), col(F32),
            col(F32), col(F32), col(F32), col(F32), col(F32), col(F32), col(BF16), col(BF16), col(BF16), col(F32),
            col(BF16), col(F32), col(F32), col(F32),
            col(BF16), col(F32), col(F32), pltpu.VMEM((num, 8, head), F32), states, states,
        ],
        compiler_params=pltpu.CompilerParams(vmem_limit_bytes=48 * 1024 * 1024),
        name="core_grads",
    )(*args)


def pack_kernel(chips, hidden_ref, cot_ref, *outs):
    chip = lax.axis_index("head") // 2
    width, features = cot_ref.shape[1] // chips, hidden_ref.shape[1]
    for far, out in enumerate(outs):
        out[:, :features] = hidden_ref[...]
        out[:, features:] = cot_ref[:, pl.ds(pl.multiple_of((chip ^ far) * width, width), width)]


def narrow_kernel(wq_ref, wk_ref, wb_ref, wa_ref, after_ref, out_ref):
    half, features = wq_ref.shape
    out_ref[pl.ds(0, half), :] = wq_ref[...]
    out_ref[pl.ds(half, half), :] = wk_ref[...]
    line = lax.broadcasted_iota(jnp.int32, (16, features), 0)
    beta, decay = wb_ref[...].astype(F32), wa_ref[...].astype(F32)
    out_ref[pl.ds(2 * half, 16), :] = jnp.where(line == 0, beta, jnp.where(line == 1, decay, 0.0)).astype(BF16)


def gram_kernel(rows_ref, near_ref, away_ref, out_ref):
    rows = rows_ref[...]
    out_ref[...] = (tn(near_ref[...], rows) + tn(away_ref[...], rows)).astype(BF16)


def term_kernel(part, mine_ref, recv_ref, own, partner, wv_ref, wv2_ref, *outs):
    chip = lax.axis_index("head") // 2
    head = wv_ref.shape[1]
    half = head // 2
    narrow = jnp.concatenate([own[:half, :], partner[:half, :], own[half:head, :], partner[half:head, :]], 0)
    small, small2 = own[pl.ds(head, 16), :], partner[pl.ds(head, 16), :]
    for far, out in enumerate(outs):
        to = pl.ds(pl.multiple_of((chip ^ far) * part, part), part)
        mine, recv = mine_ref[to, :], recv_ref[to, :]
        both = nn(jnp.concatenate([mine[:, : 2 * head], recv[:, : 2 * head]], 1), jnp.concatenate([narrow, narrow], 0))
        both = both + nt(mine[:, 2 * head : 3 * head], wv_ref[...]) + nt(recv[:, 2 * head : 3 * head], wv2_ref[...])
        both = both + nn(mine[:, 3 * head : 3 * head + 16], small) + nn(recv[:, 3 * head : 3 * head + 16], small2)
        out[...] = both.astype(BF16)


def sum_kernel(*refs):
    total = refs[0][...].astype(F32)
    for ref in refs[1:-1]:
        total = total + ref[...].astype(F32)
    refs[-1][...] = total.astype(BF16)


def mean_kernel(count, own_qk, recv_qk, own_v, recv_v, q_ref, k_ref, v_ref):
    half = q_ref.shape[0]
    qk = (own_qk[...].astype(F32) + recv_qk[...].astype(F32)) * (1.0 / count)
    q_ref[...] = qk[:half]
    k_ref[...] = qk[half:]
    v_ref[...] = ((own_v[...].astype(F32) + recv_v[...].astype(F32)) * (1.0 / count)).T


def add_kernel(own_ref, recv_ref, after_ref, out_ref):
    out_ref[...] = (own_ref[...].astype(F32) + recv_ref[...].astype(F32)).astype(BF16)


def local_call(body, outs, args, name, flops):
    many = isinstance(outs, tuple)
    spec = pl.BlockSpec(memory_space=pltpu.VMEM)
    return pl.pallas_call(
        body,
        out_shape=outs,
        in_specs=[spec] * len(args),
        out_specs=[spec] * len(outs) if many else spec,
        compiler_params=pltpu.CompilerParams(vmem_limit_bytes=48 * 1024 * 1024),
        cost_estimate=pl.CostEstimate(flops=flops, bytes_accessed=1 << 20, transcendentals=0),
        name=name,
    )(*args)


def across(block, distance):
    count = lax.axis_size("head")
    return lax.ppermute(block, "head", [(i, i ^ distance) for i in range(count)])


def across_data(block, step):
    groups, places = lax.axis_size("dp"), lax.axis_size("head")
    bits = groups.bit_length() - 1
    route = []
    for g in range(groups):
        for p in range(places):
            bit = step if p % 2 == 0 else bits - 1 - step
            route.append((g * places + p, (g ^ (1 << bit)) * places + p))
    return lax.ppermute(block, ("dp", "head"), route)


def body(
    hidden, core_grad, query_weight, key_weight, value_weight, beta_weight, decay_weight, decay_log, decay_bias,
):
    half = query_weight.shape[1]
    head = value_weight.shape[1]
    chips = lax.axis_size("head") // 2
    part, features = hidden.shape[1:]
    order = sorted(range(chips), key=lambda d: -d)
    block = lambda rows, dt: jax.ShapeDtypeStruct((rows, features), dt)
    message = jax.ShapeDtypeStruct((part, features + 2 * head), BF16)
    sent = local_call(
        functools.partial(pack_kernel, chips), (message,) * chips, (hidden[0], core_grad[0]), "pack", 1048576)
    got = {d: across(sent[d], 2 * d) if d else sent[0] for d in order}
    narrow = local_call(
        narrow_kernel, block(head + 16, BF16),
        (query_weight.T, key_weight.T, beta_weight.T, decay_weight.T, got[order[0]]), "narrow", 1048576)
    wv = value_weight
    messages = []
    for d in order:
        messages += [got[d], across(got[d], 1)]
    narrow2, wv2 = across(narrow, 1), across(wv, 1)

    all_rows, near, away, value, mine, theirs = core_grads(
        order, messages, narrow, narrow2, wv, decay_log.reshape(1, 1), decay_bias.reshape(1, 1))
    recv = across(away, 1)
    other = across(theirs, 1)
    qk = local_call(gram_kernel, block(head, BF16), (all_rows, near, recv), "gram", 268435456)
    terms = local_call(
        functools.partial(term_kernel, part), (block(part, BF16),) * chips,
        (mine, other, narrow, narrow2, wv, wv2), "terms", 1073741824,
    )
    received = [across(terms[d], 2 * d) for d in order if d]
    groups = lax.axis_size("dp")
    rounds = groups.bit_length() - 1
    sums = {"value": value, "qk": qk}
    for step in range(rounds - 1):
        for name in sums:
            own = sums[name]
            sums[name] = local_call(add_kernel, block(head, BF16), (own, across_data(own, step), terms[0]), "add", 1048576)
    last = {name: across_data(sums[name], rounds - 1) for name in sums}
    token = local_call(sum_kernel, block(part, BF16), (terms[0], *received), "token_sum", 17179869184)
    q_mean, k_mean, v_mean = local_call(
        functools.partial(mean_kernel, groups),
        (block(half, F32), block(half, F32), jax.ShapeDtypeStruct((features, head), F32)),
        (sums["qk"], last["qk"], sums["value"], last["value"]), "weight_mean", 1048576,
    )
    return token[None], q_mean.T, k_mean.T, v_mean


def solution(mesh):
    rows = P("dp", "head", None)
    cols = P(None, "head")
    return jax.shard_map(
        body,
        mesh=mesh,
        in_specs=(rows, rows, cols, cols, cols, cols, cols, P("head"), P("head")),
        out_specs=(rows, cols, cols, cols),
        check_vma=False,
    )
```

time: 65.4 us -> 49.8 us (0.76)
  waiting for transfers between devices: 28.4 us -> 18.9 us
  Pallas kernels: 12.2 us -> 9.78 us
  local copies, waits for them, and re-layouts: 3.78 us -> 1.82 us
  starting transfers between devices: 18.5 us -> 17 us
    ppermute x4, waiting for transfers between devices: 6.3 us -> 0.01 us  [across_data(): return lax.ppermute(block, ('dp', 'head'), route)]
    ppermute x17 -> x14, waiting for transfers between devices: 22.1 us -> 18.9 us  [across(): lax.ppermute(block, 'head', [(i, i ^ distance) for i in range(count)])]
    pallas_call x1, Pallas kernels: 8.23 us -> 5.38 us  [core_grads(): pl.pallas_call(functools.partial(core_kernel, order), out_shape=(out(tota...]
    unnamed x14, local copies, waits for them, and re-layouts: 3.78 us -> 1.82 us
    ppermute x17 -> x14, starting transfers between devices: 12.9 us -> 12.1 us  [across(): lax.ppermute(block, 'head', [(i, i ^ distance) for i in range(count)])]
    ppermute x4, starting transfers between devices: 5.68 us -> 4.98 us  [across_data(): return lax.ppermute(block, ('dp', 'head'), route)]
    pallas_call x4 -> x8, Pallas kernels: 3.98 us -> 4.4 us  [local_call(): pl.pallas_call(body, out_shape=outs, in_specs=[spec] * len(args), out_spe...]
  transfers between devices with their start and end apart: 21 -> 18, of which waited for: 8 -> 4; matrix products, arithmetic and copies ran while one was open for 0% -> 0% of each run, Pallas kernels for 17% -> 17%
where the time goes in v3:
time: 49.8 us; the launch traced here: 49.6 us
  waiting for transfers between devices  18.9 us (38%)
  starting transfers between devices  17 us (34%)
  Pallas kernels  9.78 us (20%)
  between operations  2.08 us (4%)
  local copies, waits for them, and re-layouts  1.82 us (4%)
    ppermute x14, waiting for transfers between devices, across(): lax.ppermute(block, 'head', [(i, i ^ distance) for i in range(count)])  18.9 us
    ppermute x14, starting transfers between devices, across(): lax.ppermute(block, 'head', [(i, i ^ distance) for i in range(count)])  12.1 us
    pallas_call x1, Pallas kernels, core_grads(): pl.pallas_call(functools.partial(core_kernel, order), out_shape=(out(tota...  5.38 us
    ppermute x4, starting transfers between devices, across_data(): return lax.ppermute(block, ('dp', 'head'), route)  4.98 us
    pallas_call x8, Pallas kernels, local_call(): pl.pallas_call(body, out_shape=outs, in_specs=[spec] * len(args), out_spe...  4.4 us
    unnamed x14, local copies, waits for them, and re-layouts  1.82 us
  transfers between devices with their start and end apart: 18, of which 4 were waited for; matrix products, arithmetic and copies ran while one was open for 0% of the time, Pallas kernels for 17%

profile of v3, /device:TPU:0, one launch (start us, length us, event | category | flops | bytes accessed | tf_op | source)
XLA Modules:
  0.0 49.6 jit_solution(9415624750519718320)
XLA Ops:
  0.6 0.9 %copy-done.1 = bf16[1,64,1024]{2,1,0:T(8,128)(2,1)S(1)} copy-done((bf16[1,64,1024]{2,1,0:T(8,128)(2,1)S(1)}, bf16[1,64,1024]{2,1,0:T(8,128)(2,1)}, u32[]{:S(2)}) %copy-start.1) | copy-done | bytes 131096
  1.5 0.9 %copy-done.2 = bf16[1,64,1024]{2,1,0:T(8,128)(2,1)S(1)} copy-done((bf16[1,64,1024]{2,1,0:T(8,128)(2,1)S(1)}, bf16[1,64,1024]{2,1,0:T(8,128)(2,1)}, u32[]{:S(2)}) %copy-start.2) | copy-done | bytes 131096
  2.5 5.1 %collective-permute-start = (bf16[64,1280]{1,0:T(8,128)(2,1)S(1)}, bf16[64,1280]{1,0:T(8,128)(2,1)S(1)}, u32[]{:S(2)}, u32[]{:S(2)}) collective-permute-start(bf16[64,1280]{1,0:T(8,128)(2,1)S(1)} %get-tuple-element.21), channel_id=1, source_target_pairs={{0,6},{1,7},{2,4},{3,5},{4,2},{5,3},{6,0},{7,1},{8,14},{9,15},{10,... | collective-permute-start | bytes 491528 | tf_op jit(solution)/shard_map/ppermute | solution.py:379
  7.6 0.0 collective-permute-start.2
  7.6 0.6 %collective-permute-start.4 = (bf16[64,1280]{1,0:T(8,128)(2,1)S(1)}, bf16[64,1280]{1,0:T(8,128)(2,1)S(1)}, u32[]{:S(2)}, u32[]{:S(2)}) collective-permute-start(bf16[64,1280]{1,0:T(8,128)(2,1)S(1)} %get-tuple-element.23), channel_id=1, source_target_pairs={{0,2},{1,3},{2,0},{3,1},{4,6},{5,7},{6,4},{7,5},{8,10},{9,11},{10,... | collective-permute-start | bytes 491528 | tf_op jit(solution)/shard_map/ppermute | solution.py:379
  8.3 4.5 %collective-permute-done.after_ref.refs_0_ = bf16[64,1280]{1,0:T(8,128)(2,1)S(1)} collective-permute-done((bf16[64,1280]{1,0:T(8,128)(2,1)S(1)}, bf16[64,1280]{1,0:T(8,128)(2,1)S(1)}, u32[]{:S(2)}, u32[]{:S(2)}) %collective-permute-start) | collective-permute-done | bytes 163872 | tf_op jit(solution)/shard_map/ppermute | solution.py:379
  12.8 0.0 copy-start
  12.8 0.1 collective-permute-start.7
  12.9 0.5 %collective-permute-start.6 = (bf16[64,1280]{1,0:T(8,128)(2,1)S(1)}, bf16[64,1280]{1,0:T(8,128)(2,1)S(1)}, u32[]{:S(2)}, u32[]{:S(2)}) collective-permute-start(bf16[64,1280]{1,0:T(8,128)(2,1)S(1)} %get-tuple-element.24.refs_6_), channel_id=1, source_target_pairs={{0,1},{1,0},{2,3},{3,2},{4,5},{5,4},{6,7},{7,6},{8,9},{9,8},{10,11... | collective-permute-start | bytes 491528 | tf_op jit(solution)/shard_map/ppermute | solution.py:379
  13.4 0.1 collective-permute-start.1
  13.5 8.0 %collective-permute-done.2.refs_2_ = bf16[64,1280]{1,0:T(8,128)(2,1)S(1)} collective-permute-done((bf16[64,1280]{1,0:T(8,128)(2,1)S(1)}, bf16[64,1280]{1,0:T(8,128)(2,1)S(1)}, u32[]{:S(2)}, u32[]{:S(2)}) %collective-permute-start.2) | collective-permute-done | bytes 163872 | tf_op jit(solution)/shard_map/ppermute | solution.py:379
  21.5 0.0 collective-permute-start.3
  21.5 0.0 collective-permute-done.4.refs_4_
  21.5 0.5 %collective-permute-start.5 = (bf16[64,1280]{1,0:T(8,128)(2,1)S(1)}, bf16[64,1280]{1,0:T(8,128)(2,1)S(1)}, u32[]{:S(2)}, u32[]{:S(2)}) collective-permute-start(bf16[64,1280]{1,0:T(8,128)(2,1)S(1)} %collective-permute-done.4.refs_4_), channel_id=1, source_target_pairs={{0,1},{1,0},{2,3},{3,2},{4,5},{5,4},{6,7},{7,6},{8,9},{9,8},{10,11... | collective-permute-start | bytes 491528 | tf_op jit(solution)/shard_map/ppermute | solution.py:379
  23.3 0.1 collective-permute-start.9
  23.4 5.4 %core_grads.1 = (bf16[512,1024]{1,0:T(8,128)(2,1)S(1)}, bf16[512,128]{1,0:T(8,128)(2,1)S(1)}, bf16[512,128]{1,0:T(8,128)(2,1)S(1)}, bf16[128,1024]{1,0:T(8,128)(...) custom-call(bf16[64,1280]{1,0:T(8,128)(2,1)S(1)} %collective-permute-done.after_ref.refs_0_, ...), custom_call_target="tpu_custom_call" | custom-call | tf_op jit(solution)/shard_map/core_grads/pallas_call | solution.py:288
  28.8 0.5 %collective-permute-start.8 = (bf16[256,512]{1,0:T(8,128)(2,1)S(1)}, bf16[256,512]{1,0:T(8,128)(2,1)S(1)}, u32[]{:S(2)}, u32[]{:S(2)}) collective-permute-start(bf16[256,512]{1,0:T(8,128)(2,1)S(1)} %get-tuple-element.26), channel_id=1, source_target_pairs={{0,1},{1,0},{2,3},{3,2},{4,5},{5,4},{6,7},{7,6},{8,9},{9,8},{10,11... | collective-permute-start | bytes 786440 | tf_op jit(solution)/shard_map/ppermute | solution.py:379
  29.4 0.1 collective-permute-start.13
  29.5 1.5 %collective-permute-start.16 = (bf16[128,1024]{1,0:T(8,128)(2,1)S(1)}, bf16[128,1024]{1,0:T(8,128)(2,1)S(1)}, u32[]{:S(2)}, u32[]{:S(2)}) collective-permute-start(bf16[128,1024]{1,0:T(8,128)(2,1)S(1)} %get-tuple-element.34.own_ref), channel_id=1, source_target_pairs={{0,8},{1,17},{2,10},{3,19},{4,12},{5,21},{6,14},{7,23},{8,0},{9,25... | collective-permute-start | bytes 786440 | tf_op jit(solution)/shard_map/ppermute | solution.py:390
  30.9 0.5 gram.1.own_ref
  31.4 1.3 %collective-permute-start.14 = (bf16[128,1024]{1,0:T(8,128)(2,1)S(1)}, bf16[128,1024]{1,0:T(8,128)(2,1)S(1)}, u32[]{:S(2)}, u32[]{:S(2)}) collective-permute-start(bf16[128,1024]{1,0:T(8,128)(2,1)S(1)} %gram.1.own_ref), channel_id=1, source_target_pairs={{0,8},{1,17},{2,10},{3,19},{4,12},{5,21},{6,14},{7,23},{8,0},{9,25... | collective-permute-start | bytes 786440 | tf_op jit(solution)/shard_map/ppermute | solution.py:390
  32.8 1.9 %terms.1 = (bf16[64,1024]{1,0:T(8,128)(2,1)S(1)}, bf16[64,1024]{1,0:T(8,128)(2,1)S(1)}, bf16[64,1024]{1,0:T(8,128)(2,1)S(1)}, bf16[64,1024]{1,0:T(8,128)(2,1)S(1)}) custom-call(bf16[256,512]{1,0:T(8,128)(2,1)S(1)} %get-tuple-element.25.mine_ref, bf16[256,512]{1,0:T(8,128)(2,1)S(1)} %collective-permute-done.8.recv_ref, ...), custom_call_target="tpu_custom_call" | custom-call | flops 1073741824 | bytes 1048576 | tf_op jit(solution)/shard_map/terms/pallas_call | solution.py:366
  34.6 2.5 %collective-permute-start.10 = (bf16[64,1024]{1,0:T(8,128)(2,1)S(1)}, bf16[64,1024]{1,0:T(8,128)(2,1)S(1)}, u32[]{:S(2)}, u32[]{:S(2)}) collective-permute-start(bf16[64,1024]{1,0:T(8,128)(2,1)S(1)} %get-tuple-element.28), channel_id=1, source_target_pairs={{0,6},{1,7},{2,4},{3,5},{4,2},{5,3},{6,0},{7,1},{8,14},{9,15},{10,... | collective-permute-start | bytes 393224 | tf_op jit(solution)/shard_map/ppermute | solution.py:379
  37.2 1.9 %collective-permute-start.12 = (bf16[64,1024]{1,0:T(8,128)(2,1)S(1)}, bf16[64,1024]{1,0:T(8,128)(2,1)S(1)}, u32[]{:S(2)}, u32[]{:S(2)}) collective-permute-start(bf16[64,1024]{1,0:T(8,128)(2,1)S(1)} %get-tuple-element.30), channel_id=1, source_target_pairs={{0,2},{1,3},{2,0},{3,1},{4,6},{5,7},{6,4},{7,5},{8,10},{9,11},{10,... | collective-permute-start | bytes 393224 | tf_op jit(solution)/shard_map/ppermute | solution.py:379
  39.1 0.1 add.3.own_v
  39.1 1.6 %collective-permute-start.17 = (bf16[128,1024]{1,0:T(8,128)(2,1)S(1)}, bf16[128,1024]{1,0:T(8,128)(2,1)S(1)}, u32[]{:S(2)}, u32[]{:S(2)}) collective-permute-start(bf16[128,1024]{1,0:T(8,128)(2,1)S(1)} %add.3.own_v), channel_id=1, source_target_pairs={{0,16},{1,9},{2,18},{3,11},{4,20},{5,13},{6,22},{7,15},{8,24},{9,1... | collective-permute-start | bytes 786440 | tf_op jit(solution)/shard_map/ppermute | solution.py:390
  40.7 0.1 add.2.own_qk
  40.8 0.6 %collective-permute-start.15 = (bf16[128,1024]{1,0:T(8,128)(2,1)S(1)}, bf16[128,1024]{1,0:T(8,128)(2,1)S(1)}, u32[]{:S(2)}, u32[]{:S(2)}) collective-permute-start(bf16[128,1024]{1,0:T(8,128)(2,1)S(1)} %add.2.own_qk), channel_id=1, source_target_pairs={{0,16},{1,9},{2,18},{3,11},{4,20},{5,13},{6,22},{7,15},{8,24},{9,1... | collective-permute-start | bytes 786440 | tf_op jit(solution)/shard_map/ppermute | solution.py:390
  41.4 1.6 %collective-permute-done.10.refs_1_ = bf16[64,1024]{1,0:T(8,128)(2,1)S(1)} collective-permute-done((bf16[64,1024]{1,0:T(8,128)(2,1)S(1)}, bf16[64,1024]{1,0:T(8,128)(2,1)S(1)}, u32[]{:S(2)}, u32[]{:S(2)}) %collective-permute-start.10) | collective-permute-done | bytes 131104 | tf_op jit(solution)/shard_map/ppermute | solution.py:379
  43.0 4.8 %collective-permute-done.11.refs_2_ = bf16[64,1024]{1,0:T(8,128)(2,1)S(1)} collective-permute-done((bf16[64,1024]{1,0:T(8,128)(2,1)S(1)}, bf16[64,1024]{1,0:T(8,128)(2,1)S(1)}, u32[]{:S(2)}, u32[]{:S(2)}) %collective-permute-start.11) | collective-permute-done | bytes 131104 | tf_op jit(solution)/shard_map/ppermute | solution.py:379
  47.8 0.7 %token_sum.1 = bf16[64,1024]{1,0:T(8,128)(2,1)} custom-call(bf16[64,1024]{1,0:T(8,128)(2,1)S(1)} %get-tuple-element.27.refs_0_.after_ref, bf16[64,1024]{1,0:T(8,128)(2,1)S(1)} %collective-permute-done.10.refs_1_, bf16[64,1024]{1,0:T(8,128)(2,1)S(1)} %collective-permute-done.11.refs_2_, bf16[64,1024]{1,0:T(8,128)(2,1)S(1)} %collective-permute-done.12.refs_3_), custom_call_target="tpu_custom_call" | custom-call | flops 17179869184 | bytes 1048576 | tf_op jit(solution)/shard_map/token_sum/pallas_call | solution.py:366
  48.5 1.2 %weight_mean.1 = (f32[64,1024]{1,0:T(8,128)}, f32[64,1024]{1,0:T(8,128)}, f32[1024,128]{1,0:T(8,128)}) custom-call(bf16[128,1024]{1,0:T(8,128)(2,1)S(1)} %add.2.own_qk, bf16[128,1024]{1,0:T(8,128)(2,1)S(1)} %collective-permute-done.15.recv_qk, bf16[128,1024]{1,0:T(8,128)(2,1)S(1)} %add.3.own_v, bf16[128,1024]{1,0:T(8,128)(2,1)S(1)} %collective-permute-done.17.recv_v), custom_call_target="tpu_custom_call" | custom-call | flops 1048576 | bytes 1048576 | tf_op jit(solution)/shard_map/weight_mean/pallas_call | solution.py:366
  (27 shorter events, 0.1 us)
Async XLA Ops:
  0.6 0.9 %copy-start.1 = (bf16[1,64,1024]{2,1,0:T(8,128)(2,1)S(1)}, bf16[1,64,1024]{2,1,0:T(8,128)(2,1)}, u32[]{:S(2)}) copy-start(bf16[1,64,1024]{2,1,0:T(8,128)(2,1)} %param.9) | copy-start | bytes 393220
  1.5 0.9 %copy-start.2 = (bf16[1,64,1024]{2,1,0:T(8,128)(2,1)S(1)}, bf16[1,64,1024]{2,1,0:T(8,128)(2,1)}, u32[]{:S(2)}) copy-start(bf16[1,64,1024]{2,1,0:T(8,128)(2,1)} %param.10) | copy-start | bytes 393220
  2.4 10.3 %copy-start.3 = (bf16[1024,64]{0,1:T(8,128)(2,1)S(1)}, bf16[1024,64]{0,1:T(8,128)(2,1)}, u32[]{:S(2)}) copy-start(bf16[1024,64]{0,1:T(8,128)(2,1)} %param.11) | copy-start | bytes 393220
  2.4 10.3 %copy-start.4 = (bf16[1024,64]{0,1:T(8,128)(2,1)S(1)}, bf16[1024,64]{0,1:T(8,128)(2,1)}, u32[]{:S(2)}) copy-start(bf16[1024,64]{0,1:T(8,128)(2,1)} %param.12) | copy-start | bytes 393220
  2.5 10.2 %collective-permute-start = (bf16[64,1280]{1,0:T(8,128)(2,1)S(1)}, bf16[64,1280]{1,0:T(8,128)(2,1)S(1)}, u32[]{:S(2)}, u32[]{:S(2)}) collective-permute-start(bf16[64,1280]{1,0:T(8,128)(2,1)S(1)} %get-tuple-element.21), channel_id=1, source_target_pairs={{0,6},{1,7},{2,4},{3,5},{4,2},{5,3},{6,0},{7,1},{8,14},{9,15},{10,... | collective-permute-start | bytes 491528 | tf_op jit(solution)/shard_map/ppermute | solution.py:379
  7.6 13.9 %collective-permute-start.2 = (bf16[64,1280]{1,0:T(8,128)(2,1)S(1)}, bf16[64,1280]{1,0:T(8,128)(2,1)S(1)}, u32[]{:S(2)}, u32[]{:S(2)}) collective-permute-start(bf16[64,1280]{1,0:T(8,128)(2,1)S(1)} %get-tuple-element.22), channel_id=1, source_target_pairs={{0,4},{1,5},{2,6},{3,7},{4,0},{5,1},{6,2},{7,3},{8,12},{9,13},{10,... | collective-permute-start | bytes 491528 | tf_op jit(solution)/shard_map/ppermute | solution.py:379
  7.6 5.1 %copy-start.6 = (bf16[1024,1]{0,1:T(2,128)(2,1)S(1)}, bf16[1024,1]{0,1:T(2,128)(2,1)}, u32[]{:S(2)}) copy-start(bf16[1024,1]{0,1:T(2,128)(2,1)} %param.15) | copy-start | bytes 6148
  7.6 5.1 %copy-start.5 = (bf16[1024,1]{0,1:T(2,128)(2,1)S(1)}, bf16[1024,1]{0,1:T(2,128)(2,1)}, u32[]{:S(2)}) copy-start(bf16[1024,1]{0,1:T(2,128)(2,1)} %param.14) | copy-start | bytes 6148
  7.6 13.9 %collective-permute-start.4 = (bf16[64,1280]{1,0:T(8,128)(2,1)S(1)}, bf16[64,1280]{1,0:T(8,128)(2,1)S(1)}, u32[]{:S(2)}, u32[]{:S(2)}) collective-permute-start(bf16[64,1280]{1,0:T(8,128)(2,1)S(1)} %get-tuple-element.23), channel_id=1, source_target_pairs={{0,2},{1,3},{2,0},{3,1},{4,6},{5,7},{6,4},{7,5},{8,10},{9,11},{10,... | collective-permute-start | bytes 491528 | tf_op jit(solution)/shard_map/ppermute | solution.py:379
  12.8 10.6 %copy-start = (bf16[1024,128]{1,0:T(8,128)(2,1)S(1)}, bf16[1024,128]{1,0:T(8,128)(2,1)}, u32[]{:S(2)}) copy-start(bf16[1024,128]{1,0:T(8,128)(2,1)} %wv_ref.1) | copy-start | bytes 786436
  12.8 10.6 %collective-permute-start.7 = (bf16[144,1024]{1,0:T(8,128)(2,1)S(1)}, bf16[144,1024]{1,0:T(8,128)(2,1)S(1)}, u32[]{:S(2)}, u32[]{:S(2)}) collective-permute-start(bf16[144,1024]{1,0:T(8,128)(2,1)S(1)} %narrow.1.refs_8_.own), channel_id=1, source_target_pairs={{0,1},{1,0},{2,3},{3,2},{4,5},{5,4},{6,7},{7,6},{8,9},{9,8},{10,11... | collective-permute-start | bytes 884744 | tf_op jit(solution)/shard_map/ppermute | solution.py:379
  12.9 10.4 %collective-permute-start.6 = (bf16[64,1280]{1,0:T(8,128)(2,1)S(1)}, bf16[64,1280]{1,0:T(8,128)(2,1)S(1)}, u32[]{:S(2)}, u32[]{:S(2)}) collective-permute-start(bf16[64,1280]{1,0:T(8,128)(2,1)S(1)} %get-tuple-element.24.refs_6_), channel_id=1, source_target_pairs={{0,1},{1,0},{2,3},{3,2},{4,5},{5,4},{6,7},{7,6},{8,9},{9,8},{10,11... | collective-permute-start | bytes 491528 | tf_op jit(solution)/shard_map/ppermute | solution.py:379
  13.4 10.0 %collective-permute-start.1 = (bf16[64,1280]{1,0:T(8,128)(2,1)S(1)}, bf16[64,1280]{1,0:T(8,128)(2,1)S(1)}, u32[]{:S(2)}, u32[]{:S(2)}) collective-permute-start(bf16[64,1280]{1,0:T(8,128)(2,1)S(1)} %collective-permute-done.after_ref.refs_0_), channel_id=1, source_target_pairs={{0,1},{1,0},{2,3},{3,2},{4,5},{5,4},{6,7},{7,6},{8,9},{9,8},{10,11... | collective-permute-start | bytes 491528 | tf_op jit(solution)/shard_map/ppermute | solution.py:379
  21.5 1.9 %collective-permute-start.3 = (bf16[64,1280]{1,0:T(8,128)(2,1)S(1)}, bf16[64,1280]{1,0:T(8,128)(2,1)S(1)}, u32[]{:S(2)}, u32[]{:S(2)}) collective-permute-start(bf16[64,1280]{1,0:T(8,128)(2,1)S(1)} %collective-permute-done.2.refs_2_), channel_id=1, source_target_pairs={{0,1},{1,0},{2,3},{3,2},{4,5},{5,4},{6,7},{7,6},{8,9},{9,8},{10,11... | collective-permute-start | bytes 491528 | tf_op jit(solution)/shard_map/ppermute | solution.py:379
  21.5 1.9 %collective-permute-start.5 = (bf16[64,1280]{1,0:T(8,128)(2,1)S(1)}, bf16[64,1280]{1,0:T(8,128)(2,1)S(1)}, u32[]{:S(2)}, u32[]{:S(2)}) collective-permute-start(bf16[64,1280]{1,0:T(8,128)(2,1)S(1)} %collective-permute-done.4.refs_4_), channel_id=1, source_target_pairs={{0,1},{1,0},{2,3},{3,2},{4,5},{5,4},{6,7},{7,6},{8,9},{9,8},{10,11... | collective-permute-start | bytes 491528 | tf_op jit(solution)/shard_map/ppermute | solution.py:379
  23.3 9.4 %collective-permute-start.9 = (bf16[1024,128]{1,0:T(8,128)(2,1)S(1)}, bf16[1024,128]{1,0:T(8,128)(2,1)S(1)}, u32[]{:S(2)}, u32[]{:S(2)}) collective-permute-start(bf16[1024,128]{1,0:T(8,128)(2,1)S(1)} %copy-done), channel_id=1, source_target_pairs={{0,1},{1,0},{2,3},{3,2},{4,5},{5,4},{6,7},{7,6},{8,9},{9,8},{10,11... | collective-permute-start | bytes 786440 | tf_op jit(solution)/shard_map/ppermute | solution.py:379
  28.8 3.9 %collective-permute-start.8 = (bf16[256,512]{1,0:T(8,128)(2,1)S(1)}, bf16[256,512]{1,0:T(8,128)(2,1)S(1)}, u32[]{:S(2)}, u32[]{:S(2)}) collective-permute-start(bf16[256,512]{1,0:T(8,128)(2,1)S(1)} %get-tuple-element.26), channel_id=1, source_target_pairs={{0,1},{1,0},{2,3},{3,2},{4,5},{5,4},{6,7},{7,6},{8,9},{9,8},{10,11... | collective-permute-start | bytes 786440 | tf_op jit(solution)/shard_map/ppermute | solution.py:379
  29.4 1.6 %collective-permute-start.13 = (bf16[512,128]{1,0:T(8,128)(2,1)S(1)}, bf16[512,128]{1,0:T(8,128)(2,1)S(1)}, u32[]{:S(2)}, u32[]{:S(2)}) collective-permute-start(bf16[512,128]{1,0:T(8,128)(2,1)S(1)} %get-tuple-element.33), channel_id=1, source_target_pairs={{0,1},{1,0},{2,3},{3,2},{4,5},{5,4},{6,7},{7,6},{8,9},{9,8},{10,11... | collective-permute-start | bytes 393224 | tf_op jit(solution)/shard_map/ppermute | solution.py:379
  29.5 9.6 %collective-permute-start.16 = (bf16[128,1024]{1,0:T(8,128)(2,1)S(1)}, bf16[128,1024]{1,0:T(8,128)(2,1)S(1)}, u32[]{:S(2)}, u32[]{:S(2)}) collective-permute-start(bf16[128,1024]{1,0:T(8,128)(2,1)S(1)} %get-tuple-element.34.own_ref), channel_id=1, source_target_pairs={{0,8},{1,17},{2,10},{3,19},{4,12},{5,21},{6,14},{7,23},{8,0},{9,25... | collective-permute-start | bytes 786440 | tf_op jit(solution)/shard_map/ppermute | solution.py:390
  31.4 9.3 %collective-permute-start.14 = (bf16[128,1024]{1,0:T(8,128)(2,1)S(1)}, bf16[128,1024]{1,0:T(8,128)(2,1)S(1)}, u32[]{:S(2)}, u32[]{:S(2)}) collective-permute-start(bf16[128,1024]{1,0:T(8,128)(2,1)S(1)} %gram.1.own_ref), channel_id=1, source_target_pairs={{0,8},{1,17},{2,10},{3,19},{4,12},{5,21},{6,14},{7,23},{8,0},{9,25... | collective-permute-start | bytes 786440 | tf_op jit(solution)/shard_map/ppermute | solution.py:390
  34.6 8.3 %collective-permute-start.10 = (bf16[64,1024]{1,0:T(8,128)(2,1)S(1)}, bf16[64,1024]{1,0:T(8,128)(2,1)S(1)}, u32[]{:S(2)}, u32[]{:S(2)}) collective-permute-start(bf16[64,1024]{1,0:T(8,128)(2,1)S(1)} %get-tuple-element.28), channel_id=1, source_target_pairs={{0,6},{1,7},{2,4},{3,5},{4,2},{5,3},{6,0},{7,1},{8,14},{9,15},{10,... | collective-permute-start | bytes 393224 | tf_op jit(solution)/shard_map/ppermute | solution.py:379
  37.2 10.6 %collective-permute-start.11 = (bf16[64,1024]{1,0:T(8,128)(2,1)S(1)}, bf16[64,1024]{1,0:T(8,128)(2,1)S(1)}, u32[]{:S(2)}, u32[]{:S(2)}) collective-permute-start(bf16[64,1024]{1,0:T(8,128)(2,1)S(1)} %get-tuple-element.29), channel_id=1, source_target_pairs={{0,4},{1,5},{2,6},{3,7},{4,0},{5,1},{6,2},{7,3},{8,12},{9,13},{10,... | collective-permute-start | bytes 393224 | tf_op jit(solution)/shard_map/ppermute | solution.py:379
  37.2 10.6 %collective-permute-start.12 = (bf16[64,1024]{1,0:T(8,128)(2,1)S(1)}, bf16[64,1024]{1,0:T(8,128)(2,1)S(1)}, u32[]{:S(2)}, u32[]{:S(2)}) collective-permute-start(bf16[64,1024]{1,0:T(8,128)(2,1)S(1)} %get-tuple-element.30), channel_id=1, source_target_pairs={{0,2},{1,3},{2,0},{3,1},{4,6},{5,7},{6,4},{7,5},{8,10},{9,11},{10,... | collective-permute-start | bytes 393224 | tf_op jit(solution)/shard_map/ppermute | solution.py:379
  39.1 9.3 %collective-permute-start.17 = (bf16[128,1024]{1,0:T(8,128)(2,1)S(1)}, bf16[128,1024]{1,0:T(8,128)(2,1)S(1)}, u32[]{:S(2)}, u32[]{:S(2)}) collective-permute-start(bf16[128,1024]{1,0:T(8,128)(2,1)S(1)} %add.3.own_v), channel_id=1, source_target_pairs={{0,16},{1,9},{2,18},{3,11},{4,20},{5,13},{6,22},{7,15},{8,24},{9,1... | collective-permute-start | bytes 786440 | tf_op jit(solution)/shard_map/ppermute | solution.py:390
  40.8 7.7 %collective-permute-start.15 = (bf16[128,1024]{1,0:T(8,128)(2,1)S(1)}, bf16[128,1024]{1,0:T(8,128)(2,1)S(1)}, u32[]{:S(2)}, u32[]{:S(2)}) collective-permute-start(bf16[128,1024]{1,0:T(8,128)(2,1)S(1)} %add.2.own_qk), channel_id=1, source_target_pairs={{0,16},{1,9},{2,18},{3,11},{4,20},{5,13},{6,22},{7,15},{8,24},{9,1... | collective-permute-start | bytes 786440 | tf_op jit(solution)/shard_map/ppermute | solution.py:390

commit v4 on v3

--- a/solution.py
+++ b/solution.py
@@ -327,23 +327,26 @@
 
 
 def term_kernel(part, mine_ref, recv_ref, own, partner, wv_ref, wv2_ref, *outs):
+    outs, all_ref = outs[:-1], outs[-1]
     chip = lax.axis_index("head") // 2
     head = wv_ref.shape[1]
     half = head // 2
     narrow = jnp.concatenate([own[:half, :], partner[:half, :], own[half:head, :], partner[half:head, :]], 0)
     small, small2 = own[pl.ds(head, 16), :], partner[pl.ds(head, 16), :]
+    mine, recv = mine_ref[...], recv_ref[...]
+    both = nn(jnp.concatenate([mine[:, : 2 * head], recv[:, : 2 * head]], 1), jnp.concatenate([narrow, narrow], 0))
+    both = both + nt(
+        jnp.concatenate([mine[:, 2 * head : 3 * head], recv[:, 2 * head : 3 * head]], 1),
+        jnp.concatenate([wv_ref[...], wv2_ref[...]], 1))
+    both = both + nn(mine[:, 3 * head : 3 * head + 16], small) + nn(recv[:, 3 * head : 3 * head + 16], small2)
+    all_ref[...] = both.astype(BF16)
     for far, out in enumerate(outs):
-        to = pl.ds(pl.multiple_of((chip ^ far) * part, part), part)
-        mine, recv = mine_ref[to, :], recv_ref[to, :]
-        both = nn(jnp.concatenate([mine[:, : 2 * head], recv[:, : 2 * head]], 1), jnp.concatenate([narrow, narrow], 0))
-        both = both + nt(mine[:, 2 * head : 3 * head], wv_ref[...]) + nt(recv[:, 2 * head : 3 * head], wv2_ref[...])
-        both = both + nn(mine[:, 3 * head : 3 * head + 16], small) + nn(recv[:, 3 * head : 3 * head + 16], small2)
-        out[...] = both.astype(BF16)
-
-
-def sum_kernel(*refs):
+        out[...] = all_ref[pl.ds(pl.multiple_of((chip ^ far) * part, part), part), :]
+
+
+def sum_kernel(count, *refs):
     total = refs[0][...].astype(F32)
-    for ref in refs[1:-1]:
+    for ref in refs[1:count]:
         total = total + ref[...].astype(F32)
     refs[-1][...] = total.astype(BF16)
 
@@ -360,18 +363,19 @@
     out_ref[...] = (own_ref[...].astype(F32) + recv_ref[...].astype(F32)).astype(BF16)
 
 
-def local_call(body, outs, args, name, flops):
+def local_call(body, outs, args, name, flops, scratch=(), after=()):
     many = isinstance(outs, tuple)
     spec = pl.BlockSpec(memory_space=pltpu.VMEM)
     return pl.pallas_call(
         body,
         out_shape=outs,
-        in_specs=[spec] * len(args),
+        in_specs=[spec] * len(args) + [pl.BlockSpec(memory_space=pl.ANY)] * len(after),
         out_specs=[spec] * len(outs) if many else spec,
+        scratch_shapes=scratch,
         compiler_params=pltpu.CompilerParams(vmem_limit_bytes=48 * 1024 * 1024),
         cost_estimate=pl.CostEstimate(flops=flops, bytes_accessed=1 << 20, transcendentals=0),
         name=name,
-    )(*args)
+    )(*args, *after)
 
 
 def across(block, distance):
@@ -406,20 +410,20 @@
     narrow = local_call(
         narrow_kernel, block(head + 16, BF16),
         (query_weight.T, key_weight.T, beta_weight.T, decay_weight.T, got[order[0]]), "narrow", 1048576)
-    wv = value_weight
     messages = []
     for d in order:
         messages += [got[d], across(got[d], 1)]
-    narrow2, wv2 = across(narrow, 1), across(wv, 1)
+    narrow2, wv2 = across(narrow, 1), across(value_weight, 1)
 
     all_rows, near, away, value, mine, theirs = core_grads(
-        order, messages, narrow, narrow2, wv, decay_log.reshape(1, 1), decay_bias.reshape(1, 1))
+        order, messages, narrow, narrow2, value_weight, decay_log.reshape(1, 1), decay_bias.reshape(1, 1))
     recv = across(away, 1)
     other = across(theirs, 1)
     qk = local_call(gram_kernel, block(head, BF16), (all_rows, near, recv), "gram", 268435456)
     terms = local_call(
         functools.partial(term_kernel, part), (block(part, BF16),) * chips,
-        (mine, other, narrow, narrow2, wv, wv2), "terms", 1073741824,
+        (mine, other, narrow, narrow2, value_weight, wv2), "terms", 1073741824,
+        [pltpu.VMEM((mine.shape[0], features), BF16)],
     )
     received = [across(terms[d], 2 * d) for d in order if d]
     groups = lax.axis_size("dp")
@@ -430,12 +434,12 @@
             own = sums[name]
             sums[name] = local_call(add_kernel, block(head, BF16), (own, across_data(own, step), terms[0]), "add", 1048576)
     last = {name: across_data(sums[name], rounds - 1) for name in sums}
-    token = local_call(sum_kernel, block(part, BF16), (terms[0], *received), "token_sum", 17179869184)
     q_mean, k_mean, v_mean = local_call(
         functools.partial(mean_kernel, groups),
         (block(half, F32), block(half, F32), jax.ShapeDtypeStruct((features, head), F32)),
-        (sums["qk"], last["qk"], sums["value"], last["value"]), "weight_mean", 1048576,
-    )
+        (sums["qk"], last["qk"], sums["value"], last["value"]), "mean", 1048576)
+    token = local_call(
+        functools.partial(sum_kernel, chips), block(part, BF16), (terms[0], *received), "token_sum", 17179869184, after=())
     return token[None], q_mean.T, k_mean.T, v_mean
 
 

time: 49.8 us -> 48.9 us (0.982)
  Pallas kernels: 9.78 us -> 8.84 us
    pallas_call x8, Pallas kernels: 4.4 us -> 3.46 us  [local_call(): pl.pallas_call(body, out_shape=outs, in_specs=[spec] * len(args) + [pl.Bl...]
  transfers between devices with their start and end apart: 18 -> 18, of which waited for: 4 -> 4; matrix products, arithmetic and copies ran while one was open for 0% -> 0% of each run, Pallas kernels for 17% -> 16%
where the time goes in v4:
time: 48.9 us; the launch traced here: 48.7 us
  waiting for transfers between devices  18.9 us (39%)
  starting transfers between devices  17 us (35%)
  Pallas kernels  8.84 us (18%)
  between operations  2.08 us (4%)
  local copies, waits for them, and re-layouts  1.82 us (4%)
    ppermute x14, waiting for transfers between devices, across(): lax.ppermute(block, 'head', [(i, i ^ distance) for i in range(count)])  18.9 us
    ppermute x14, starting transfers between devices, across(): lax.ppermute(block, 'head', [(i, i ^ distance) for i in range(count)])  12.1 us
    pallas_call x1, Pallas kernels, core_grads(): pl.pallas_call(functools.partial(core_kernel, order), out_shape=(out(tota...  5.38 us
    ppermute x4, starting transfers between devices, across_data(): return lax.ppermute(block, ('dp', 'head'), route)  4.98 us
    pallas_call x8, Pallas kernels, local_call(): pl.pallas_call(body, out_shape=outs, in_specs=[spec] * len(args) + [pl.Bl...  3.46 us
    unnamed x14, local copies, waits for them, and re-layouts  1.82 us
  transfers between devices with their start and end apart: 18, of which 4 were waited for; matrix products, arithmetic and copies ran while one was open for 0% of the time, Pallas kernels for 16%

profile of v4, /device:TPU:0, one launch (start us, length us, event | category | flops | bytes accessed | tf_op | source)
XLA Modules:
  0.0 48.7 jit_solution(5960810475761645014)
XLA Ops:
  0.6 0.9 %copy-done.1 = bf16[1,64,1024]{2,1,0:T(8,128)(2,1)S(1)} copy-done((bf16[1,64,1024]{2,1,0:T(8,128)(2,1)S(1)}, bf16[1,64,1024]{2,1,0:T(8,128)(2,1)}, u32[]{:S(2)}) %copy-start.1) | copy-done | bytes 131096
  1.5 0.9 %copy-done.2 = bf16[1,64,1024]{2,1,0:T(8,128)(2,1)S(1)} copy-done((bf16[1,64,1024]{2,1,0:T(8,128)(2,1)S(1)}, bf16[1,64,1024]{2,1,0:T(8,128)(2,1)}, u32[]{:S(2)}) %copy-start.2) | copy-done | bytes 131096
  2.5 5.1 %collective-permute-start = (bf16[64,1280]{1,0:T(8,128)(2,1)S(1)}, bf16[64,1280]{1,0:T(8,128)(2,1)S(1)}, u32[]{:S(2)}, u32[]{:S(2)}) collective-permute-start(bf16[64,1280]{1,0:T(8,128)(2,1)S(1)} %get-tuple-element.21), channel_id=1, source_target_pairs={{0,6},{1,7},{2,4},{3,5},{4,2},{5,3},{6,0},{7,1},{8,14},{9,15},{10,... | collective-permute-start | bytes 491528 | tf_op jit(solution)/shard_map/ppermute | solution.py:383
  7.6 0.0 collective-permute-start.2
  7.6 0.6 %collective-permute-start.4 = (bf16[64,1280]{1,0:T(8,128)(2,1)S(1)}, bf16[64,1280]{1,0:T(8,128)(2,1)S(1)}, u32[]{:S(2)}, u32[]{:S(2)}) collective-permute-start(bf16[64,1280]{1,0:T(8,128)(2,1)S(1)} %get-tuple-element.23), channel_id=1, source_target_pairs={{0,2},{1,3},{2,0},{3,1},{4,6},{5,7},{6,4},{7,5},{8,10},{9,11},{10,... | collective-permute-start | bytes 491528 | tf_op jit(solution)/shard_map/ppermute | solution.py:383
  8.3 4.5 %collective-permute-done.after_ref.refs_0_ = bf16[64,1280]{1,0:T(8,128)(2,1)S(1)} collective-permute-done((bf16[64,1280]{1,0:T(8,128)(2,1)S(1)}, bf16[64,1280]{1,0:T(8,128)(2,1)S(1)}, u32[]{:S(2)}, u32[]{:S(2)}) %collective-permute-start) | collective-permute-done | bytes 163872 | tf_op jit(solution)/shard_map/ppermute | solution.py:383
  12.8 0.0 copy-start
  12.8 0.1 collective-permute-start.7
  12.9 0.5 %collective-permute-start.6 = (bf16[64,1280]{1,0:T(8,128)(2,1)S(1)}, bf16[64,1280]{1,0:T(8,128)(2,1)S(1)}, u32[]{:S(2)}, u32[]{:S(2)}) collective-permute-start(bf16[64,1280]{1,0:T(8,128)(2,1)S(1)} %get-tuple-element.24.refs_6_), channel_id=1, source_target_pairs={{0,1},{1,0},{2,3},{3,2},{4,5},{5,4},{6,7},{7,6},{8,9},{9,8},{10,11... | collective-permute-start | bytes 491528 | tf_op jit(solution)/shard_map/ppermute | solution.py:383
  13.4 0.1 collective-permute-start.1
  13.5 8.0 %collective-permute-done.2.refs_2_ = bf16[64,1280]{1,0:T(8,128)(2,1)S(1)} collective-permute-done((bf16[64,1280]{1,0:T(8,128)(2,1)S(1)}, bf16[64,1280]{1,0:T(8,128)(2,1)S(1)}, u32[]{:S(2)}, u32[]{:S(2)}) %collective-permute-start.2) | collective-permute-done | bytes 163872 | tf_op jit(solution)/shard_map/ppermute | solution.py:383
  21.5 0.5 %collective-permute-start.5 = (bf16[64,1280]{1,0:T(8,128)(2,1)S(1)}, bf16[64,1280]{1,0:T(8,128)(2,1)S(1)}, u32[]{:S(2)}, u32[]{:S(2)}) collective-permute-start(bf16[64,1280]{1,0:T(8,128)(2,1)S(1)} %collective-permute-done.4.refs_4_), channel_id=1, source_target_pairs={{0,1},{1,0},{2,3},{3,2},{4,5},{5,4},{6,7},{7,6},{8,9},{9,8},{10,11... | collective-permute-start | bytes 491528 | tf_op jit(solution)/shard_map/ppermute | solution.py:383
  23.3 0.0 collective-permute-done.6.refs_7_
  23.3 0.1 collective-permute-start.9
  23.4 0.0 collective-permute-done.3.refs_3_
  23.4 5.4 %core_grads.1 = (bf16[512,1024]{1,0:T(8,128)(2,1)S(1)}, bf16[512,128]{1,0:T(8,128)(2,1)S(1)}, bf16[512,128]{1,0:T(8,128)(2,1)S(1)}, bf16[128,1024]{1,0:T(8,128)(...) custom-call(bf16[64,1280]{1,0:T(8,128)(2,1)S(1)} %collective-permute-done.after_ref.refs_0_, ...), custom_call_target="tpu_custom_call" | custom-call | tf_op jit(solution)/shard_map/core_grads/pallas_call | solution.py:288
  28.8 0.5 %collective-permute-start.8 = (bf16[256,512]{1,0:T(8,128)(2,1)S(1)}, bf16[256,512]{1,0:T(8,128)(2,1)S(1)}, u32[]{:S(2)}, u32[]{:S(2)}) collective-permute-start(bf16[256,512]{1,0:T(8,128)(2,1)S(1)} %get-tuple-element.26), channel_id=1, source_target_pairs={{0,1},{1,0},{2,3},{3,2},{4,5},{5,4},{6,7},{7,6},{8,9},{9,8},{10,11... | collective-permute-start | bytes 786440 | tf_op jit(solution)/shard_map/ppermute | solution.py:383
  29.4 0.1 collective-permute-start.13
  29.5 1.5 %collective-permute-start.16 = (bf16[128,1024]{1,0:T(8,128)(2,1)S(1)}, bf16[128,1024]{1,0:T(8,128)(2,1)S(1)}, u32[]{:S(2)}, u32[]{:S(2)}) collective-permute-start(bf16[128,1024]{1,0:T(8,128)(2,1)S(1)} %get-tuple-element.34.own_ref), channel_id=1, source_target_pairs={{0,8},{1,17},{2,10},{3,19},{4,12},{5,21},{6,14},{7,23},{8,0},{9,25... | collective-permute-start | bytes 786440 | tf_op jit(solution)/shard_map/ppermute | solution.py:394
  30.9 0.5 gram.1.own_ref
  31.4 1.3 %collective-permute-start.14 = (bf16[128,1024]{1,0:T(8,128)(2,1)S(1)}, bf16[128,1024]{1,0:T(8,128)(2,1)S(1)}, u32[]{:S(2)}, u32[]{:S(2)}) collective-permute-start(bf16[128,1024]{1,0:T(8,128)(2,1)S(1)} %gram.1.own_ref), channel_id=1, source_target_pairs={{0,8},{1,17},{2,10},{3,19},{4,12},{5,21},{6,14},{7,23},{8,0},{9,25... | collective-permute-start | bytes 786440 | tf_op jit(solution)/shard_map/ppermute | solution.py:394
  32.8 0.9 %terms.1 = (bf16[64,1024]{1,0:T(8,128)(2,1)S(1)}, bf16[64,1024]{1,0:T(8,128)(2,1)S(1)}, bf16[64,1024]{1,0:T(8,128)(2,1)S(1)}, bf16[64,1024]{1,0:T(8,128)(2,1)S(1)}) custom-call(bf16[256,512]{1,0:T(8,128)(2,1)S(1)} %get-tuple-element.25.mine_ref, bf16[256,512]{1,0:T(8,128)(2,1)S(1)} %collective-permute-done.8.recv_ref, ...), custom_call_target="tpu_custom_call" | custom-call | flops 1073741824 | bytes 1048576 | tf_op jit(solution)/shard_map/terms/pallas_call | solution.py:369
  33.7 2.5 %collective-permute-start.10 = (bf16[64,1024]{1,0:T(8,128)(2,1)S(1)}, bf16[64,1024]{1,0:T(8,128)(2,1)S(1)}, u32[]{:S(2)}, u32[]{:S(2)}) collective-permute-start(bf16[64,1024]{1,0:T(8,128)(2,1)S(1)} %get-tuple-element.28), channel_id=1, source_target_pairs={{0,6},{1,7},{2,4},{3,5},{4,2},{5,3},{6,0},{7,1},{8,14},{9,15},{10,... | collective-permute-start | bytes 393224 | tf_op jit(solution)/shard_map/ppermute | solution.py:383
  36.2 1.9 %collective-permute-start.12 = (bf16[64,1024]{1,0:T(8,128)(2,1)S(1)}, bf16[64,1024]{1,0:T(8,128)(2,1)S(1)}, u32[]{:S(2)}, u32[]{:S(2)}) collective-permute-start(bf16[64,1024]{1,0:T(8,128)(2,1)S(1)} %get-tuple-element.30), channel_id=1, source_target_pairs={{0,2},{1,3},{2,0},{3,1},{4,6},{5,7},{6,4},{7,5},{8,10},{9,11},{10,... | collective-permute-start | bytes 393224 | tf_op jit(solution)/shard_map/ppermute | solution.py:383
  38.1 0.1 add.3.own_v
  38.2 1.6 %collective-permute-start.17 = (bf16[128,1024]{1,0:T(8,128)(2,1)S(1)}, bf16[128,1024]{1,0:T(8,128)(2,1)S(1)}, u32[]{:S(2)}, u32[]{:S(2)}) collective-permute-start(bf16[128,1024]{1,0:T(8,128)(2,1)S(1)} %add.3.own_v), channel_id=1, source_target_pairs={{0,16},{1,9},{2,18},{3,11},{4,20},{5,13},{6,22},{7,15},{8,24},{9,1... | collective-permute-start | bytes 786440 | tf_op jit(solution)/shard_map/ppermute | solution.py:394
  39.8 0.1 add.2.own_qk
  39.9 0.6 %collective-permute-start.15 = (bf16[128,1024]{1,0:T(8,128)(2,1)S(1)}, bf16[128,1024]{1,0:T(8,128)(2,1)S(1)}, u32[]{:S(2)}, u32[]{:S(2)}) collective-permute-start(bf16[128,1024]{1,0:T(8,128)(2,1)S(1)} %add.2.own_qk), channel_id=1, source_target_pairs={{0,16},{1,9},{2,18},{3,11},{4,20},{5,13},{6,22},{7,15},{8,24},{9,1... | collective-permute-start | bytes 786440 | tf_op jit(solution)/shard_map/ppermute | solution.py:394
  40.4 1.6 %collective-permute-done.10.refs_1_ = bf16[64,1024]{1,0:T(8,128)(2,1)S(1)} collective-permute-done((bf16[64,1024]{1,0:T(8,128)(2,1)S(1)}, bf16[64,1024]{1,0:T(8,128)(2,1)S(1)}, u32[]{:S(2)}, u32[]{:S(2)}) %collective-permute-start.10) | collective-permute-done | bytes 131104 | tf_op jit(solution)/shard_map/ppermute | solution.py:383
  42.0 4.8 %collective-permute-done.11.refs_2_ = bf16[64,1024]{1,0:T(8,128)(2,1)S(1)} collective-permute-done((bf16[64,1024]{1,0:T(8,128)(2,1)S(1)}, bf16[64,1024]{1,0:T(8,128)(2,1)S(1)}, u32[]{:S(2)}, u32[]{:S(2)}) %collective-permute-start.11) | collective-permute-done | bytes 131104 | tf_op jit(solution)/shard_map/ppermute | solution.py:383
  46.8 0.7 %token_sum.1 = bf16[64,1024]{1,0:T(8,128)(2,1)} custom-call(bf16[64,1024]{1,0:T(8,128)(2,1)S(1)} %get-tuple-element.27.refs_0_.after_ref, bf16[64,1024]{1,0:T(8,128)(2,1)S(1)} %collective-permute-done.10.refs_1_, bf16[64,1024]{1,0:T(8,128)(2,1)S(1)} %collective-permute-done.11.refs_2_, bf16[64,1024]{1,0:T(8,128)(2,1)S(1)} %collective-permute-done.12.refs_3_), custom_call_target="tpu_custom_call" | custom-call | flops 17179869184 | bytes 1048576 | tf_op jit(solution)/shard_map/token_sum/pallas_call | solution.py:369
  47.5 1.2 %mean.1 = (f32[64,1024]{1,0:T(8,128)}, f32[64,1024]{1,0:T(8,128)}, f32[1024,128]{1,0:T(8,128)}) custom-call(bf16[128,1024]{1,0:T(8,128)(2,1)S(1)} %add.2.own_qk, bf16[128,1024]{1,0:T(8,128)(2,1)S(1)} %collective-permute-done.15.recv_qk, bf16[128,1024]{1,0:T(8,128)(2,1)S(1)} %add.3.own_v, bf16[128,1024]{1,0:T(8,128)(2,1)S(1)} %collective-permute-done.17.recv_v), custom_call_target="tpu_custom_call" | custom-call | flops 1048576 | bytes 1048576 | tf_op jit(solution)/shard_map/mean/pallas_call | solution.py:369
  (27 shorter events, 0.1 us)
Async XLA Ops:
  0.6 0.9 %copy-start.1 = (bf16[1,64,1024]{2,1,0:T(8,128)(2,1)S(1)}, bf16[1,64,1024]{2,1,0:T(8,128)(2,1)}, u32[]{:S(2)}) copy-start(bf16[1,64,1024]{2,1,0:T(8,128)(2,1)} %param.9) | copy-start | bytes 393220
  1.5 0.9 %copy-start.2 = (bf16[1,64,1024]{2,1,0:T(8,128)(2,1)S(1)}, bf16[1,64,1024]{2,1,0:T(8,128)(2,1)}, u32[]{:S(2)}) copy-start(bf16[1,64,1024]{2,1,0:T(8,128)(2,1)} %param.10) | copy-start | bytes 393220
  2.4 10.3 %copy-start.3 = (bf16[1024,64]{0,1:T(8,128)(2,1)S(1)}, bf16[1024,64]{0,1:T(8,128)(2,1)}, u32[]{:S(2)}) copy-start(bf16[1024,64]{0,1:T(8,128)(2,1)} %param.11) | copy-start | bytes 393220
  2.4 10.3 %copy-start.4 = (bf16[1024,64]{0,1:T(8,128)(2,1)S(1)}, bf16[1024,64]{0,1:T(8,128)(2,1)}, u32[]{:S(2)}) copy-start(bf16[1024,64]{0,1:T(8,128)(2,1)} %param.12) | copy-start | bytes 393220
  2.5 10.2 %collective-permute-start = (bf16[64,1280]{1,0:T(8,128)(2,1)S(1)}, bf16[64,1280]{1,0:T(8,128)(2,1)S(1)}, u32[]{:S(2)}, u32[]{:S(2)}) collective-permute-start(bf16[64,1280]{1,0:T(8,128)(2,1)S(1)} %get-tuple-element.21), channel_id=1, source_target_pairs={{0,6},{1,7},{2,4},{3,5},{4,2},{5,3},{6,0},{7,1},{8,14},{9,15},{10,... | collective-permute-start | bytes 491528 | tf_op jit(solution)/shard_map/ppermute | solution.py:383
  7.6 13.9 %collective-permute-start.2 = (bf16[64,1280]{1,0:T(8,128)(2,1)S(1)}, bf16[64,1280]{1,0:T(8,128)(2,1)S(1)}, u32[]{:S(2)}, u32[]{:S(2)}) collective-permute-start(bf16[64,1280]{1,0:T(8,128)(2,1)S(1)} %get-tuple-element.22), channel_id=1, source_target_pairs={{0,4},{1,5},{2,6},{3,7},{4,0},{5,1},{6,2},{7,3},{8,12},{9,13},{10,... | collective-permute-start | bytes 491528 | tf_op jit(solution)/shard_map/ppermute | solution.py:383
  7.6 5.1 %copy-start.6 = (bf16[1024,1]{0,1:T(2,128)(2,1)S(1)}, bf16[1024,1]{0,1:T(2,128)(2,1)}, u32[]{:S(2)}) copy-start(bf16[1024,1]{0,1:T(2,128)(2,1)} %param.15) | copy-start | bytes 6148
  7.6 5.1 %copy-start.5 = (bf16[1024,1]{0,1:T(2,128)(2,1)S(1)}, bf16[1024,1]{0,1:T(2,128)(2,1)}, u32[]{:S(2)}) copy-start(bf16[1024,1]{0,1:T(2,128)(2,1)} %param.14) | copy-start | bytes 6148
  7.6 13.9 %collective-permute-start.4 = (bf16[64,1280]{1,0:T(8,128)(2,1)S(1)}, bf16[64,1280]{1,0:T(8,128)(2,1)S(1)}, u32[]{:S(2)}, u32[]{:S(2)}) collective-permute-start(bf16[64,1280]{1,0:T(8,128)(2,1)S(1)} %get-tuple-element.23), channel_id=1, source_target_pairs={{0,2},{1,3},{2,0},{3,1},{4,6},{5,7},{6,4},{7,5},{8,10},{9,11},{10,... | collective-permute-start | bytes 491528 | tf_op jit(solution)/shard_map/ppermute | solution.py:383
  12.8 10.6 %copy-start = (bf16[1024,128]{1,0:T(8,128)(2,1)S(1)}, bf16[1024,128]{1,0:T(8,128)(2,1)}, u32[]{:S(2)}) copy-start(bf16[1024,128]{1,0:T(8,128)(2,1)} %wv_ref.1) | copy-start | bytes 786436
  12.8 10.6 %collective-permute-start.7 = (bf16[144,1024]{1,0:T(8,128)(2,1)S(1)}, bf16[144,1024]{1,0:T(8,128)(2,1)S(1)}, u32[]{:S(2)}, u32[]{:S(2)}) collective-permute-start(bf16[144,1024]{1,0:T(8,128)(2,1)S(1)} %narrow.1.refs_8_.own), channel_id=1, source_target_pairs={{0,1},{1,0},{2,3},{3,2},{4,5},{5,4},{6,7},{7,6},{8,9},{9,8},{10,11... | collective-permute-start | bytes 884744 | tf_op jit(solution)/shard_map/ppermute | solution.py:383
  12.9 10.4 %collective-permute-start.6 = (bf16[64,1280]{1,0:T(8,128)(2,1)S(1)}, bf16[64,1280]{1,0:T(8,128)(2,1)S(1)}, u32[]{:S(2)}, u32[]{:S(2)}) collective-permute-start(bf16[64,1280]{1,0:T(8,128)(2,1)S(1)} %get-tuple-element.24.refs_6_), channel_id=1, source_target_pairs={{0,1},{1,0},{2,3},{3,2},{4,5},{5,4},{6,7},{7,6},{8,9},{9,8},{10,11... | collective-permute-start | bytes 491528 | tf_op jit(solution)/shard_map/ppermute | solution.py:383
  13.4 10.0 %collective-permute-start.1 = (bf16[64,1280]{1,0:T(8,128)(2,1)S(1)}, bf16[64,1280]{1,0:T(8,128)(2,1)S(1)}, u32[]{:S(2)}, u32[]{:S(2)}) collective-permute-start(bf16[64,1280]{1,0:T(8,128)(2,1)S(1)} %collective-permute-done.after_ref.refs_0_), channel_id=1, source_target_pairs={{0,1},{1,0},{2,3},{3,2},{4,5},{5,4},{6,7},{7,6},{8,9},{9,8},{10,11... | collective-permute-start | bytes 491528 | tf_op jit(solution)/shard_map/ppermute | solution.py:383
  21.5 1.9 %collective-permute-start.3 = (bf16[64,1280]{1,0:T(8,128)(2,1)S(1)}, bf16[64,1280]{1,0:T(8,128)(2,1)S(1)}, u32[]{:S(2)}, u32[]{:S(2)}) collective-permute-start(bf16[64,1280]{1,0:T(8,128)(2,1)S(1)} %collective-permute-done.2.refs_2_), channel_id=1, source_target_pairs={{0,1},{1,0},{2,3},{3,2},{4,5},{5,4},{6,7},{7,6},{8,9},{9,8},{10,11... | collective-permute-start | bytes 491528 | tf_op jit(solution)/shard_map/ppermute | solution.py:383
  21.5 1.9 %collective-permute-start.5 = (bf16[64,1280]{1,0:T(8,128)(2,1)S(1)}, bf16[64,1280]{1,0:T(8,128)(2,1)S(1)}, u32[]{:S(2)}, u32[]{:S(2)}) collective-permute-start(bf16[64,1280]{1,0:T(8,128)(2,1)S(1)} %collective-permute-done.4.refs_4_), channel_id=1, source_target_pairs={{0,1},{1,0},{2,3},{3,2},{4,5},{5,4},{6,7},{7,6},{8,9},{9,8},{10,11... | collective-permute-start | bytes 491528 | tf_op jit(solution)/shard_map/ppermute | solution.py:383
  23.3 9.4 %collective-permute-start.9 = (bf16[1024,128]{1,0:T(8,128)(2,1)S(1)}, bf16[1024,128]{1,0:T(8,128)(2,1)S(1)}, u32[]{:S(2)}, u32[]{:S(2)}) collective-permute-start(bf16[1024,128]{1,0:T(8,128)(2,1)S(1)} %copy-done), channel_id=1, source_target_pairs={{0,1},{1,0},{2,3},{3,2},{4,5},{5,4},{6,7},{7,6},{8,9},{9,8},{10,11... | collective-permute-start | bytes 786440 | tf_op jit(solution)/shard_map/ppermute | solution.py:383
  28.8 3.9 %collective-permute-start.8 = (bf16[256,512]{1,0:T(8,128)(2,1)S(1)}, bf16[256,512]{1,0:T(8,128)(2,1)S(1)}, u32[]{:S(2)}, u32[]{:S(2)}) collective-permute-start(bf16[256,512]{1,0:T(8,128)(2,1)S(1)} %get-tuple-element.26), channel_id=1, source_target_pairs={{0,1},{1,0},{2,3},{3,2},{4,5},{5,4},{6,7},{7,6},{8,9},{9,8},{10,11... | collective-permute-start | bytes 786440 | tf_op jit(solution)/shard_map/ppermute | solution.py:383
  29.4 1.6 %collective-permute-start.13 = (bf16[512,128]{1,0:T(8,128)(2,1)S(1)}, bf16[512,128]{1,0:T(8,128)(2,1)S(1)}, u32[]{:S(2)}, u32[]{:S(2)}) collective-permute-start(bf16[512,128]{1,0:T(8,128)(2,1)S(1)} %get-tuple-element.33), channel_id=1, source_target_pairs={{0,1},{1,0},{2,3},{3,2},{4,5},{5,4},{6,7},{7,6},{8,9},{9,8},{10,11... | collective-permute-start | bytes 393224 | tf_op jit(solution)/shard_map/ppermute | solution.py:383
  29.5 8.7 %collective-permute-start.16 = (bf16[128,1024]{1,0:T(8,128)(2,1)S(1)}, bf16[128,1024]{1,0:T(8,128)(2,1)S(1)}, u32[]{:S(2)}, u32[]{:S(2)}) collective-permute-start(bf16[128,1024]{1,0:T(8,128)(2,1)S(1)} %get-tuple-element.34.own_ref), channel_id=1, source_target_pairs={{0,8},{1,17},{2,10},{3,19},{4,12},{5,21},{6,14},{7,23},{8,0},{9,25... | collective-permute-start | bytes 786440 | tf_op jit(solution)/shard_map/ppermute | solution.py:394
  31.4 8.4 %collective-permute-start.14 = (bf16[128,1024]{1,0:T(8,128)(2,1)S(1)}, bf16[128,1024]{1,0:T(8,128)(2,1)S(1)}, u32[]{:S(2)}, u32[]{:S(2)}) collective-permute-start(bf16[128,1024]{1,0:T(8,128)(2,1)S(1)} %gram.1.own_ref), channel_id=1, source_target_pairs={{0,8},{1,17},{2,10},{3,19},{4,12},{5,21},{6,14},{7,23},{8,0},{9,25... | collective-permute-start | bytes 786440 | tf_op jit(solution)/shard_map/ppermute | solution.py:394
  33.7 8.3 %collective-permute-start.10 = (bf16[64,1024]{1,0:T(8,128)(2,1)S(1)}, bf16[64,1024]{1,0:T(8,128)(2,1)S(1)}, u32[]{:S(2)}, u32[]{:S(2)}) collective-permute-start(bf16[64,1024]{1,0:T(8,128)(2,1)S(1)} %get-tuple-element.28), channel_id=1, source_target_pairs={{0,6},{1,7},{2,4},{3,5},{4,2},{5,3},{6,0},{7,1},{8,14},{9,15},{10,... | collective-permute-start | bytes 393224 | tf_op jit(solution)/shard_map/ppermute | solution.py:383
  36.2 10.6 %collective-permute-start.11 = (bf16[64,1024]{1,0:T(8,128)(2,1)S(1)}, bf16[64,1024]{1,0:T(8,128)(2,1)S(1)}, u32[]{:S(2)}, u32[]{:S(2)}) collective-permute-start(bf16[64,1024]{1,0:T(8,128)(2,1)S(1)} %get-tuple-element.29), channel_id=1, source_target_pairs={{0,4},{1,5},{2,6},{3,7},{4,0},{5,1},{6,2},{7,3},{8,12},{9,13},{10,... | collective-permute-start | bytes 393224 | tf_op jit(solution)/shard_map/ppermute | solution.py:383
  36.2 10.6 %collective-permute-start.12 = (bf16[64,1024]{1,0:T(8,128)(2,1)S(1)}, bf16[64,1024]{1,0:T(8,128)(2,1)S(1)}, u32[]{:S(2)}, u32[]{:S(2)}) collective-permute-start(bf16[64,1024]{1,0:T(8,128)(2,1)S(1)} %get-tuple-element.30), channel_id=1, source_target_pairs={{0,2},{1,3},{2,0},{3,1},{4,6},{5,7},{6,4},{7,5},{8,10},{9,11},{10,... | collective-permute-start | bytes 393224 | tf_op jit(solution)/shard_map/ppermute | solution.py:383
  38.2 9.3 %collective-permute-start.17 = (bf16[128,1024]{1,0:T(8,128)(2,1)S(1)}, bf16[128,1024]{1,0:T(8,128)(2,1)S(1)}, u32[]{:S(2)}, u32[]{:S(2)}) collective-permute-start(bf16[128,1024]{1,0:T(8,128)(2,1)S(1)} %add.3.own_v), channel_id=1, source_target_pairs={{0,16},{1,9},{2,18},{3,11},{4,20},{5,13},{6,22},{7,15},{8,24},{9,1... | collective-permute-start | bytes 786440 | tf_op jit(solution)/shard_map/ppermute | solution.py:394
  39.9 7.7 %collective-permute-start.15 = (bf16[128,1024]{1,0:T(8,128)(2,1)S(1)}, bf16[128,1024]{1,0:T(8,128)(2,1)S(1)}, u32[]{:S(2)}, u32[]{:S(2)}) collective-permute-start(bf16[128,1024]{1,0:T(8,128)(2,1)S(1)} %add.2.own_qk), channel_id=1, source_target_pairs={{0,16},{1,9},{2,18},{3,11},{4,20},{5,13},{6,22},{7,15},{8,24},{9,1... | collective-permute-start | bytes 786440 | tf_op jit(solution)/shard_map/ppermute | solution.py:394

commit v5 on v4

--- a/solution.py
+++ b/solution.py
@@ -348,15 +348,20 @@
     total = refs[0][...].astype(F32)
     for ref in refs[1:count]:
         total = total + ref[...].astype(F32)
-    refs[-1][...] = total.astype(BF16)
-
-
-def mean_kernel(count, own_qk, recv_qk, own_v, recv_v, q_ref, k_ref, v_ref):
+    refs[-1][...] = total
+
+
+def last_kernel(count, own_qk, recv_qk, own_v, recv_v, *refs):
+    blocks, (q_ref, k_ref, v_ref, token_ref) = refs[:-4], refs[-4:]
     half = q_ref.shape[0]
     qk = (own_qk[...].astype(F32) + recv_qk[...].astype(F32)) * (1.0 / count)
     q_ref[...] = qk[:half]
     k_ref[...] = qk[half:]
     v_ref[...] = ((own_v[...].astype(F32) + recv_v[...].astype(F32)) * (1.0 / count)).T
+    total = blocks[0][...].astype(F32)
+    for ref in blocks[1:]:
+        total = total + ref[...].astype(F32)
+    token_ref[...] = total.astype(BF16)
 
 
 def add_kernel(own_ref, recv_ref, after_ref, out_ref):
@@ -434,12 +439,12 @@
             own = sums[name]
             sums[name] = local_call(add_kernel, block(head, BF16), (own, across_data(own, step), terms[0]), "add", 1048576)
     last = {name: across_data(sums[name], rounds - 1) for name in sums}
-    q_mean, k_mean, v_mean = local_call(
-        functools.partial(mean_kernel, groups),
-        (block(half, F32), block(half, F32), jax.ShapeDtypeStruct((features, head), F32)),
-        (sums["qk"], last["qk"], sums["value"], last["value"]), "mean", 1048576)
-    token = local_call(
-        functools.partial(sum_kernel, chips), block(part, BF16), (terms[0], *received), "token_sum", 17179869184, after=())
+    begun = local_call(
+        functools.partial(sum_kernel, 2), block(part, F32), (terms[0], received[0]), "token_begin", 17179869184)
+    q_mean, k_mean, v_mean, token = local_call(
+        functools.partial(last_kernel, groups),
+        (block(half, F32), block(half, F32), jax.ShapeDtypeStruct((features, head), F32), block(part, BF16)),
+        (sums["qk"], last["qk"], sums["value"], last["value"], begun, *received[1:]), "last", 1048576)
     return token[None], q_mean.T, k_mean.T, v_mean
 
 

time: 48.9 us -> 48.4 us (0.990)
  starting transfers between devices: 17 us -> 17.8 us
  Pallas kernels: 8.84 us -> 8.18 us
  waiting for transfers between devices: 18.9 us -> 18.4 us
    ppermute x14, waiting for transfers between devices: 18.9 us -> 18.1 us  [across(): lax.ppermute(block, 'head', [(i, i ^ distance) for i in range(count)])]
    ppermute x14, starting transfers between devices: 12.1 us -> 12.8 us  [across(): lax.ppermute(block, 'head', [(i, i ^ distance) for i in range(count)])]
    pallas_call x8, Pallas kernels: 3.46 us -> 2.8 us  [local_call(): pl.pallas_call(body, out_shape=outs, in_specs=[spec] * len(args) + [pl.Bl...]
  transfers between devices with their start and end apart: 18 -> 18, of which waited for: 4 -> 5; matrix products, arithmetic and copies ran while one was open for 0% -> 0% of each run, Pallas kernels for 16% -> 14%
where the time goes in v5:
time: 48.4 us; the launch traced here: 48.2 us
  waiting for transfers between devices  18.4 us (38%)
  starting transfers between devices  17.8 us (37%)
  Pallas kernels  8.18 us (17%)
  between operations  2.08 us (4%)
  local copies, waits for them, and re-layouts  1.82 us (4%)
    ppermute x14, waiting for transfers between devices, across(): lax.ppermute(block, 'head', [(i, i ^ distance) for i in range(count)])  18.1 us
    ppermute x14, starting transfers between devices, across(): lax.ppermute(block, 'head', [(i, i ^ distance) for i in range(count)])  12.8 us
    pallas_call x1, Pallas kernels, core_grads(): pl.pallas_call(functools.partial(core_kernel, order), out_shape=(out(tota...  5.38 us
    ppermute x4, starting transfers between devices, across_data(): return lax.ppermute(block, ('dp', 'head'), route)  4.98 us
    pallas_call x8, Pallas kernels, local_call(): pl.pallas_call(body, out_shape=outs, in_specs=[spec] * len(args) + [pl.Bl...  2.8 us
    unnamed x14, local copies, waits for them, and re-layouts  1.82 us
  transfers between devices with their start and end apart: 18, of which 5 were waited for; matrix products, arithmetic and copies ran while one was open for 0% of the time, Pallas kernels for 14%

profile of v5, /device:TPU:0, one launch (start us, length us, event | category | flops | bytes accessed | tf_op | source)
XLA Modules:
  0.0 48.2 jit_solution(13967411293118173569)
XLA Ops:
  0.6 0.9 %copy-done.1 = bf16[1,64,1024]{2,1,0:T(8,128)(2,1)S(1)} copy-done((bf16[1,64,1024]{2,1,0:T(8,128)(2,1)S(1)}, bf16[1,64,1024]{2,1,0:T(8,128)(2,1)}, u32[]{:S(2)}) %copy-start.1) | copy-done | bytes 131096
  1.5 0.9 %copy-done.2 = bf16[1,64,1024]{2,1,0:T(8,128)(2,1)S(1)} copy-done((bf16[1,64,1024]{2,1,0:T(8,128)(2,1)S(1)}, bf16[1,64,1024]{2,1,0:T(8,128)(2,1)}, u32[]{:S(2)}) %copy-start.2) | copy-done | bytes 131096
  2.5 5.1 %collective-permute-start = (bf16[64,1280]{1,0:T(8,128)(2,1)S(1)}, bf16[64,1280]{1,0:T(8,128)(2,1)S(1)}, u32[]{:S(2)}, u32[]{:S(2)}) collective-permute-start(bf16[64,1280]{1,0:T(8,128)(2,1)S(1)} %get-tuple-element.22), channel_id=1, source_target_pairs={{0,6},{1,7},{2,4},{3,5},{4,2},{5,3},{6,0},{7,1},{8,14},{9,15},{10,... | collective-permute-start | bytes 491528 | tf_op jit(solution)/shard_map/ppermute | solution.py:388
  7.6 0.6 %collective-permute-start.4 = (bf16[64,1280]{1,0:T(8,128)(2,1)S(1)}, bf16[64,1280]{1,0:T(8,128)(2,1)S(1)}, u32[]{:S(2)}, u32[]{:S(2)}) collective-permute-start(bf16[64,1280]{1,0:T(8,128)(2,1)S(1)} %get-tuple-element.24), channel_id=1, source_target_pairs={{0,2},{1,3},{2,0},{3,1},{4,6},{5,7},{6,4},{7,5},{8,10},{9,11},{10,... | collective-permute-start | bytes 491528 | tf_op jit(solution)/shard_map/ppermute | solution.py:388
  8.3 4.5 %collective-permute-done.after_ref.refs_0_ = bf16[64,1280]{1,0:T(8,128)(2,1)S(1)} collective-permute-done((bf16[64,1280]{1,0:T(8,128)(2,1)S(1)}, bf16[64,1280]{1,0:T(8,128)(2,1)S(1)}, u32[]{:S(2)}, u32[]{:S(2)}) %collective-permute-start) | collective-permute-done | bytes 163872 | tf_op jit(solution)/shard_map/ppermute | solution.py:388
  12.8 0.0 copy-start
  12.8 0.1 collective-permute-start.7
  12.9 0.5 %collective-permute-start.6 = (bf16[64,1280]{1,0:T(8,128)(2,1)S(1)}, bf16[64,1280]{1,0:T(8,128)(2,1)S(1)}, u32[]{:S(2)}, u32[]{:S(2)}) collective-permute-start(bf16[64,1280]{1,0:T(8,128)(2,1)S(1)} %get-tuple-element.25.refs_6_), channel_id=1, source_target_pairs={{0,1},{1,0},{2,3},{3,2},{4,5},{5,4},{6,7},{7,6},{8,9},{9,8},{10,11... | collective-permute-start | bytes 491528 | tf_op jit(solution)/shard_map/ppermute | solution.py:388
  13.4 0.1 collective-permute-start.1
  13.5 8.0 %collective-permute-done.2.refs_2_ = bf16[64,1280]{1,0:T(8,128)(2,1)S(1)} collective-permute-done((bf16[64,1280]{1,0:T(8,128)(2,1)S(1)}, bf16[64,1280]{1,0:T(8,128)(2,1)S(1)}, u32[]{:S(2)}, u32[]{:S(2)}) %collective-permute-start.2) | collective-permute-done | bytes 163872 | tf_op jit(solution)/shard_map/ppermute | solution.py:388
  21.5 0.5 %collective-permute-start.5 = (bf16[64,1280]{1,0:T(8,128)(2,1)S(1)}, bf16[64,1280]{1,0:T(8,128)(2,1)S(1)}, u32[]{:S(2)}, u32[]{:S(2)}) collective-permute-start(bf16[64,1280]{1,0:T(8,128)(2,1)S(1)} %collective-permute-done.4.refs_4_), channel_id=1, source_target_pairs={{0,1},{1,0},{2,3},{3,2},{4,5},{5,4},{6,7},{7,6},{8,9},{9,8},{10,11... | collective-permute-start | bytes 491528 | tf_op jit(solution)/shard_map/ppermute | solution.py:388
  23.3 0.0 collective-permute-done.6.refs_7_
  23.3 0.1 collective-permute-start.11
  23.4 0.0 collective-permute-done.1.refs_1_
  23.4 0.0 collective-permute-done.3.refs_3_
  23.4 5.4 %core_grads.1 = (bf16[512,1024]{1,0:T(8,128)(2,1)S(1)}, bf16[512,128]{1,0:T(8,128)(2,1)S(1)}, bf16[512,128]{1,0:T(8,128)(2,1)S(1)}, bf16[128,1024]{1,0:T(8,128)(...) custom-call(bf16[64,1280]{1,0:T(8,128)(2,1)S(1)} %collective-permute-done.after_ref.refs_0_, ...), custom_call_target="tpu_custom_call" | custom-call | tf_op jit(solution)/shard_map/core_grads/pallas_call | solution.py:288
  28.8 0.5 %collective-permute-start.10 = (bf16[256,512]{1,0:T(8,128)(2,1)S(1)}, bf16[256,512]{1,0:T(8,128)(2,1)S(1)}, u32[]{:S(2)}, u32[]{:S(2)}) collective-permute-start(bf16[256,512]{1,0:T(8,128)(2,1)S(1)} %get-tuple-element.30), channel_id=1, source_target_pairs={{0,1},{1,0},{2,3},{3,2},{4,5},{5,4},{6,7},{7,6},{8,9},{9,8},{10,11... | collective-permute-start | bytes 786440 | tf_op jit(solution)/shard_map/ppermute | solution.py:388
  29.4 0.1 collective-permute-start.8
  29.5 1.5 %collective-permute-start.13 = (bf16[128,1024]{1,0:T(8,128)(2,1)S(1)}, bf16[128,1024]{1,0:T(8,128)(2,1)S(1)}, u32[]{:S(2)}, u32[]{:S(2)}) collective-permute-start(bf16[128,1024]{1,0:T(8,128)(2,1)S(1)} %get-tuple-element.32.own_ref), channel_id=1, source_target_pairs={{0,8},{1,17},{2,10},{3,19},{4,12},{5,21},{6,14},{7,23},{8,0},{9,25... | collective-permute-start | bytes 786440 | tf_op jit(solution)/shard_map/ppermute | solution.py:399
  30.9 0.5 gram.1.own_ref
  31.4 1.3 %collective-permute-start.9 = (bf16[128,1024]{1,0:T(8,128)(2,1)S(1)}, bf16[128,1024]{1,0:T(8,128)(2,1)S(1)}, u32[]{:S(2)}, u32[]{:S(2)}) collective-permute-start(bf16[128,1024]{1,0:T(8,128)(2,1)S(1)} %gram.1.own_ref), channel_id=1, source_target_pairs={{0,8},{1,17},{2,10},{3,19},{4,12},{5,21},{6,14},{7,23},{8,0},{9,25... | collective-permute-start | bytes 786440 | tf_op jit(solution)/shard_map/ppermute | solution.py:399
  32.8 0.9 %terms.1 = (bf16[64,1024]{1,0:T(8,128)(2,1)S(1)}, bf16[64,1024]{1,0:T(8,128)(2,1)S(1)}, bf16[64,1024]{1,0:T(8,128)(2,1)S(1)}, bf16[64,1024]{1,0:T(8,128)(2,1)S(1)}) custom-call(bf16[256,512]{1,0:T(8,128)(2,1)S(1)} %get-tuple-element.29.mine_ref, bf16[256,512]{1,0:T(8,128)(2,1)S(1)} %collective-permute-done.10.recv_ref, ...), custom_call_target="tpu_custom_call" | custom-call | flops 1073741824 | bytes 1048576 | tf_op jit(solution)/shard_map/terms/pallas_call | solution.py:374
  33.7 2.5 %collective-permute-start.15 = (bf16[64,1024]{1,0:T(8,128)(2,1)S(1)}, bf16[64,1024]{1,0:T(8,128)(2,1)S(1)}, u32[]{:S(2)}, u32[]{:S(2)}) collective-permute-start(bf16[64,1024]{1,0:T(8,128)(2,1)S(1)} %get-tuple-element.33), channel_id=1, source_target_pairs={{0,6},{1,7},{2,4},{3,5},{4,2},{5,3},{6,0},{7,1},{8,14},{9,15},{10,... | collective-permute-start | bytes 393224 | tf_op jit(solution)/shard_map/ppermute | solution.py:388
  36.2 0.1 add.3.own_v
  36.3 1.6 %collective-permute-start.14 = (bf16[128,1024]{1,0:T(8,128)(2,1)S(1)}, bf16[128,1024]{1,0:T(8,128)(2,1)S(1)}, u32[]{:S(2)}, u32[]{:S(2)}) collective-permute-start(bf16[128,1024]{1,0:T(8,128)(2,1)S(1)} %add.3.own_v), channel_id=1, source_target_pairs={{0,16},{1,9},{2,18},{3,11},{4,20},{5,13},{6,22},{7,15},{8,24},{9,1... | collective-permute-start | bytes 786440 | tf_op jit(solution)/shard_map/ppermute | solution.py:399
  37.9 2.6 %collective-permute-start.17 = (bf16[64,1024]{1,0:T(8,128)(2,1)S(1)}, bf16[64,1024]{1,0:T(8,128)(2,1)S(1)}, u32[]{:S(2)}, u32[]{:S(2)}) collective-permute-start(bf16[64,1024]{1,0:T(8,128)(2,1)S(1)} %get-tuple-element.35), channel_id=1, source_target_pairs={{0,2},{1,3},{2,0},{3,1},{4,6},{5,7},{6,4},{7,5},{8,10},{9,11},{10,... | collective-permute-start | bytes 393224 | tf_op jit(solution)/shard_map/ppermute | solution.py:388
  40.5 0.1 add.2.own_qk
  40.6 0.6 %collective-permute-start.12 = (bf16[128,1024]{1,0:T(8,128)(2,1)S(1)}, bf16[128,1024]{1,0:T(8,128)(2,1)S(1)}, u32[]{:S(2)}, u32[]{:S(2)}) collective-permute-start(bf16[128,1024]{1,0:T(8,128)(2,1)S(1)} %add.2.own_qk), channel_id=1, source_target_pairs={{0,16},{1,9},{2,18},{3,11},{4,20},{5,13},{6,22},{7,15},{8,24},{9,1... | collective-permute-start | bytes 786440 | tf_op jit(solution)/shard_map/ppermute | solution.py:399
  41.2 0.8 %collective-permute-done.15.refs_1_ = bf16[64,1024]{1,0:T(8,128)(2,1)S(1)} collective-permute-done((bf16[64,1024]{1,0:T(8,128)(2,1)S(1)}, bf16[64,1024]{1,0:T(8,128)(2,1)S(1)}, u32[]{:S(2)}, u32[]{:S(2)}) %collective-permute-start.15) | collective-permute-done | bytes 131104 | tf_op jit(solution)/shard_map/ppermute | solution.py:388
  42.0 4.7 %collective-permute-done.16.refs_1_ = bf16[64,1024]{1,0:T(8,128)(2,1)S(1)} collective-permute-done((bf16[64,1024]{1,0:T(8,128)(2,1)S(1)}, bf16[64,1024]{1,0:T(8,128)(2,1)S(1)}, u32[]{:S(2)}, u32[]{:S(2)}) %collective-permute-start.16) | collective-permute-done | bytes 131104 | tf_op jit(solution)/shard_map/ppermute | solution.py:388
  46.7 0.3 collective-permute-done.12.recv_qk
  47.0 1.2 %last.1 = (f32[64,1024]{1,0:T(8,128)}, f32[64,1024]{1,0:T(8,128)}, f32[1024,128]{1,0:T(8,128)}, bf16[64,1024]{1,0:T(8,128)(2,1)}) custom-call(bf16[128,1024]{1,0:T(8,128)(2,1)S(1)} %add.2.own_qk, bf16[128,1024]{1,0:T(8,128)(2,1)S(1)} %collective-permute-done.12.recv_qk, bf16[128,1024]{1,0:T(8,128)(2,1)S(1)} %add.3.own_v, ...), custom_call_target="tpu_custom_call" | custom-call | flops 1048576 | bytes 1048576 | tf_op jit(solution)/shard_map/last/pallas_call | solution.py:374
  (27 shorter events, 0.2 us)
Async XLA Ops:
  0.6 0.9 %copy-start.1 = (bf16[1,64,1024]{2,1,0:T(8,128)(2,1)S(1)}, bf16[1,64,1024]{2,1,0:T(8,128)(2,1)}, u32[]{:S(2)}) copy-start(bf16[1,64,1024]{2,1,0:T(8,128)(2,1)} %param.9) | copy-start | bytes 393220
  1.5 0.9 %copy-start.2 = (bf16[1,64,1024]{2,1,0:T(8,128)(2,1)S(1)}, bf16[1,64,1024]{2,1,0:T(8,128)(2,1)}, u32[]{:S(2)}) copy-start(bf16[1,64,1024]{2,1,0:T(8,128)(2,1)} %param.10) | copy-start | bytes 393220
  2.4 10.3 %copy-start.3 = (bf16[1024,64]{0,1:T(8,128)(2,1)S(1)}, bf16[1024,64]{0,1:T(8,128)(2,1)}, u32[]{:S(2)}) copy-start(bf16[1024,64]{0,1:T(8,128)(2,1)} %param.11) | copy-start | bytes 393220
  2.4 10.3 %copy-start.4 = (bf16[1024,64]{0,1:T(8,128)(2,1)S(1)}, bf16[1024,64]{0,1:T(8,128)(2,1)}, u32[]{:S(2)}) copy-start(bf16[1024,64]{0,1:T(8,128)(2,1)} %param.12) | copy-start | bytes 393220
  2.5 10.2 %collective-permute-start = (bf16[64,1280]{1,0:T(8,128)(2,1)S(1)}, bf16[64,1280]{1,0:T(8,128)(2,1)S(1)}, u32[]{:S(2)}, u32[]{:S(2)}) collective-permute-start(bf16[64,1280]{1,0:T(8,128)(2,1)S(1)} %get-tuple-element.22), channel_id=1, source_target_pairs={{0,6},{1,7},{2,4},{3,5},{4,2},{5,3},{6,0},{7,1},{8,14},{9,15},{10,... | collective-permute-start | bytes 491528 | tf_op jit(solution)/shard_map/ppermute | solution.py:388
  7.6 13.9 %collective-permute-start.2 = (bf16[64,1280]{1,0:T(8,128)(2,1)S(1)}, bf16[64,1280]{1,0:T(8,128)(2,1)S(1)}, u32[]{:S(2)}, u32[]{:S(2)}) collective-permute-start(bf16[64,1280]{1,0:T(8,128)(2,1)S(1)} %get-tuple-element.23), channel_id=1, source_target_pairs={{0,4},{1,5},{2,6},{3,7},{4,0},{5,1},{6,2},{7,3},{8,12},{9,13},{10,... | collective-permute-start | bytes 491528 | tf_op jit(solution)/shard_map/ppermute | solution.py:388
  7.6 5.1 %copy-start.6 = (bf16[1024,1]{0,1:T(2,128)(2,1)S(1)}, bf16[1024,1]{0,1:T(2,128)(2,1)}, u32[]{:S(2)}) copy-start(bf16[1024,1]{0,1:T(2,128)(2,1)} %param.15) | copy-start | bytes 6148
  7.6 5.1 %copy-start.5 = (bf16[1024,1]{0,1:T(2,128)(2,1)S(1)}, bf16[1024,1]{0,1:T(2,128)(2,1)}, u32[]{:S(2)}) copy-start(bf16[1024,1]{0,1:T(2,128)(2,1)} %param.14) | copy-start | bytes 6148
  7.6 13.9 %collective-permute-start.4 = (bf16[64,1280]{1,0:T(8,128)(2,1)S(1)}, bf16[64,1280]{1,0:T(8,128)(2,1)S(1)}, u32[]{:S(2)}, u32[]{:S(2)}) collective-permute-start(bf16[64,1280]{1,0:T(8,128)(2,1)S(1)} %get-tuple-element.24), channel_id=1, source_target_pairs={{0,2},{1,3},{2,0},{3,1},{4,6},{5,7},{6,4},{7,5},{8,10},{9,11},{10,... | collective-permute-start | bytes 491528 | tf_op jit(solution)/shard_map/ppermute | solution.py:388
  12.8 10.6 %copy-start = (bf16[1024,128]{1,0:T(8,128)(2,1)S(1)}, bf16[1024,128]{1,0:T(8,128)(2,1)}, u32[]{:S(2)}) copy-start(bf16[1024,128]{1,0:T(8,128)(2,1)} %wv_ref.1) | copy-start | bytes 786436
  12.8 10.6 %collective-permute-start.7 = (bf16[144,1024]{1,0:T(8,128)(2,1)S(1)}, bf16[144,1024]{1,0:T(8,128)(2,1)S(1)}, u32[]{:S(2)}, u32[]{:S(2)}) collective-permute-start(bf16[144,1024]{1,0:T(8,128)(2,1)S(1)} %narrow.1.refs_8_.own), channel_id=1, source_target_pairs={{0,1},{1,0},{2,3},{3,2},{4,5},{5,4},{6,7},{7,6},{8,9},{9,8},{10,11... | collective-permute-start | bytes 884744 | tf_op jit(solution)/shard_map/ppermute | solution.py:388
  12.9 10.4 %collective-permute-start.6 = (bf16[64,1280]{1,0:T(8,128)(2,1)S(1)}, bf16[64,1280]{1,0:T(8,128)(2,1)S(1)}, u32[]{:S(2)}, u32[]{:S(2)}) collective-permute-start(bf16[64,1280]{1,0:T(8,128)(2,1)S(1)} %get-tuple-element.25.refs_6_), channel_id=1, source_target_pairs={{0,1},{1,0},{2,3},{3,2},{4,5},{5,4},{6,7},{7,6},{8,9},{9,8},{10,11... | collective-permute-start | bytes 491528 | tf_op jit(solution)/shard_map/ppermute | solution.py:388
  13.4 10.0 %collective-permute-start.1 = (bf16[64,1280]{1,0:T(8,128)(2,1)S(1)}, bf16[64,1280]{1,0:T(8,128)(2,1)S(1)}, u32[]{:S(2)}, u32[]{:S(2)}) collective-permute-start(bf16[64,1280]{1,0:T(8,128)(2,1)S(1)} %collective-permute-done.after_ref.refs_0_), channel_id=1, source_target_pairs={{0,1},{1,0},{2,3},{3,2},{4,5},{5,4},{6,7},{7,6},{8,9},{9,8},{10,11... | collective-permute-start | bytes 491528 | tf_op jit(solution)/shard_map/ppermute | solution.py:388
  21.5 1.9 %collective-permute-start.3 = (bf16[64,1280]{1,0:T(8,128)(2,1)S(1)}, bf16[64,1280]{1,0:T(8,128)(2,1)S(1)}, u32[]{:S(2)}, u32[]{:S(2)}) collective-permute-start(bf16[64,1280]{1,0:T(8,128)(2,1)S(1)} %collective-permute-done.2.refs_2_), channel_id=1, source_target_pairs={{0,1},{1,0},{2,3},{3,2},{4,5},{5,4},{6,7},{7,6},{8,9},{9,8},{10,11... | collective-permute-start | bytes 491528 | tf_op jit(solution)/shard_map/ppermute | solution.py:388
  21.5 1.9 %collective-permute-start.5 = (bf16[64,1280]{1,0:T(8,128)(2,1)S(1)}, bf16[64,1280]{1,0:T(8,128)(2,1)S(1)}, u32[]{:S(2)}, u32[]{:S(2)}) collective-permute-start(bf16[64,1280]{1,0:T(8,128)(2,1)S(1)} %collective-permute-done.4.refs_4_), channel_id=1, source_target_pairs={{0,1},{1,0},{2,3},{3,2},{4,5},{5,4},{6,7},{7,6},{8,9},{9,8},{10,11... | collective-permute-start | bytes 491528 | tf_op jit(solution)/shard_map/ppermute | solution.py:388
  23.3 9.4 %collective-permute-start.11 = (bf16[1024,128]{1,0:T(8,128)(2,1)S(1)}, bf16[1024,128]{1,0:T(8,128)(2,1)S(1)}, u32[]{:S(2)}, u32[]{:S(2)}) collective-permute-start(bf16[1024,128]{1,0:T(8,128)(2,1)S(1)} %copy-done), channel_id=1, source_target_pairs={{0,1},{1,0},{2,3},{3,2},{4,5},{5,4},{6,7},{7,6},{8,9},{9,8},{10,11... | collective-permute-start | bytes 786440 | tf_op jit(solution)/shard_map/ppermute | solution.py:388
  28.8 3.9 %collective-permute-start.10 = (bf16[256,512]{1,0:T(8,128)(2,1)S(1)}, bf16[256,512]{1,0:T(8,128)(2,1)S(1)}, u32[]{:S(2)}, u32[]{:S(2)}) collective-permute-start(bf16[256,512]{1,0:T(8,128)(2,1)S(1)} %get-tuple-element.30), channel_id=1, source_target_pairs={{0,1},{1,0},{2,3},{3,2},{4,5},{5,4},{6,7},{7,6},{8,9},{9,8},{10,11... | collective-permute-start | bytes 786440 | tf_op jit(solution)/shard_map/ppermute | solution.py:388
  29.4 1.6 %collective-permute-start.8 = (bf16[512,128]{1,0:T(8,128)(2,1)S(1)}, bf16[512,128]{1,0:T(8,128)(2,1)S(1)}, u32[]{:S(2)}, u32[]{:S(2)}) collective-permute-start(bf16[512,128]{1,0:T(8,128)(2,1)S(1)} %get-tuple-element.28), channel_id=1, source_target_pairs={{0,1},{1,0},{2,3},{3,2},{4,5},{5,4},{6,7},{7,6},{8,9},{9,8},{10,11... | collective-permute-start | bytes 393224 | tf_op jit(solution)/shard_map/ppermute | solution.py:388
  29.5 6.8 %collective-permute-start.13 = (bf16[128,1024]{1,0:T(8,128)(2,1)S(1)}, bf16[128,1024]{1,0:T(8,128)(2,1)S(1)}, u32[]{:S(2)}, u32[]{:S(2)}) collective-permute-start(bf16[128,1024]{1,0:T(8,128)(2,1)S(1)} %get-tuple-element.32.own_ref), channel_id=1, source_target_pairs={{0,8},{1,17},{2,10},{3,19},{4,12},{5,21},{6,14},{7,23},{8,0},{9,25... | collective-permute-start | bytes 786440 | tf_op jit(solution)/shard_map/ppermute | solution.py:399
  31.4 9.1 %collective-permute-start.9 = (bf16[128,1024]{1,0:T(8,128)(2,1)S(1)}, bf16[128,1024]{1,0:T(8,128)(2,1)S(1)}, u32[]{:S(2)}, u32[]{:S(2)}) collective-permute-start(bf16[128,1024]{1,0:T(8,128)(2,1)S(1)} %gram.1.own_ref), channel_id=1, source_target_pairs={{0,8},{1,17},{2,10},{3,19},{4,12},{5,21},{6,14},{7,23},{8,0},{9,25... | collective-permute-start | bytes 786440 | tf_op jit(solution)/shard_map/ppermute | solution.py:399
  33.7 8.3 %collective-permute-start.15 = (bf16[64,1024]{1,0:T(8,128)(2,1)S(1)}, bf16[64,1024]{1,0:T(8,128)(2,1)S(1)}, u32[]{:S(2)}, u32[]{:S(2)}) collective-permute-start(bf16[64,1024]{1,0:T(8,128)(2,1)S(1)} %get-tuple-element.33), channel_id=1, source_target_pairs={{0,6},{1,7},{2,4},{3,5},{4,2},{5,3},{6,0},{7,1},{8,14},{9,15},{10,... | collective-permute-start | bytes 393224 | tf_op jit(solution)/shard_map/ppermute | solution.py:388
  36.3 10.4 %collective-permute-start.14 = (bf16[128,1024]{1,0:T(8,128)(2,1)S(1)}, bf16[128,1024]{1,0:T(8,128)(2,1)S(1)}, u32[]{:S(2)}, u32[]{:S(2)}) collective-permute-start(bf16[128,1024]{1,0:T(8,128)(2,1)S(1)} %add.3.own_v), channel_id=1, source_target_pairs={{0,16},{1,9},{2,18},{3,11},{4,20},{5,13},{6,22},{7,15},{8,24},{9,1... | collective-permute-start | bytes 786440 | tf_op jit(solution)/shard_map/ppermute | solution.py:399
  37.9 8.9 %collective-permute-start.16 = (bf16[64,1024]{1,0:T(8,128)(2,1)S(1)}, bf16[64,1024]{1,0:T(8,128)(2,1)S(1)}, u32[]{:S(2)}, u32[]{:S(2)}) collective-permute-start(bf16[64,1024]{1,0:T(8,128)(2,1)S(1)} %get-tuple-element.34), channel_id=1, source_target_pairs={{0,4},{1,5},{2,6},{3,7},{4,0},{5,1},{6,2},{7,3},{8,12},{9,13},{10,... | collective-permute-start | bytes 393224 | tf_op jit(solution)/shard_map/ppermute | solution.py:388
  37.9 8.9 %collective-permute-start.17 = (bf16[64,1024]{1,0:T(8,128)(2,1)S(1)}, bf16[64,1024]{1,0:T(8,128)(2,1)S(1)}, u32[]{:S(2)}, u32[]{:S(2)}) collective-permute-start(bf16[64,1024]{1,0:T(8,128)(2,1)S(1)} %get-tuple-element.35), channel_id=1, source_target_pairs={{0,2},{1,3},{2,0},{3,1},{4,6},{5,7},{6,4},{7,5},{8,10},{9,11},{10,... | collective-permute-start | bytes 393224 | tf_op jit(solution)/shard_map/ppermute | solution.py:388
  40.6 6.4 %collective-permute-start.12 = (bf16[128,1024]{1,0:T(8,128)(2,1)S(1)}, bf16[128,1024]{1,0:T(8,128)(2,1)S(1)}, u32[]{:S(2)}, u32[]{:S(2)}) collective-permute-start(bf16[128,1024]{1,0:T(8,128)(2,1)S(1)} %add.2.own_qk), channel_id=1, source_target_pairs={{0,16},{1,9},{2,18},{3,11},{4,20},{5,13},{6,22},{7,15},{8,24},{9,1... | collective-permute-start | bytes 786440 | tf_op jit(solution)/shard_map/ppermute | solution.py:399

commit v6 on v5

--- a/solution.py
+++ b/solution.py
@@ -160,15 +160,19 @@
         pairs = [halves(a) for a in mats]
         level = 1
         while (2 << level) <= CHUNK:
-            joint = ((row_id >> (level + 1)) == (col_id >> (level + 1))) & ((row_id >> level) > (col_id >> level))
+            wide = (4 << level) <= CHUNK
+            reach = level + (2 if wide else 1)
+            joint = ((row_id >> reach) == (col_id >> reach)) & ((row_id >> level) > (col_id >> level))
             tp = [halves(t) for t in inv]
             left = [
-                fine_nn(tp[i], tuple(jnp.where(joint, half, jnp.zeros_like(half)) for half in pairs[i]))
+                halves(fine_nn(tp[i], tuple(jnp.where(joint, half, jnp.zeros_like(half)) for half in pairs[i])))
                 for i in each
             ]
-            lp = [halves(z) for z in left]
-            inv = [inv[i] - fine_nn(lp[i], tp[i]) for i in each]
-            level += 1
+            inv = [inv[i] - fine_nn(left[i], tp[i]) for i in each]
+            if wide:
+                square = [halves(fine_nn(z, z)) for z in left]
+                inv = [inv[i] + fine_nn(square[i], halves(inv[i])) for i in each]
+            level = reach
         tp = [halves(t) for t in inv]
         ep = [halves(y) for y in ek_bv]
         wu = [

time: 48.4 us -> 48.2 us (level)
  no operation moved by 1% of the time
where the time goes in v6:
time: 48.2 us; the launch traced here: 48 us
  waiting for transfers between devices  18.4 us (38%)
  starting transfers between devices  17.8 us (37%)
  Pallas kernels  7.99 us (17%)
  between operations  2.08 us (4%)
  local copies, waits for them, and re-layouts  1.82 us (4%)
    ppermute x14, waiting for transfers between devices, across(): lax.ppermute(block, 'head', [(i, i ^ distance) for i in range(count)])  18.1 us
    ppermute x14, starting transfers between devices, across(): lax.ppermute(block, 'head', [(i, i ^ distance) for i in range(count)])  12.8 us
    pallas_call x1, Pallas kernels, core_grads(): pl.pallas_call(functools.partial(core_kernel, order), out_shape=(out(tota...  5.19 us
    ppermute x4, starting transfers between devices, across_data(): return lax.ppermute(block, ('dp', 'head'), route)  4.97 us
    pallas_call x8, Pallas kernels, local_call(): pl.pallas_call(body, out_shape=outs, in_specs=[spec] * len(args) + [pl.Bl...  2.8 us
    unnamed x14, local copies, waits for them, and re-layouts  1.82 us
  transfers between devices with their start and end apart: 18, of which 5 were waited for; matrix products, arithmetic and copies ran while one was open for 0% of the time, Pallas kernels for 14%

profile of v6, /device:TPU:0, one launch (start us, length us, event | category | flops | bytes accessed | tf_op | source)
XLA Modules:
  0.0 48.0 jit_solution(2046645620182376990)
XLA Ops:
  0.6 0.9 %copy-done.1 = bf16[1,64,1024]{2,1,0:T(8,128)(2,1)S(1)} copy-done((bf16[1,64,1024]{2,1,0:T(8,128)(2,1)S(1)}, bf16[1,64,1024]{2,1,0:T(8,128)(2,1)}, u32[]{:S(2)}) %copy-start.1) | copy-done | bytes 131096
  1.5 0.9 %copy-done.2 = bf16[1,64,1024]{2,1,0:T(8,128)(2,1)S(1)} copy-done((bf16[1,64,1024]{2,1,0:T(8,128)(2,1)S(1)}, bf16[1,64,1024]{2,1,0:T(8,128)(2,1)}, u32[]{:S(2)}) %copy-start.2) | copy-done | bytes 131096
  2.5 5.1 %collective-permute-start = (bf16[64,1280]{1,0:T(8,128)(2,1)S(1)}, bf16[64,1280]{1,0:T(8,128)(2,1)S(1)}, u32[]{:S(2)}, u32[]{:S(2)}) collective-permute-start(bf16[64,1280]{1,0:T(8,128)(2,1)S(1)} %get-tuple-element.22), channel_id=1, source_target_pairs={{0,6},{1,7},{2,4},{3,5},{4,2},{5,3},{6,0},{7,1},{8,14},{9,15},{10,... | collective-permute-start | bytes 491528 | tf_op jit(solution)/shard_map/ppermute | solution.py:392
  7.6 0.6 %collective-permute-start.4 = (bf16[64,1280]{1,0:T(8,128)(2,1)S(1)}, bf16[64,1280]{1,0:T(8,128)(2,1)S(1)}, u32[]{:S(2)}, u32[]{:S(2)}) collective-permute-start(bf16[64,1280]{1,0:T(8,128)(2,1)S(1)} %get-tuple-element.24), channel_id=1, source_target_pairs={{0,2},{1,3},{2,0},{3,1},{4,6},{5,7},{6,4},{7,5},{8,10},{9,11},{10,... | collective-permute-start | bytes 491528 | tf_op jit(solution)/shard_map/ppermute | solution.py:392
  8.3 4.5 %collective-permute-done.after_ref.refs_0_ = bf16[64,1280]{1,0:T(8,128)(2,1)S(1)} collective-permute-done((bf16[64,1280]{1,0:T(8,128)(2,1)S(1)}, bf16[64,1280]{1,0:T(8,128)(2,1)S(1)}, u32[]{:S(2)}, u32[]{:S(2)}) %collective-permute-start) | collective-permute-done | bytes 163872 | tf_op jit(solution)/shard_map/ppermute | solution.py:392
  12.8 0.0 copy-start
  12.8 0.1 collective-permute-start.7
  12.9 0.5 %collective-permute-start.6 = (bf16[64,1280]{1,0:T(8,128)(2,1)S(1)}, bf16[64,1280]{1,0:T(8,128)(2,1)S(1)}, u32[]{:S(2)}, u32[]{:S(2)}) collective-permute-start(bf16[64,1280]{1,0:T(8,128)(2,1)S(1)} %get-tuple-element.25.refs_6_), channel_id=1, source_target_pairs={{0,1},{1,0},{2,3},{3,2},{4,5},{5,4},{6,7},{7,6},{8,9},{9,8},{10,11... | collective-permute-start | bytes 491528 | tf_op jit(solution)/shard_map/ppermute | solution.py:392
  13.4 0.1 collective-permute-start.1
  13.5 8.0 %collective-permute-done.2.refs_2_ = bf16[64,1280]{1,0:T(8,128)(2,1)S(1)} collective-permute-done((bf16[64,1280]{1,0:T(8,128)(2,1)S(1)}, bf16[64,1280]{1,0:T(8,128)(2,1)S(1)}, u32[]{:S(2)}, u32[]{:S(2)}) %collective-permute-start.2) | collective-permute-done | bytes 163872 | tf_op jit(solution)/shard_map/ppermute | solution.py:392
  21.5 0.0 collective-permute-start.3
  21.5 0.5 %collective-permute-start.5 = (bf16[64,1280]{1,0:T(8,128)(2,1)S(1)}, bf16[64,1280]{1,0:T(8,128)(2,1)S(1)}, u32[]{:S(2)}, u32[]{:S(2)}) collective-permute-start(bf16[64,1280]{1,0:T(8,128)(2,1)S(1)} %collective-permute-done.4.refs_4_), channel_id=1, source_target_pairs={{0,1},{1,0},{2,3},{3,2},{4,5},{5,4},{6,7},{7,6},{8,9},{9,8},{10,11... | collective-permute-start | bytes 491528 | tf_op jit(solution)/shard_map/ppermute | solution.py:392
  23.3 0.1 collective-permute-start.11
  23.4 0.0 collective-permute-done.1.refs_1_
  23.4 0.0 collective-permute-done.7.refs_9_.partner
  23.4 5.2 %core_grads.1 = (bf16[512,1024]{1,0:T(8,128)(2,1)S(1)}, bf16[512,128]{1,0:T(8,128)(2,1)S(1)}, bf16[512,128]{1,0:T(8,128)(2,1)S(1)}, bf16[128,1024]{1,0:T(8,128)(...) custom-call(bf16[64,1280]{1,0:T(8,128)(2,1)S(1)} %collective-permute-done.after_ref.refs_0_, ...), custom_call_target="tpu_custom_call" | custom-call | tf_op jit(solution)/shard_map/core_grads/pallas_call | solution.py:292
  28.6 0.5 %collective-permute-start.10 = (bf16[256,512]{1,0:T(8,128)(2,1)S(1)}, bf16[256,512]{1,0:T(8,128)(2,1)S(1)}, u32[]{:S(2)}, u32[]{:S(2)}) collective-permute-start(bf16[256,512]{1,0:T(8,128)(2,1)S(1)} %get-tuple-element.30), channel_id=1, source_target_pairs={{0,1},{1,0},{2,3},{3,2},{4,5},{5,4},{6,7},{7,6},{8,9},{9,8},{10,11... | collective-permute-start | bytes 786440 | tf_op jit(solution)/shard_map/ppermute | solution.py:392
  29.2 0.1 collective-permute-start.8
  29.3 1.5 %collective-permute-start.13 = (bf16[128,1024]{1,0:T(8,128)(2,1)S(1)}, bf16[128,1024]{1,0:T(8,128)(2,1)S(1)}, u32[]{:S(2)}, u32[]{:S(2)}) collective-permute-start(bf16[128,1024]{1,0:T(8,128)(2,1)S(1)} %get-tuple-element.32.own_ref), channel_id=1, source_target_pairs={{0,8},{1,17},{2,10},{3,19},{4,12},{5,21},{6,14},{7,23},{8,0},{9,25... | collective-permute-start | bytes 786440 | tf_op jit(solution)/shard_map/ppermute | solution.py:403
  30.8 0.5 gram.1.own_ref
  31.2 1.3 %collective-permute-start.9 = (bf16[128,1024]{1,0:T(8,128)(2,1)S(1)}, bf16[128,1024]{1,0:T(8,128)(2,1)S(1)}, u32[]{:S(2)}, u32[]{:S(2)}) collective-permute-start(bf16[128,1024]{1,0:T(8,128)(2,1)S(1)} %gram.1.own_ref), channel_id=1, source_target_pairs={{0,8},{1,17},{2,10},{3,19},{4,12},{5,21},{6,14},{7,23},{8,0},{9,25... | collective-permute-start | bytes 786440 | tf_op jit(solution)/shard_map/ppermute | solution.py:403
  32.6 0.9 %terms.1 = (bf16[64,1024]{1,0:T(8,128)(2,1)S(1)}, bf16[64,1024]{1,0:T(8,128)(2,1)S(1)}, bf16[64,1024]{1,0:T(8,128)(2,1)S(1)}, bf16[64,1024]{1,0:T(8,128)(2,1)S(1)}) custom-call(bf16[256,512]{1,0:T(8,128)(2,1)S(1)} %get-tuple-element.29.mine_ref, bf16[256,512]{1,0:T(8,128)(2,1)S(1)} %collective-permute-done.10.recv_ref, ...), custom_call_target="tpu_custom_call" | custom-call | flops 1073741824 | bytes 1048576 | tf_op jit(solution)/shard_map/terms/pallas_call | solution.py:378
  33.5 2.5 %collective-permute-start.15 = (bf16[64,1024]{1,0:T(8,128)(2,1)S(1)}, bf16[64,1024]{1,0:T(8,128)(2,1)S(1)}, u32[]{:S(2)}, u32[]{:S(2)}) collective-permute-start(bf16[64,1024]{1,0:T(8,128)(2,1)S(1)} %get-tuple-element.33), channel_id=1, source_target_pairs={{0,6},{1,7},{2,4},{3,5},{4,2},{5,3},{6,0},{7,1},{8,14},{9,15},{10,... | collective-permute-start | bytes 393224 | tf_op jit(solution)/shard_map/ppermute | solution.py:392
  36.0 0.1 add.3.own_v
  36.1 1.6 %collective-permute-start.14 = (bf16[128,1024]{1,0:T(8,128)(2,1)S(1)}, bf16[128,1024]{1,0:T(8,128)(2,1)S(1)}, u32[]{:S(2)}, u32[]{:S(2)}) collective-permute-start(bf16[128,1024]{1,0:T(8,128)(2,1)S(1)} %add.3.own_v), channel_id=1, source_target_pairs={{0,16},{1,9},{2,18},{3,11},{4,20},{5,13},{6,22},{7,15},{8,24},{9,1... | collective-permute-start | bytes 786440 | tf_op jit(solution)/shard_map/ppermute | solution.py:403
  37.7 2.6 %collective-permute-start.17 = (bf16[64,1024]{1,0:T(8,128)(2,1)S(1)}, bf16[64,1024]{1,0:T(8,128)(2,1)S(1)}, u32[]{:S(2)}, u32[]{:S(2)}) collective-permute-start(bf16[64,1024]{1,0:T(8,128)(2,1)S(1)} %get-tuple-element.35), channel_id=1, source_target_pairs={{0,2},{1,3},{2,0},{3,1},{4,6},{5,7},{6,4},{7,5},{8,10},{9,11},{10,... | collective-permute-start | bytes 393224 | tf_op jit(solution)/shard_map/ppermute | solution.py:392
  40.3 0.1 add.2.own_qk
  40.4 0.6 %collective-permute-start.12 = (bf16[128,1024]{1,0:T(8,128)(2,1)S(1)}, bf16[128,1024]{1,0:T(8,128)(2,1)S(1)}, u32[]{:S(2)}, u32[]{:S(2)}) collective-permute-start(bf16[128,1024]{1,0:T(8,128)(2,1)S(1)} %add.2.own_qk), channel_id=1, source_target_pairs={{0,16},{1,9},{2,18},{3,11},{4,20},{5,13},{6,22},{7,15},{8,24},{9,1... | collective-permute-start | bytes 786440 | tf_op jit(solution)/shard_map/ppermute | solution.py:403
  41.0 0.8 %collective-permute-done.15.refs_1_ = bf16[64,1024]{1,0:T(8,128)(2,1)S(1)} collective-permute-done((bf16[64,1024]{1,0:T(8,128)(2,1)S(1)}, bf16[64,1024]{1,0:T(8,128)(2,1)S(1)}, u32[]{:S(2)}, u32[]{:S(2)}) %collective-permute-start.15) | collective-permute-done | bytes 131104 | tf_op jit(solution)/shard_map/ppermute | solution.py:392
  41.8 4.8 %collective-permute-done.16.refs_1_ = bf16[64,1024]{1,0:T(8,128)(2,1)S(1)} collective-permute-done((bf16[64,1024]{1,0:T(8,128)(2,1)S(1)}, bf16[64,1024]{1,0:T(8,128)(2,1)S(1)}, u32[]{:S(2)}, u32[]{:S(2)}) %collective-permute-start.16) | collective-permute-done | bytes 131104 | tf_op jit(solution)/shard_map/ppermute | solution.py:392
  46.6 0.2 collective-permute-done.12.recv_qk
  46.8 1.2 %last.1 = (f32[64,1024]{1,0:T(8,128)}, f32[64,1024]{1,0:T(8,128)}, f32[1024,128]{1,0:T(8,128)}, bf16[64,1024]{1,0:T(8,128)(2,1)}) custom-call(bf16[128,1024]{1,0:T(8,128)(2,1)S(1)} %add.2.own_qk, bf16[128,1024]{1,0:T(8,128)(2,1)S(1)} %collective-permute-done.12.recv_qk, bf16[128,1024]{1,0:T(8,128)(2,1)S(1)} %add.3.own_v, ...), custom_call_target="tpu_custom_call" | custom-call | flops 1048576 | bytes 1048576 | tf_op jit(solution)/shard_map/last/pallas_call | solution.py:378
  (27 shorter events, 0.2 us)
Async XLA Ops:
  0.6 0.9 %copy-start.1 = (bf16[1,64,1024]{2,1,0:T(8,128)(2,1)S(1)}, bf16[1,64,1024]{2,1,0:T(8,128)(2,1)}, u32[]{:S(2)}) copy-start(bf16[1,64,1024]{2,1,0:T(8,128)(2,1)} %param.9) | copy-start | bytes 393220
  1.5 0.9 %copy-start.2 = (bf16[1,64,1024]{2,1,0:T(8,128)(2,1)S(1)}, bf16[1,64,1024]{2,1,0:T(8,128)(2,1)}, u32[]{:S(2)}) copy-start(bf16[1,64,1024]{2,1,0:T(8,128)(2,1)} %param.10) | copy-start | bytes 393220
  2.4 10.3 %copy-start.3 = (bf16[1024,64]{0,1:T(8,128)(2,1)S(1)}, bf16[1024,64]{0,1:T(8,128)(2,1)}, u32[]{:S(2)}) copy-start(bf16[1024,64]{0,1:T(8,128)(2,1)} %param.11) | copy-start | bytes 393220
  2.4 10.3 %copy-start.4 = (bf16[1024,64]{0,1:T(8,128)(2,1)S(1)}, bf16[1024,64]{0,1:T(8,128)(2,1)}, u32[]{:S(2)}) copy-start(bf16[1024,64]{0,1:T(8,128)(2,1)} %param.12) | copy-start | bytes 393220
  2.5 10.2 %collective-permute-start = (bf16[64,1280]{1,0:T(8,128)(2,1)S(1)}, bf16[64,1280]{1,0:T(8,128)(2,1)S(1)}, u32[]{:S(2)}, u32[]{:S(2)}) collective-permute-start(bf16[64,1280]{1,0:T(8,128)(2,1)S(1)} %get-tuple-element.22), channel_id=1, source_target_pairs={{0,6},{1,7},{2,4},{3,5},{4,2},{5,3},{6,0},{7,1},{8,14},{9,15},{10,... | collective-permute-start | bytes 491528 | tf_op jit(solution)/shard_map/ppermute | solution.py:392
  7.6 13.9 %collective-permute-start.2 = (bf16[64,1280]{1,0:T(8,128)(2,1)S(1)}, bf16[64,1280]{1,0:T(8,128)(2,1)S(1)}, u32[]{:S(2)}, u32[]{:S(2)}) collective-permute-start(bf16[64,1280]{1,0:T(8,128)(2,1)S(1)} %get-tuple-element.23), channel_id=1, source_target_pairs={{0,4},{1,5},{2,6},{3,7},{4,0},{5,1},{6,2},{7,3},{8,12},{9,13},{10,... | collective-permute-start | bytes 491528 | tf_op jit(solution)/shard_map/ppermute | solution.py:392
  7.6 5.1 %copy-start.6 = (bf16[1024,1]{0,1:T(2,128)(2,1)S(1)}, bf16[1024,1]{0,1:T(2,128)(2,1)}, u32[]{:S(2)}) copy-start(bf16[1024,1]{0,1:T(2,128)(2,1)} %param.15) | copy-start | bytes 6148
  7.6 5.1 %copy-start.5 = (bf16[1024,1]{0,1:T(2,128)(2,1)S(1)}, bf16[1024,1]{0,1:T(2,128)(2,1)}, u32[]{:S(2)}) copy-start(bf16[1024,1]{0,1:T(2,128)(2,1)} %param.14) | copy-start | bytes 6148
  7.6 13.9 %collective-permute-start.4 = (bf16[64,1280]{1,0:T(8,128)(2,1)S(1)}, bf16[64,1280]{1,0:T(8,128)(2,1)S(1)}, u32[]{:S(2)}, u32[]{:S(2)}) collective-permute-start(bf16[64,1280]{1,0:T(8,128)(2,1)S(1)} %get-tuple-element.24), channel_id=1, source_target_pairs={{0,2},{1,3},{2,0},{3,1},{4,6},{5,7},{6,4},{7,5},{8,10},{9,11},{10,... | collective-permute-start | bytes 491528 | tf_op jit(solution)/shard_map/ppermute | solution.py:392
  12.8 10.6 %copy-start = (bf16[1024,128]{1,0:T(8,128)(2,1)S(1)}, bf16[1024,128]{1,0:T(8,128)(2,1)}, u32[]{:S(2)}) copy-start(bf16[1024,128]{1,0:T(8,128)(2,1)} %wv_ref.1) | copy-start | bytes 786436
  12.8 10.6 %collective-permute-start.7 = (bf16[144,1024]{1,0:T(8,128)(2,1)S(1)}, bf16[144,1024]{1,0:T(8,128)(2,1)S(1)}, u32[]{:S(2)}, u32[]{:S(2)}) collective-permute-start(bf16[144,1024]{1,0:T(8,128)(2,1)S(1)} %narrow.1.refs_8_.own), channel_id=1, source_target_pairs={{0,1},{1,0},{2,3},{3,2},{4,5},{5,4},{6,7},{7,6},{8,9},{9,8},{10,11... | collective-permute-start | bytes 884744 | tf_op jit(solution)/shard_map/ppermute | solution.py:392
  12.9 10.4 %collective-permute-start.6 = (bf16[64,1280]{1,0:T(8,128)(2,1)S(1)}, bf16[64,1280]{1,0:T(8,128)(2,1)S(1)}, u32[]{:S(2)}, u32[]{:S(2)}) collective-permute-start(bf16[64,1280]{1,0:T(8,128)(2,1)S(1)} %get-tuple-element.25.refs_6_), channel_id=1, source_target_pairs={{0,1},{1,0},{2,3},{3,2},{4,5},{5,4},{6,7},{7,6},{8,9},{9,8},{10,11... | collective-permute-start | bytes 491528 | tf_op jit(solution)/shard_map/ppermute | solution.py:392
  13.4 10.0 %collective-permute-start.1 = (bf16[64,1280]{1,0:T(8,128)(2,1)S(1)}, bf16[64,1280]{1,0:T(8,128)(2,1)S(1)}, u32[]{:S(2)}, u32[]{:S(2)}) collective-permute-start(bf16[64,1280]{1,0:T(8,128)(2,1)S(1)} %collective-permute-done.after_ref.refs_0_), channel_id=1, source_target_pairs={{0,1},{1,0},{2,3},{3,2},{4,5},{5,4},{6,7},{7,6},{8,9},{9,8},{10,11... | collective-permute-start | bytes 491528 | tf_op jit(solution)/shard_map/ppermute | solution.py:392
  21.5 1.9 %collective-permute-start.3 = (bf16[64,1280]{1,0:T(8,128)(2,1)S(1)}, bf16[64,1280]{1,0:T(8,128)(2,1)S(1)}, u32[]{:S(2)}, u32[]{:S(2)}) collective-permute-start(bf16[64,1280]{1,0:T(8,128)(2,1)S(1)} %collective-permute-done.2.refs_2_), channel_id=1, source_target_pairs={{0,1},{1,0},{2,3},{3,2},{4,5},{5,4},{6,7},{7,6},{8,9},{9,8},{10,11... | collective-permute-start | bytes 491528 | tf_op jit(solution)/shard_map/ppermute | solution.py:392
  21.5 1.9 %collective-permute-start.5 = (bf16[64,1280]{1,0:T(8,128)(2,1)S(1)}, bf16[64,1280]{1,0:T(8,128)(2,1)S(1)}, u32[]{:S(2)}, u32[]{:S(2)}) collective-permute-start(bf16[64,1280]{1,0:T(8,128)(2,1)S(1)} %collective-permute-done.4.refs_4_), channel_id=1, source_target_pairs={{0,1},{1,0},{2,3},{3,2},{4,5},{5,4},{6,7},{7,6},{8,9},{9,8},{10,11... | collective-permute-start | bytes 491528 | tf_op jit(solution)/shard_map/ppermute | solution.py:392
  23.3 9.2 %collective-permute-start.11 = (bf16[1024,128]{1,0:T(8,128)(2,1)S(1)}, bf16[1024,128]{1,0:T(8,128)(2,1)S(1)}, u32[]{:S(2)}, u32[]{:S(2)}) collective-permute-start(bf16[1024,128]{1,0:T(8,128)(2,1)S(1)} %copy-done), channel_id=1, source_target_pairs={{0,1},{1,0},{2,3},{3,2},{4,5},{5,4},{6,7},{7,6},{8,9},{9,8},{10,11... | collective-permute-start | bytes 786440 | tf_op jit(solution)/shard_map/ppermute | solution.py:392
  28.6 3.9 %collective-permute-start.10 = (bf16[256,512]{1,0:T(8,128)(2,1)S(1)}, bf16[256,512]{1,0:T(8,128)(2,1)S(1)}, u32[]{:S(2)}, u32[]{:S(2)}) collective-permute-start(bf16[256,512]{1,0:T(8,128)(2,1)S(1)} %get-tuple-element.30), channel_id=1, source_target_pairs={{0,1},{1,0},{2,3},{3,2},{4,5},{5,4},{6,7},{7,6},{8,9},{9,8},{10,11... | collective-permute-start | bytes 786440 | tf_op jit(solution)/shard_map/ppermute | solution.py:392
  29.2 1.6 %collective-permute-start.8 = (bf16[512,128]{1,0:T(8,128)(2,1)S(1)}, bf16[512,128]{1,0:T(8,128)(2,1)S(1)}, u32[]{:S(2)}, u32[]{:S(2)}) collective-permute-start(bf16[512,128]{1,0:T(8,128)(2,1)S(1)} %get-tuple-element.28), channel_id=1, source_target_pairs={{0,1},{1,0},{2,3},{3,2},{4,5},{5,4},{6,7},{7,6},{8,9},{9,8},{10,11... | collective-permute-start | bytes 393224 | tf_op jit(solution)/shard_map/ppermute | solution.py:392
  29.3 6.8 %collective-permute-start.13 = (bf16[128,1024]{1,0:T(8,128)(2,1)S(1)}, bf16[128,1024]{1,0:T(8,128)(2,1)S(1)}, u32[]{:S(2)}, u32[]{:S(2)}) collective-permute-start(bf16[128,1024]{1,0:T(8,128)(2,1)S(1)} %get-tuple-element.32.own_ref), channel_id=1, source_target_pairs={{0,8},{1,17},{2,10},{3,19},{4,12},{5,21},{6,14},{7,23},{8,0},{9,25... | collective-permute-start | bytes 786440 | tf_op jit(solution)/shard_map/ppermute | solution.py:403
  31.2 9.1 %collective-permute-start.9 = (bf16[128,1024]{1,0:T(8,128)(2,1)S(1)}, bf16[128,1024]{1,0:T(8,128)(2,1)S(1)}, u32[]{:S(2)}, u32[]{:S(2)}) collective-permute-start(bf16[128,1024]{1,0:T(8,128)(2,1)S(1)} %gram.1.own_ref), channel_id=1, source_target_pairs={{0,8},{1,17},{2,10},{3,19},{4,12},{5,21},{6,14},{7,23},{8,0},{9,25... | collective-permute-start | bytes 786440 | tf_op jit(solution)/shard_map/ppermute | solution.py:403
  33.5 8.3 %collective-permute-start.15 = (bf16[64,1024]{1,0:T(8,128)(2,1)S(1)}, bf16[64,1024]{1,0:T(8,128)(2,1)S(1)}, u32[]{:S(2)}, u32[]{:S(2)}) collective-permute-start(bf16[64,1024]{1,0:T(8,128)(2,1)S(1)} %get-tuple-element.33), channel_id=1, source_target_pairs={{0,6},{1,7},{2,4},{3,5},{4,2},{5,3},{6,0},{7,1},{8,14},{9,15},{10,... | collective-permute-start | bytes 393224 | tf_op jit(solution)/shard_map/ppermute | solution.py:392
  36.1 10.5 %collective-permute-start.14 = (bf16[128,1024]{1,0:T(8,128)(2,1)S(1)}, bf16[128,1024]{1,0:T(8,128)(2,1)S(1)}, u32[]{:S(2)}, u32[]{:S(2)}) collective-permute-start(bf16[128,1024]{1,0:T(8,128)(2,1)S(1)} %add.3.own_v), channel_id=1, source_target_pairs={{0,16},{1,9},{2,18},{3,11},{4,20},{5,13},{6,22},{7,15},{8,24},{9,1... | collective-permute-start | bytes 786440 | tf_op jit(solution)/shard_map/ppermute | solution.py:403
  37.7 8.9 %collective-permute-start.16 = (bf16[64,1024]{1,0:T(8,128)(2,1)S(1)}, bf16[64,1024]{1,0:T(8,128)(2,1)S(1)}, u32[]{:S(2)}, u32[]{:S(2)}) collective-permute-start(bf16[64,1024]{1,0:T(8,128)(2,1)S(1)} %get-tuple-element.34), channel_id=1, source_target_pairs={{0,4},{1,5},{2,6},{3,7},{4,0},{5,1},{6,2},{7,3},{8,12},{9,13},{10,... | collective-permute-start | bytes 393224 | tf_op jit(solution)/shard_map/ppermute | solution.py:392
  37.7 8.9 %collective-permute-start.17 = (bf16[64,1024]{1,0:T(8,128)(2,1)S(1)}, bf16[64,1024]{1,0:T(8,128)(2,1)S(1)}, u32[]{:S(2)}, u32[]{:S(2)}) collective-permute-start(bf16[64,1024]{1,0:T(8,128)(2,1)S(1)} %get-tuple-element.35), channel_id=1, source_target_pairs={{0,2},{1,3},{2,0},{3,1},{4,6},{5,7},{6,4},{7,5},{8,10},{9,11},{10,... | collective-permute-start | bytes 393224 | tf_op jit(solution)/shard_map/ppermute | solution.py:392
  40.4 6.4 %collective-permute-start.12 = (bf16[128,1024]{1,0:T(8,128)(2,1)S(1)}, bf16[128,1024]{1,0:T(8,128)(2,1)S(1)}, u32[]{:S(2)}, u32[]{:S(2)}) collective-permute-start(bf16[128,1024]{1,0:T(8,128)(2,1)S(1)} %add.2.own_qk), channel_id=1, source_target_pairs={{0,16},{1,9},{2,18},{3,11},{4,20},{5,13},{6,22},{7,15},{8,24},{9,1... | collective-permute-start | bytes 786440 | tf_op jit(solution)/shard_map/ppermute | solution.py:403
